TPU v7x, 32 devices: a whole 2x2x4 slice. The times are simulated.
32 devices in a mesh: dp: 16 (over z, y, x), tensor: 2 (over core).
Axes of the slice: x: 2, y: 2, z: 4, core: 2. Of those that a mesh axis runs over, the one named last changes fastest.
Arguments:
- activations: bfloat16 [16384, 1024], P(('dp', 'tensor')), may hold values from -6 to 6
- targets: float32 [16384, 1024], P(('dp', 'tensor')), may hold values from -6 to 6
- lengths: int32 [16], P('dp'), may hold values from 1 to 1024, as said below
- token_mask: int32 [16384], P(('dp', 'tensor')), may hold values 0 or 1
- routes: int32 [16384, 8], P('dp'), may hold values from 0 to 31, all different within a row; in each aligned block of 1024 rows (0 to 1023, 1024 to 2047, ...) at most 384 rows name the same one
- route_weights: float32 [16384, 8], P('dp'), may hold values from 0.3 to 0.9
- norm_gains: float32 [2, 1024], replicated, may hold values from 0.5 to 1.5
- attention_master: float32 [1024, 3072], P('dp', 'tensor')
- expert_master: float32 [128, 3, 128, 1024], P('dp', None, 'tensor'), may hold values from -0.1875 to 0.1875
- attention_left: float32 [16, 12, 64, 64], P('dp', 'tensor'), as said below
- attention_right: float32 [16, 12, 256, 256], P('dp', 'tensor'), as said below
- attention_left_root: float32 [16, 12, 64, 64], P('dp', 'tensor'), as said below
- attention_right_root: float32 [16, 12, 256, 256], P('dp', 'tensor'), as said below
- expert_left: float32 [128, 3, 4, 128, 64], P('dp', None, None, 'tensor'), as said below
- expert_right: float32 [128, 3, 8, 256, 256], P('dp', None, 'tensor'), as said below
- expert_left_root: float32 [128, 3, 4, 128, 64], P('dp', None, None, 'tensor'), as said below
- expert_right_root: float32 [128, 3, 8, 256, 256], P('dp', None, 'tensor'), as said below
Outputs:
- output: float32 [16384, 1024], P(('dp', 'tensor'))
- mean_loss: float32 [], replicated
- input_grad: float32 [16384, 1024], P(('dp', 'tensor'))
- gain_grad: float32 [2, 1024], replicated
- gains_new: float32 [2, 1024], replicated
- attention_grad: float32 [1024, 3072], P('dp', 'tensor')
- attention_left_new: float32 [16, 12, 64, 64], P('dp', 'tensor')
- attention_right_new: float32 [16, 12, 256, 256], P('dp', 'tensor')
- attention_new: float32 [1024, 3072], P('dp', 'tensor')
- expert_grad: float32 [128, 3, 128, 1024], P('dp', None, 'tensor')
- expert_left_new: float32 [128, 3, 4, 128, 64], P('dp', None, None, 'tensor')
- expert_right_new: float32 [128, 3, 8, 256, 256], P('dp', None, 'tensor')
- expert_new: float32 [128, 3, 128, 1024], P('dp', None, 'tensor')
Inputs may be any that keep to these rules, and one draw needn't show every extreme that they name: `lengths`: at least one sequence is 1024 tokens long. `routes`: each row names 8 different experts. Among the rows of one sequence no expert is named more than 384 times, and in every draw some expert is named exactly 384 times in some sequence. `attention_left`: symmetric matrices. `attention_right`: symmetric matrices. `attention_left_root`: symmetric matrices. `attention_right_root`: symmetric matrices. `expert_left`: symmetric matrices. `expert_right`: symmetric matrices. `expert_left_root`: symmetric matrices. `expert_right_root`: symmetric matrices.
All inputs are finite; a program needn't handle non-finite values. No bound on the sum of `token_mask` on one device may be relied on, other than what follows from the above.
Results may differ from a plain program's by a relative error of at most 0.013.
Values may be sent and summed in bfloat16 or wider, within the bound.
No kernel may reach another device: no remote copies, remote signals or barrier semaphores. Data moves between devices by JAX's collectives and lax.ppermute only.
A program may use at most 832 MiB of HBM per device.

v0:
```python
import jax
import jax.numpy as jnp
from jax import lax
from jax.sharding import PartitionSpec as P

D = 1024
HEADS = 16
KV_HEADS = 8
HEAD_DIM = 64
EXPERTS = 32
TOPK = 8
BLK = 256
QROWS = 512
GROUPS = 4
BLOCK = 256
CAP = 384


epsilon = 1e-05
stat_decay = 0.9
gain_rate = 0.02
theta_base = 10000.0
masked_score = -1e30
highest = lax.Precision.HIGHEST


def product(left_side, right_side):
    return jnp.dot(left_side, right_side, preferred_element_type=jnp.float32)


def rope_tables(total_rows):
    half_width = HEAD_DIM // 2
    frequency = theta_base ** (-jnp.arange(half_width, dtype=jnp.float32) * 2.0 / HEAD_DIM)
    angles = jnp.arange(total_rows, dtype=jnp.float32)[:, None] * frequency[None, :]
    return (jnp.cos(angles)[:, None, :], jnp.sin(angles)[:, None, :])


def rotate(values, cosine, sine):
    half_width = values.shape[-1] // 2
    first_half = values[..., :half_width]
    second_half = values[..., half_width:]
    return jnp.concatenate(
        [first_half * cosine - second_half * sine, second_half * cosine + first_half * sine],
        axis=-1,
    )


def normalize(hidden, gain):
    scaling = lax.rsqrt(jnp.mean(hidden * hidden, axis=-1, keepdims=True) + epsilon)
    return (hidden * scaling * gain, scaling)


def normalize_back(hidden, scaling, gain, upstream):
    weighted = upstream * gain
    center = jnp.mean(weighted * hidden, axis=-1, keepdims=True)
    input_part = scaling * weighted - hidden * (scaling * scaling * scaling) * center
    return (input_part, jnp.sum(upstream * hidden * scaling, axis=0))


def gather_rows(values):
    return lax.all_gather(values, "tensor", axis=0, tiled=True)


def sum_rows(values):
    return lax.psum_scatter(values, "tensor", scatter_dimension=0, tiled=True)


def block_scores(query_block, key_vectors, block_start, seq_length):
    block_rows = query_block.shape[0]
    scores = jnp.einsum(
        "qkgd,skd->kgqs", query_block, key_vectors, preferred_element_type=jnp.float32
    ) * HEAD_DIM ** (-0.5)
    row_place = block_start + jnp.arange(block_rows, dtype=jnp.int32)
    key_place = jnp.arange(key_vectors.shape[0], dtype=jnp.int32)
    visible = (key_place[None, :] // BLK <= row_place[:, None] // BLK) & (
        key_place[None, :] < seq_length
    )
    return jnp.where(visible, scores, masked_score)


def attention_forward(queries, key_vectors, value_vectors, seq_length):
    block_total = queries.shape[0] // QROWS

    def one_block(block_index):
        block_start = block_index * QROWS
        query_block = lax.dynamic_slice_in_dim(queries, block_start, QROWS, 0)
        scores = block_scores(query_block, key_vectors, block_start, seq_length)
        top_score = jnp.max(scores, axis=-1, keepdims=True)
        exponent = jnp.exp(scores - top_score)
        denominator = jnp.sum(exponent, axis=-1, keepdims=True)
        weights = (exponent / denominator).astype(jnp.bfloat16)
        attended = jnp.einsum(
            "kgqs,skd->qkgd", weights, value_vectors, preferred_element_type=jnp.float32
        )
        return (attended.astype(jnp.bfloat16), top_score[..., 0] + jnp.log(denominator[..., 0]))

    return lax.map(one_block, jnp.arange(block_total, dtype=jnp.int32))


def attention_backward(queries, key_vectors, value_vectors, attended_grad, log_totals, seq_length):
    block_total = queries.shape[0] // QROWS
    score_scale = HEAD_DIM ** (-0.5)

    def one_block(running, operands):
        key_grad, value_grad = running
        block_index, block_totals = operands
        block_start = block_index * QROWS
        query_block = lax.dynamic_slice_in_dim(queries, block_start, QROWS, 0)
        grad_block = lax.dynamic_slice_in_dim(attended_grad, block_start, QROWS, 0)
        scores = block_scores(query_block, key_vectors, block_start, seq_length)
        probability = jnp.exp(scores - block_totals[..., None])
        prob_grad = jnp.einsum(
            "qkgd,skd->kgqs", grad_block, value_vectors, preferred_element_type=jnp.float32
        )
        center = jnp.sum(probability * prob_grad, axis=-1, keepdims=True)
        score_grad = (probability * (prob_grad - center)).astype(jnp.bfloat16)
        query_grad = (
            jnp.einsum(
                "kgqs,skd->qkgd", score_grad, key_vectors, preferred_element_type=jnp.float32
            )
            * score_scale
        )
        key_grad = (
            key_grad
            + jnp.einsum(
                "kgqs,qkgd->skd", score_grad, query_block, preferred_element_type=jnp.float32
            )
            * score_scale
        )
        value_grad = value_grad + jnp.einsum(
            "kgqs,qkgd->skd",
            probability.astype(jnp.bfloat16),
            grad_block,
            preferred_element_type=jnp.float32,
        )
        return ((key_grad, value_grad), query_grad)

    zero_grads = jnp.zeros(key_vectors.shape, jnp.float32)
    finals, query_grad = lax.scan(
        one_block, (zero_grads, zero_grads), (jnp.arange(block_total, dtype=jnp.int32), log_totals)
    )
    return (query_grad, finals[0], finals[1])


def silu_gate(gate_value, upper_value):
    return jax.nn.silu(gate_value) * upper_value


def owners(unit_count):
    return jnp.arange(unit_count, dtype=jnp.int32) // GROUPS


def gate_up_of(inputs, weight_piece):
    return jnp.einsum(
        "ncd,nkfd->nkfc", inputs, weight_piece[:, 0:2], preferred_element_type=jnp.float32
    )


def on_device(
    activations,
    targets,
    lengths,
    token_mask,
    routes,
    route_weights,
    norm_gains,
    attention_master,
    expert_master,
    attention_left,
    attention_right,
    attention_left_root,
    attention_right_root,
    expert_left,
    expert_right,
    expert_left_root,
    expert_right_root,
):
    own_rows = activations.shape[0]
    tensor_size = lax.axis_size("tensor")
    tokens_total = own_rows * tensor_size * lax.axis_size("dp")
    seq_length = lengths[0]
    position = lax.axis_index("tensor") * own_rows + jnp.arange(own_rows, dtype=jnp.int32)
    valid_rows = ((token_mask == 1) & (position < seq_length)).astype(jnp.float32)
    valid_total = lax.psum(jnp.sum(valid_rows), ("dp", "tensor"))
    attention_full = lax.all_gather(attention_master.astype(jnp.bfloat16), "dp", axis=0, tiled=True)
    heads_here = HEADS // tensor_size
    kv_here = KV_HEADS // tensor_size
    group_size = HEADS // KV_HEADS
    query_cols = heads_here * HEAD_DIM
    key_cols = kv_here * HEAD_DIM
    qkv_cols = query_cols + 2 * key_cols
    w_qkv = attention_full[:, :qkv_cols]
    w_output = attention_full[:, qkv_cols:]
    hidden = activations.astype(jnp.float32)
    normed_own, attention_scaling = normalize(hidden, norm_gains[0])
    normed = gather_rows(normed_own.astype(jnp.bfloat16))
    seq_rows = normed.shape[0]
    cosine, sine = rope_tables(seq_rows)
    projected = product(normed, w_qkv)
    queries = rotate(
        projected[:, :query_cols].reshape(seq_rows, heads_here, HEAD_DIM), cosine, sine
    )
    queries = queries.astype(jnp.bfloat16).reshape(seq_rows, kv_here, group_size, HEAD_DIM)
    key_vectors = rotate(
        projected[:, query_cols : query_cols + key_cols].reshape(seq_rows, kv_here, HEAD_DIM),
        cosine,
        sine,
    ).astype(jnp.bfloat16)
    value_vectors = (
        projected[:, query_cols + key_cols :]
        .reshape(seq_rows, kv_here, HEAD_DIM)
        .astype(jnp.bfloat16)
    )
    attended, log_totals = attention_forward(queries, key_vectors, value_vectors, seq_length)
    attended = attended.reshape(seq_rows, query_cols)
    branch = sum_rows(
        jnp.einsum("tc,dc->td", attended, w_output, preferred_element_type=jnp.float32)
    )
    middle = hidden + branch
    mix_own, mix_scaling = normalize(middle, norm_gains[1])
    normed_mix = gather_rows(mix_own.astype(jnp.bfloat16))
    flat_routes = routes.reshape(-1)
    route_total = flat_routes.shape[0]
    expert_ids = jnp.arange(EXPERTS, dtype=jnp.int32)
    one_hot = (flat_routes[:, None] == expert_ids[None, :]).astype(jnp.int32)
    earlier = jnp.cumsum(one_hot, axis=0) - one_hot
    slot_place = flat_routes * CAP + jnp.sum(earlier * one_hot, axis=1)
    source_row = (
        jnp.zeros((EXPERTS * CAP,), jnp.int32)
        .at[slot_place]
        .set(jnp.arange(route_total, dtype=jnp.int32) // TOPK)
    )
    slot_gate = (
        jnp.zeros((EXPERTS * CAP,), jnp.float32).at[slot_place].set(route_weights.reshape(-1))
    )
    dispatched = jnp.take(normed_mix, source_row, axis=0).reshape(EXPERTS, CAP, D)
    expert_low = expert_master.astype(jnp.bfloat16)
    unit_here = expert_low.shape[0]
    slice_rows = expert_low.shape[2]
    preact_start = jnp.zeros((1,), jnp.float32)
    weight_start = jnp.zeros((1,), jnp.bfloat16)
    weight_piece = lax.all_gather(expert_low, "dp", axis=0, tiled=True)
    mixed_slots = jnp.zeros((EXPERTS, CAP, D), jnp.float32)
    kept_preacts = preact_start
    kept_weights = weight_start
    owner_ids = owners(weight_piece.shape[0])
    gate_up = gate_up_of(jnp.take(dispatched, owner_ids, axis=0), weight_piece)
    inner_value = (jax.nn.silu(gate_up[:, 0]) * gate_up[:, 1]).astype(jnp.bfloat16)
    result = jnp.einsum(
        "nfc,nfd->ncd", inner_value, weight_piece[:, 2], preferred_element_type=jnp.float32
    )
    mixed_slots = mixed_slots.at[owner_ids].add(result)
    forward_inner_all = inner_value
    mixed_slots, inner_all, kept_preacts, kept_weights = (
        mixed_slots,
        forward_inner_all,
        kept_preacts,
        kept_weights,
    )
    picked = jnp.take(mixed_slots.reshape(EXPERTS * CAP, D), slot_place, axis=0).reshape(
        seq_rows, TOPK, D
    )
    mixed_rows = sum_rows(jnp.sum(route_weights[:, :, None] * picked, axis=1))
    output = middle + mixed_rows
    residual_error = output - targets
    loss_part = jnp.sum(valid_rows[:, None] * residual_error * residual_error)
    output_grad = 2.0 / valid_total * valid_rows[:, None] * residual_error
    output_low = gather_rows(output_grad.astype(jnp.bfloat16))
    slot_grad = (
        (slot_gate[:, None] * jnp.take(output_low, source_row, axis=0))
        .astype(jnp.bfloat16)
        .reshape(EXPERTS, CAP, D)
    )
    weight_piece = lax.all_gather(expert_low, "dp", axis=0, tiled=True)
    input_slots = jnp.zeros((EXPERTS, CAP, D), jnp.float32)
    unit_count = weight_piece.shape[0]
    owner_ids = owners(unit_count)
    gate_up = gate_up_of(jnp.take(dispatched, owner_ids, axis=0), weight_piece)
    inner_grad = jnp.einsum(
        "ncd,nfd->nfc",
        jnp.take(slot_grad, owner_ids, axis=0),
        weight_piece[:, 2],
        preferred_element_type=jnp.float32,
    )
    unused_value, pullback = jax.vjp(silu_gate, gate_up[:, 0], gate_up[:, 1])
    gate_grad, upper_grad = pullback(inner_grad)
    preact_low = jnp.stack([gate_grad, upper_grad], axis=1).astype(jnp.bfloat16)
    input_slots = input_slots.at[owner_ids].add(
        jnp.einsum(
            "nkfc,nkfd->ncd", preact_low, weight_piece[:, 0:2], preferred_element_type=jnp.float32
        )
    )
    backward_preact_grad = preact_low
    input_slots, preact_grad = (input_slots, backward_preact_grad)
    mix_part = jnp.sum(
        jnp.take(input_slots.reshape(EXPERTS * CAP, D), slot_place, axis=0).reshape(
            seq_rows, TOPK, D
        ),
        axis=1,
    )
    mix_back, gain_mix = normalize_back(middle, mix_scaling, norm_gains[1], sum_rows(mix_part))
    middle_grad = output_grad + mix_back
    owner_ids = owners(lax.axis_size("dp") * unit_here)
    inner_value = inner_all
    preact_low = preact_grad
    gate_up_grad = jnp.einsum(
        "nkfc,ncd->nkfd",
        preact_low,
        jnp.take(dispatched, owner_ids, axis=0),
        preferred_element_type=jnp.float32,
    )
    down_grad = jnp.einsum(
        "nfc,ncd->nfd",
        inner_value,
        jnp.take(slot_grad, owner_ids, axis=0),
        preferred_element_type=jnp.float32,
    )
    expert_grad = lax.psum_scatter(
        jnp.concatenate([gate_up_grad, down_grad[:, None]], axis=1),
        "dp",
        scatter_dimension=0,
        tiled=True,
    )
    branch_low = gather_rows(middle_grad.astype(jnp.bfloat16))
    attended_grad = product(branch_low, w_output).astype(jnp.bfloat16)
    query_grad, key_grad, value_grad = attention_backward(
        queries,
        key_vectors,
        value_vectors,
        attended_grad.reshape(seq_rows, kv_here, group_size, HEAD_DIM),
        log_totals,
        seq_length,
    )
    query_grad = rotate(query_grad.reshape(seq_rows, heads_here, HEAD_DIM), cosine, -sine)
    key_grad = rotate(key_grad, cosine, -sine)
    qkv_grad = jnp.concatenate(
        [
            query_grad.reshape(seq_rows, query_cols),
            key_grad.reshape(seq_rows, key_cols),
            value_grad.reshape(seq_rows, key_cols),
        ],
        axis=1,
    ).astype(jnp.bfloat16)
    normed_grad = sum_rows(
        jnp.einsum("tc,dc->td", qkv_grad, w_qkv, preferred_element_type=jnp.float32)
    )
    attention_back, gain_attention = normalize_back(
        hidden, attention_scaling, norm_gains[0], normed_grad
    )
    input_grad = middle_grad + attention_back
    qkv_part = jnp.einsum("tr,tc->rc", normed, qkv_grad, preferred_element_type=jnp.float32)
    output_part = jnp.einsum("tr,tc->rc", branch_low, attended, preferred_element_type=jnp.float32)
    attention_grad = lax.psum_scatter(
        jnp.concatenate([qkv_part, output_part], axis=1), "dp", scatter_dimension=0, tiled=True
    )
    loss_total, gain_grad = lax.psum(
        (loss_part, jnp.stack([gain_attention, gain_mix])), ("dp", "tensor")
    )
    mean_loss = loss_total / valid_total
    gains_new = norm_gains - gain_rate * tokens_total**0.5 * gain_grad
    rows_here = attention_grad.shape[0]
    attention_blocks = attention_grad.reshape(rows_here, -1, BLOCK).transpose(1, 0, 2)
    attention_left_new = stat_decay * attention_left[0] + jnp.einsum(
        "bik,bjk->bij", attention_blocks, attention_blocks, precision=highest
    )
    attention_right_new = stat_decay * attention_right[0] + jnp.einsum(
        "bki,bkj->bij", attention_blocks, attention_blocks, precision=highest
    )
    attention_step = jnp.einsum(
        "bij,bjk->bik", attention_left_root[0], attention_blocks, precision=highest
    )
    attention_step = jnp.einsum(
        "bik,bkl->bil", attention_step, attention_right_root[0], precision=highest
    )
    attention_new = attention_master - D ** (-0.5) * attention_step.transpose(1, 0, 2).reshape(
        rows_here, -1
    )
    block_count = D // BLOCK
    expert_blocks = expert_grad.reshape(unit_here, 3, slice_rows, block_count, BLOCK).transpose(
        0, 1, 3, 2, 4
    )
    expert_left_new = stat_decay * expert_left + jnp.einsum(
        "...ik,...jk->...ij", expert_blocks, expert_blocks, precision=highest
    )
    expert_right_new = stat_decay * expert_right + jnp.einsum(
        "...ki,...kj->...ij", expert_blocks, expert_blocks, precision=highest
    )
    expert_step = jnp.einsum(
        "...ij,...jk->...ik", expert_left_root, expert_blocks, precision=highest
    )
    expert_step = jnp.einsum(
        "...ik,...kl->...il", expert_step, expert_right_root, precision=highest
    )
    expert_new = expert_master - D ** (-0.5) * expert_step.transpose(0, 1, 3, 2, 4).reshape(
        expert_master.shape
    )
    return (
        output,
        mean_loss,
        input_grad,
        gain_grad,
        gains_new,
        attention_grad,
        attention_left_new[None],
        attention_right_new[None],
        attention_new,
        expert_grad,
        expert_left_new,
        expert_right_new,
        expert_new,
    )


def solution(mesh):
    return jax.shard_map(
        on_device,
        mesh=mesh,
        in_specs=(
            P(("dp", "tensor"), None),
            P(("dp", "tensor"), None),
            P("dp"),
            P(("dp", "tensor")),
            P("dp", None),
            P("dp", None),
            P(),
            P("dp", "tensor"),
            P("dp", None, "tensor", None),
            P("dp", "tensor", None, None),
            P("dp", "tensor", None, None),
            P("dp", "tensor", None, None),
            P("dp", "tensor", None, None),
            P("dp", None, None, "tensor", None),
            P("dp", None, "tensor", None, None),
            P("dp", None, None, "tensor", None),
            P("dp", None, "tensor", None, None),
        ),
        out_specs=(
            P(("dp", "tensor"), None),
            P(),
            P(("dp", "tensor"), None),
            P(),
            P(),
            P("dp", "tensor"),
            P("dp", "tensor", None, None),
            P("dp", "tensor", None, None),
            P("dp", "tensor"),
            P("dp", None, "tensor", None),
            P("dp", None, None, "tensor", None),
            P("dp", None, "tensor", None, None),
            P("dp", None, "tensor", None),
        ),
        check_vma=False,
    )
```

profile of v0, /device:TPU:0, one launch (start us, length us, event | category | flops | bytes accessed | tf_op | source)
XLA Modules:
  0.0 4026.4 jit_solution(2642923830572679207)
XLA Ops:
  27.3 72.7 %all-gather.9.cloned.1.call-done = bf16[1024,1536]{1,0:T(8,128)(2,1)} async-done(((bf16[64,1536]{1,0:T(8,128)(2,1)}), bf16[1024,1536]{1,0:T(8,128)(2,1)}) %all-gather.9.cloned.1.call-update) | async-done | bytes 3145744 | tf_op jit(solution)/shard_map/all_gather | solution.py:185
  108.3 33.0 while.33
  174.8 19.2 reduce-window.6
  202.3 30.5 scatter_custom_fusion
  234.7 62.1 %gather_fusion = bf16[12288,1024]{1,0:T(8,128)(2,1)} fusion(bf16[1024,1024]{1,0:T(8,128)(2,1)} %all-gather.11.cloned.1.call-done, s32[12288]{0:T(1024)S(1)} %fusion.119), kind=kCustom, calls=%fused_computation.clone | custom fusion | bytes 50380800 | tf_op jit(solution)/shard_map/jit(_take)/gather | solution.py:236
  296.7 21.2 broadcast_select_fusion.6
  317.9 44.1 %gather_fusion.1 = bf16[128,384,1024]{2,1,0:T(8,128)(2,1)} fusion(bf16[32,384,1024]{2,1,0:T(8,128)(2,1)} %bitcast.331, s32[1024]{0:T(1024)S(1)} %pad_clamp_fusion), kind=kCustom, calls=%fused_computation.1.clone | custom fusion | bytes 201327104 | tf_op jit(solution)/shard_map/jit(_take)/gather | solution.py:247
  362.0 329.1 %all-gather.13.cloned.1.call-done = bf16[128,3,64,1024]{3,2,1,0:T(8,128)(2,1)} async-done(((bf16[8,3,64,1024]{3,2,1,0:T(8,128)(2,1)}), bf16[128,3,64,1024]{3,2,1,0:T(8,128)(2,1)}) %all-gather.13.cloned.1.call-update) | async-done | bytes 50331664 | tf_op jit(solution)/shard_map/all_gather | solution.py:242
  691.1 54.2 %fusion.69 = f32[128,2,64,384]{3,2,1,0:T(8,128)} fusion(bf16[128,384,1024]{2,1,0:T(8,128)(2,1)} %gather_fusion.1, pred[128]{0:T(512)(128)(4,1)S(1)} %compare_and_fusion.4, bf16[128,3,64,1024]{3,2,1,0:T(8,128)(2,1)} %all-gather.13.cloned.1.call-done), kind=kOutput, calls=%fused_computation.128 | convolution fusion | flops 12935233536 | bytes 159383680 | tf_op jit(solution)/shard_map/ncd,nkfd->nkfc/dot_general | solution.py:154
  757.7 75.5 %fusion.61 = f32[128,384,1024]{2,1,0:T(8,128)} fusion(bf16[128,64,384]{2,1,0:T(8,128)(2,1)} %multiply_convert_fusion.1, bf16[128,3,64,1024]{3,2,1,0:T(8,128)(2,1)} %all-gather.13.cloned.1.call-done), kind=kOutput, calls=%fused_computation.113 | convolution fusion | flops 6442450944 | bytes 224395264 | tf_op jit(solution)/shard_map/nfc,nfd->ncd/dot_general | solution.py:249
  849.5 410.6 %scatter_fusion = f32[32,384,1024]{2,1,0:T(8,128)} fusion(f32[32,384,1024]{2,1,0:T(8,128)} %broadcast.576.clone, s32[128]{0:T(128)S(1)} %copy-done.52, f32[128,384,1024]{2,1,0:T(8,128)} %fusion.61), kind=kCustom, calls=%fused_computation.7 | custom fusion | flops 50331648 | bytes 603980288 | tf_op jit(solution)/shard_map/scatter-add | solution.py:252
  1260.1 59.1 %gather_fusion.2 = f32[8192,1024]{1,0:T(8,128)} fusion(f32[12288,1024]{1,0:T(8,128)} %bitcast.329, s32[8192]{0:T(1024)S(1)} %copy-done.22), kind=kCustom, calls=%fused_computation.2.clone | custom fusion | bytes 67141632 | tf_op jit(solution)/shard_map/jit(_take)/gather | solution.py:260
  1319.2 20.0 fusion.59
  1340.6 38.8 psum.22
  1386.4 30.6 scatter_custom_fusion.2
  1417.1 62.4 %gather_fusion.3 = bf16[12288,1024]{1,0:T(8,128)(2,1)} fusion(bf16[1024,1024]{1,0:T(8,128)(2,1)} %all-gather.15.cloned.1.call-done, s32[12288]{0:T(1024)S(1)} %copy-done.21), kind=kCustom, calls=%fused_computation.3.clone | custom fusion | bytes 50380800 | tf_op jit(solution)/shard_map/jit(_take)/gather | solution.py:270
  1479.5 22.6 multiply_convert_fusion
  1502.2 44.1 %gather_fusion.4 = bf16[128,384,1024]{2,1,0:T(8,128)(2,1)} fusion(bf16[32,384,1024]{2,1,0:T(8,128)(2,1)} %bitcast.330, s32[1024]{0:T(1024)} %copy-done.48), kind=kCustom, calls=%fused_computation.4.clone | custom fusion | bytes 201327104 | tf_op jit(solution)/shard_map/jit(_take)/gather | solution.py:281
  1546.2 55.0 %fusion.75 = (bf16[128,1,64,384]{3,2,0,1:T(8,128)(2,1)}, bf16[128,1,64,384]{3,2,0,1:T(8,128)(2,1)}) fusion(f32[128,2,64,384]{3,2,1,0:T(8,128)} %fusion.69, bf16[128,3,64,1024]{3,2,1,0:T(8,128)(2,1)} %all-gather.13.cloned.1.call-done, bf16[128,384,1024]{2,1,0:T(8,128)(2,1)} %gather_fusion.4, pred[128]{0:T(512)(128)(4,1)S(1)} %copy-done.57), kind=kOutput, calls=%fused_computation.135 | convolution fusion | flops 6536822784 | bytes 155189376 | tf_op jit(solution)/shard_map/ncd,nfd->nfc/dot_general | solution.py:279
  1601.2 83.7 %convolution_bitcast_fusion.1 = f32[128,384,1024]{2,1,0:T(8,128)} fusion(bf16[128,1,64,384]{3,2,0,1:T(8,128)(2,1)} %get-tuple-element.450, bf16[128,1,64,384]{3,2,0,1:T(8,128)(2,1)} %get-tuple-element.449, bf16[128,3,64,1024]{3,2,1,0:T(8,128)(2,1)} %all-gather.13.cloned.1.call-done), kind=kOutput, calls=%fused_computation.101 | convolution fusion | flops 12891193344 | bytes 247463936 | tf_op jit(solution)/shard_map/nkfc,nkfd->ncd/dot_general | solution.py:289
  1701.2 411.2 %scatter_fusion.1 = f32[32,384,1024]{2,1,0:T(8,128)} fusion(f32[32,384,1024]{2,1,0:T(8,128)} %broadcast.576, s32[128]{0:T(128)S(1)} %copy-done.53, f32[128,384,1024]{2,1,0:T(8,128)} %convolution_bitcast_fusion.1), kind=kCustom, calls=%fused_computation.9 | custom fusion | flops 50331648 | bytes 603980288 | tf_op jit(solution)/shard_map/scatter-add | solution.py:288
  2112.4 59.1 %gather_fusion.5 = f32[8192,1024]{1,0:T(8,128)} fusion(f32[12288,1024]{1,0:T(8,128)} %bitcast.328, s32[8192]{0:T(1024)S(1)} %copy-done.23), kind=kCustom, calls=%fused_computation.5.clone | custom fusion | bytes 67141632 | tf_op jit(solution)/shard_map/jit(_take)/gather | solution.py:296
  2228.2 151.7 %while.34 = (s32[]{:T(128)}, f32[1024,4,64]{0,2,1:T(8,128)}, f32[1024,4,64]{0,2,1:T(8,128)}, f32[2,512,4,2,64]{1,0,4,3,2:T(2,128)}, s32[2]{0:T(128)S(1)}, /*inde...) while((s32[]{:T(128)}, f32[1024,4,64]{0,2,1:T(8,128)}, ...), condition=%wide.region_25.29_spmd.clone, body=%wide.region_23.28_spmd.clone.sunk | while | flops 2724738048 | bytes 184121680 | solution.py:139
  2269.6 19.7 dynamic_update_slice.32
  2345.2 19.7 dynamic_update_slice.32
  2411.8 46.6 %fusion.62 = f32[128,1,64,1024]{3,2,1,0:T(8,128)} fusion(bf16[128,64,384]{2,1,0:T(8,128)(2,1)} %multiply_convert_fusion.1, bf16[128,384,1024]{2,1,0:T(8,128)(2,1)} %gather_fusion.4, pred[128]{0:T(512)(128)(4,1)S(1)} %copy-done.58), kind=kOutput, calls=%fused_computation.114 | convolution fusion | flops 6492782592 | bytes 140509312 | tf_op jit(solution)/shard_map/nfc,ncd->nfd/dot_general | solution.py:312
  2458.4 59.5 %fusion.53 = f32[128,2,64,1024]{3,2,1,0:T(8,128)} fusion(bf16[128,384,1024]{2,1,0:T(8,128)(2,1)} %gather_fusion.1, pred[128]{0:T(512)(128)(4,1)S(1)} %copy-done.58, bf16[128,1,64,384]{3,2,0,1:T(8,128)(2,1)} %get-tuple-element.450, bf16[128,1,64,384]{3,2,0,1:T(8,128)(2,1)} %get-tuple-element.449), kind=kOutput, calls=%fused_computation.95 | convolution fusion | flops 12941524992 | bytes 180355200 | tf_op jit(solution)/shard_map/nkfc,ncd->nkfd/dot_general | solution.py:306
  2517.9 66.7 %pad_maximum_fusion = f32[128,3,64,1024]{3,2,1,0:T(8,128)} fusion(f32[128,1,64,1024]{3,2,1,0:T(8,128)} %fusion.62, f32[128,2,64,1024]{3,2,1,0:T(8,128)} %fusion.53), kind=kLoop, calls=%fused_computation.94 | loop fusion | flops 25165824 | bytes 201326592 | tf_op jit(solution)/shard_map/concatenate | solution.py:319
  2587.9 43.9 %all-reduce.1 = (f32[]{:T(128)}, f32[2,1024]{1,0:T(2,128)S(1)}) all-reduce(f32[]{:T(128)} %get-tuple-element.451, f32[2,1024]{1,0:T(2,128)S(1)} %pad_maximum_fusion.10), channel_id=1, replica_groups=mesh['dp'=16,'tensor'=2] {'dp','tensor'}, use_global_device_ids=true, to_apply=%region_15.19 | all-reduce | flops 2049 | bytes 16392 | tf_op jit(solution)/shard_map/psum | solution.py:356
  2652.4 1284.7 %reduce-scatter.21.cloned.1.call-done = f32[8,3,64,1024]{3,2,1,0:T(8,128)} async-done(((f32[128,3,64,1024]{3,2,1,0:T(8,128)}), f32[8,3,64,1024]{3,2,1,0:T(8,128)}) %reduce-scatter.21.cloned.1.call-update) | async-done | bytes 6291472
  3937.1 30.6 multiply_add_fusion
  3976.0 23.3 multiply_bitcast_fusion
  (302 shorter events, 404.0 us)
Async XLA Ops:
  7.2 3960.6 %copy-start = (f32[8,3,4,64,64]{4,3,2,1,0:T(8,128)S(1)}, f32[8,3,4,64,64]{4,3,2,1,0:T(8,128)}, u32[]{:S(2)}) copy-start(f32[8,3,4,64,64]{4,3,2,1,0:T(8,128)} %param.42) | copy-start | bytes 4718596
  7.2 20.1 all-gather.7.cloned.1.call-start
  13.9 86.1 %all-gather.9.cloned.1.call-start = ((), (), s32[]{:S(2)}) async-start(), calls=%async_computation.7 | async-start | bytes 3342336 | tf_op jit(solution)/shard_map/all_gather | solution.py:185
  15.7 144.5 %reduce-scatter.11.cloned.1.call-start = ((), (), s32[]{:S(2)}) async-start(), calls=%async_computation.8 | async-start | bytes 6291456 | tf_op jit(solution)/shard_map/reduce_scatter | solution.py:65
  17.0 89.1 %copy-start.8 = (f32[1024,32]{0,1:T(8,128)}, f32[1024,32]{0,1:T(8,128)S(1)}, u32[]{:S(2)}) copy-start(f32[1024,32]{0,1:T(8,128)S(1)} %get-tuple-element.468) | copy-start | bytes 393220
  149.5 85.2 %all-gather.11.cloned.1.call-start = ((), (), s32[]{:S(2)}) async-start(), calls=%async_computation.9 | async-start | bytes 3145728 | tf_op jit(solution)/shard_map/all_gather | solution.py:61
  165.0 526.1 %all-gather.13.cloned.1.call-start = ((), (), s32[]{:S(2)}) async-start(), calls=%async_computation.10 | async-start | bytes 53477376 | tf_op jit(solution)/shard_map/all_gather | solution.py:242
  170.0 1210.1 %reduce-scatter.13.cloned.1.call-start = ((), (), s32[]{:S(2)}) async-start(), calls=%async_computation.11 | async-start | bytes 6291456 | tf_op jit(solution)/shard_map/reduce_scatter | solution.py:65
  202.3 94.5 %copy-start.38 = (s32[8192,1]{0,1:T(1,128)}, s32[8192,1]{0,1:T(1,128)S(1)}, u32[]{:S(2)}) copy-start(s32[8192,1]{0,1:T(1,128)S(1)} %compare_select_fusion) | copy-start | bytes 98308
  232.8 458.3 %copy-start.56 = (pred[128]{0:T(512)(128)(4,1)}, pred[128]{0:T(512)(128)(4,1)S(1)}, u32[]{:S(2)}) copy-start(pred[128]{0:T(512)(128)(4,1)S(1)} %compare_and_fusion.4) | copy-start | bytes 388
  233.3 84.6 %copy-start.48 = (s32[1024]{0:T(1024)}, s32[1024]{0:T(1024)S(1)}, u32[]{:S(2)}) copy-start(s32[1024]{0:T(1024)S(1)} %pad_clamp_fusion) | copy-start | bytes 12292
  234.6 62.1 %copy-start.27 = (pred[12288]{0:T(1024)(128)(4,1)}, pred[12288]{0:T(1024)(128)(4,1)S(1)}, u32[]{:S(2)}) copy-start(pred[12288]{0:T(1024)(128)(4,1)S(1)} %compare_and_fusion.2) | copy-start | bytes 36868
  234.6 62.1 %copy-start.20 = (s32[12288]{0:T(1024)}, s32[12288]{0:T(1024)S(1)}, u32[]{:S(2)}) copy-start(s32[12288]{0:T(1024)S(1)} %fusion.119) | copy-start | bytes 147460
  849.5 410.6 %copy-start.22 = (s32[8192]{0:T(1024)S(1)}, s32[8192]{0:T(1024)}, u32[]{:S(2)}) copy-start(s32[8192]{0:T(1024)} %broadcast_clamp_fusion) | copy-start | bytes 98308
  1260.1 59.1 %copy-start.29 = (pred[8192]{0:T(1024)(128)(4,1)S(1)}, pred[8192]{0:T(1024)(128)(4,1)}, u32[]{:S(2)}) copy-start(pred[8192]{0:T(1024)(128)(4,1)} %compare_and_fusion.3) | copy-start | bytes 24580
  1339.3 77.8 %copy-start.21 = (s32[12288]{0:T(1024)S(1)}, s32[12288]{0:T(1024)}, u32[]{:S(2)}) copy-start(s32[12288]{0:T(1024)} %copy-done.20) | copy-start | bytes 147460
  1339.3 77.8 %all-gather.15.cloned.1.call-start = ((), (), s32[]{:S(2)}) async-start(), calls=%async_computation.12 | async-start | bytes 3145728 | tf_op jit(solution)/shard_map/all_gather | solution.py:61
  1340.6 44.5 %copy-start.49 = (pred[512]{0:T(512)(128)(4,1)}, pred[512]{0:T(512)(128)(4,1)S(1)}, u32[]{:S(2)}) copy-start(pred[512]{0:T(512)(128)(4,1)S(1)} %get-tuple-element.442) | copy-start | bytes 1540
  1385.1 817.6 %reduce-scatter.15.cloned.1.call-start = ((), (), s32[]{:S(2)}) async-start(), calls=%async_computation.13 | async-start | bytes 6291456 | tf_op jit(solution)/shard_map/reduce_scatter | solution.py:65
  1417.1 62.5 %copy-start.28 = (pred[12288]{0:T(1024)(128)(4,1)S(1)}, pred[12288]{0:T(1024)(128)(4,1)}, u32[]{:S(2)}) copy-start(pred[12288]{0:T(1024)(128)(4,1)} %copy-done.27) | copy-start | bytes 36868
  1502.2 44.1 %copy-start.57 = (pred[128]{0:T(512)(128)(4,1)S(1)}, pred[128]{0:T(512)(128)(4,1)}, u32[]{:S(2)}) copy-start(pred[128]{0:T(512)(128)(4,1)} %copy-done.56) | copy-start | bytes 388
  1701.2 411.2 %copy-start.23 = (s32[8192]{0:T(1024)S(1)}, s32[8192]{0:T(1024)}, u32[]{:S(2)}) copy-start(s32[8192]{0:T(1024)} %broadcast_clamp_fusion) | copy-start | bytes 98308
  2112.4 59.1 %copy-start.30 = (pred[8192]{0:T(1024)(128)(4,1)S(1)}, pred[8192]{0:T(1024)(128)(4,1)}, u32[]{:S(2)}) copy-start(pred[8192]{0:T(1024)(128)(4,1)} %compare_and_fusion.3) | copy-start | bytes 24580
  2171.6 31.2 copy-start.34
  2189.6 34.4 all-gather.17.cloned.1.call-start
  2212.0 372.7 %reduce-scatter.17.cloned.1.call-start = ((), (), s32[]{:S(2)}) async-start(), calls=%async_computation.15 | async-start | bytes 6291456 | tf_op jit(solution)/shard_map/reduce_scatter | solution.py:65
  2228.2 155.9 %copy-start.9 = (f32[1024,32]{0,1:T(8,128)S(1)}, f32[1024,32]{0,1:T(8,128)}, u32[]{:S(2)}) copy-start(f32[1024,32]{0,1:T(8,128)} %copy-done.8) | copy-start | bytes 393220
  2228.2 155.9 %copy-start.12 = (f32[1024,32]{0,1:T(8,128)S(1)}, f32[1024,32]{0,1:T(8,128)}, u32[]{:S(2)}) copy-start(f32[1024,32]{0,1:T(8,128)} %get-tuple-element.466) | copy-start | bytes 393220
  2394.5 243.8 %reduce-scatter.19.cloned.1.call-start = ((), (), s32[]{:S(2)}) async-start(), calls=%async_computation.16 | async-start | bytes 6684672
  2411.1 1526.0 %reduce-scatter.21.cloned.1.call-start = ((), (), s32[]{:S(2)}) async-start(), calls=%async_computation.17 | async-start | bytes 106954752
  2584.6 48.5 %copy-start.39 = (f32[2,1024]{1,0:T(2,128)S(1)}, f32[2,1024]{1,0:T(2,128)}, u32[]{:S(2)}) copy-start(f32[2,1024]{1,0:T(2,128)} %param.33) | copy-start | bytes 24580
  2584.6 49.1 %copy-start.45 = (f32[512]{0:T(512)S(1)}, f32[512]{0:T(512)}, u32[]{:S(2)}) copy-start(f32[512]{0:T(512)} %get-tuple-element.462) | copy-start | bytes 6148
  (46 other events, 396.7 us)
Sparse Core Ops, SparseCore 0:
  14.0 13.2 all-gather.6
  30.7 69.2 all-gather.8
  149.6 10.5 reduce-scatter.10
  165.1 11.8 all-gather.10
  180.6 510.5 all-gather.12
  1339.4 10.2 reduce-scatter.12
  1385.2 11.4 all-gather.14
  2189.7 12.9 reduce-scatter.14
  2212.1 11.8 all-gather.16
  2394.6 13.1 reduce-scatter.16
  2413.7 146.9 reduce-scatter.18
  2584.8 1352.3 reduce-scatter.20
where the time goes:
time: 4040 us; the launch traced here: 4030 us
  waiting for transfers between devices  1730 us (43%)
  other arithmetic  1100 us (27%)
  matrix products  575 us (14%)
  local copies, waits for them, and re-layouts  511 us (13%)
  blocking collectives  82.7 us (2%)
    unnamed x14, waiting for transfers between devices  1280 us
    scatter-add x1, other arithmetic, on_device(): input_slots.at[owner_ids]  411 us
    scatter-add x1, other arithmetic, on_device(): mixed_slots = mixed_slots.at[owner_ids].add(result)  411 us
    all_gather x1, waiting for transfers between devices, on_device(): weight_piece = lax.all_gather(expert_low, 'dp', axis=0, tiled=True)  329 us
    dot_general x1, matrix products, on_device(): jnp.einsum('nkfc,nkfd->ncd', preact_low, weight_piece[:, 0:2], preferred_...  83.7 us
  transfers between devices with their start and end apart: 12, of which 7 were waited for; matrix products, arithmetic and copies ran while one was open for 11% of the time, Pallas kernels for 0%

commit v1 on v0

v1 whole, which is shorter than its diff:
```python
import functools

import jax
import jax.numpy as jnp
from jax import lax
from jax.experimental import pallas as pl
from jax.experimental.pallas import tpu as pltpu
from jax.sharding import PartitionSpec as P

D = 1024
HEADS = 16
KV_HEADS = 8
HEAD_DIM = 64
EXPERTS = 32
TOPK = 8
BLK = 256
GROUPS = 4
BLOCK = 256
LANES = 128

epsilon = 1e-05
stat_decay = 0.9
gain_rate = 0.02
theta_base = 10000.0
masked_score = -1e30
MIB = 1 << 20

TOKEN_MASKS = (0, 1, 2, 3)
WEIGHT_BITS = (4, 8)


def dot(left, right, left_dim, right_dim):
    return lax.dot_general(
        left, right, (((left_dim,), (right_dim,)), ((), ())), preferred_element_type=jnp.float32
    )


def normalize(hidden, gain):
    scaling = lax.rsqrt(jnp.mean(hidden * hidden, axis=-1, keepdims=True) + epsilon)
    return (hidden * scaling * gain, scaling)


def normalize_back(hidden, scaling, gain, upstream):
    weighted = upstream * gain
    center = jnp.mean(weighted * hidden, axis=-1, keepdims=True)
    input_part = scaling * weighted - hidden * (scaling * scaling * scaling) * center
    return (input_part, jnp.sum(upstream * hidden * scaling, axis=0))


def swap_dp(values, mask):
    count = lax.axis_size("dp")
    return lax.ppermute(values, "dp", [(i, i ^ mask) for i in range(count)])


def swap_core(values):
    count = lax.axis_size("tensor")
    return lax.ppermute(values, "tensor", [(i, i ^ 1) for i in range(count)])


def sum_everywhere(values):
    values = values + swap_core(values)
    mask = 1
    while mask < lax.axis_size("dp"):
        values = values + swap_dp(values, mask)
        mask *= 2
    return values


def in_order(own, other):
    first = lax.axis_index("tensor") == 0
    return jnp.concatenate([jnp.where(first, own, other), jnp.where(first, other, own)], axis=0)


def own_half(values):
    half = values.shape[0] // 2
    return lax.dynamic_slice_in_dim(values, lax.axis_index("tensor") * half, half, 0)


def other_half(values):
    half = values.shape[0] // 2
    return lax.dynamic_slice_in_dim(values, (1 - lax.axis_index("tensor")) * half, half, 0)


def turn(values):
    lane = lax.broadcasted_iota(jnp.int32, values.shape, 1)
    half = HEAD_DIM // 2
    return jnp.where(
        lane % HEAD_DIM < half,
        -pltpu.roll(values, LANES - half, 1),
        pltpu.roll(values, half, 1),
    )


def attention_forward_kernel(
    length_ref, x_ref, w_ref, cos_ref, sin_ref, q_ref, k_ref, v_ref, att_ref, lse_ref
):
    rows = x_ref.shape[0]
    low = jnp.bfloat16
    cosine, sine = cos_ref[...], sin_ref[...]
    lane = lax.broadcasted_iota(jnp.int32, (rows, LANES), 1)
    left = lane < HEAD_DIM
    projected = dot(x_ref[...], w_ref[...], 1, 0)
    q_raw = projected[:, :LANES]
    q_turn = turn(q_raw)
    scale = HEAD_DIM ** (-0.5)
    q_rot = (q_raw * cosine + q_turn * sine) * scale
    q_rot_turn = (q_turn * cosine - q_raw * sine) * scale
    q_ref[:, :LANES] = jnp.where(left, q_rot, pltpu.roll(q_rot_turn, HEAD_DIM, 1)).astype(low)
    q_ref[:, LANES:] = jnp.where(left, pltpu.roll(q_rot, HEAD_DIM, 1), q_rot_turn).astype(low)
    kv_raw = projected[:, LANES:]
    k_turn = turn(kv_raw)
    k_rot = kv_raw * cosine + k_turn * sine
    k_rot_turn = k_turn * cosine - kv_raw * sine
    k_ref[...] = jnp.where(left, k_rot, pltpu.roll(k_rot_turn, HEAD_DIM, 1)).astype(low)
    v_high = jnp.where(left, 0.0, kv_raw)
    v_ref[...] = v_high.astype(low)
    v_low = pltpu.roll(v_high, HEAD_DIM, 1).astype(low)
    v_high = v_high.astype(low)
    k_only = jnp.where(left, k_rot, 0.0).astype(low)
    place = lax.broadcasted_iota(jnp.int32, (1, rows), 1)
    bias = jnp.where(place < length_ref[0], 0.0, masked_score)
    for block in range(rows // BLK):
        here = pl.ds(block * BLK, BLK)
        keys = (block + 1) * BLK
        total = None
        for head in range(2):
            q_block = q_ref[here, head * LANES : (head + 1) * LANES]
            scores = dot(q_block, k_only[:keys], 1, 1) + bias[:, :keys]
            top = jnp.max(scores, axis=1, keepdims=True)
            exponent = jnp.exp(scores - top)
            denominator = jnp.sum(exponent, axis=1, keepdims=True)
            weights = (exponent * (1.0 / denominator)).astype(low)
            value = v_high if head else v_low
            part = dot(weights, value[:keys], 1, 0)
            total = part if total is None else total + part
            log_total = jnp.broadcast_to(top + jnp.log(denominator), (BLK, LANES))
            lse_ref[head * 8 : (head + 1) * 8, here] = log_total.T[:8]
        att_ref[here, :] = total.astype(low)


def attention_backward_kernel(
    length_ref,
    branch_ref,
    wo_ref,
    q_ref,
    k_ref,
    v_ref,
    lse_ref,
    cos_ref,
    sin_ref,
    dq_ref,
    dkv_ref,
    dk_sum,
    d0_sum,
    d1_sum,
):
    rows = branch_ref.shape[0]
    low = jnp.bfloat16
    lane = lax.broadcasted_iota(jnp.int32, (rows, LANES), 1)
    left = lane < HEAD_DIM
    grad = dot(branch_ref[...], wo_ref[...], 1, 0).astype(low)
    k_only = jnp.where(left, k_ref[...].astype(jnp.float32), 0.0).astype(low)
    v_high = v_ref[...]
    v_low = pltpu.roll(v_high.astype(jnp.float32), HEAD_DIM, 1).astype(low)
    place = lax.broadcasted_iota(jnp.int32, (rows, BLK), 0)
    seen = place < length_ref[0]
    dk_sum[...] = jnp.zeros_like(dk_sum)
    d0_sum[...] = jnp.zeros_like(d0_sum)
    d1_sum[...] = jnp.zeros_like(d1_sum)
    scale = HEAD_DIM ** (-0.5)
    for block in range(rows // BLK):
        here = pl.ds(block * BLK, BLK)
        keys = (block + 1) * BLK
        grad_block = grad[block * BLK : keys]
        query_grads = []
        for head in range(2):
            q_block = q_ref[here, head * LANES : (head + 1) * LANES]
            value = v_high if head else v_low
            scores = dot(k_only[:keys], q_block, 1, 1)
            log_total = lse_ref[head * 8 : head * 8 + 1, here]
            scores = jnp.where(seen[:keys], scores, masked_score)
            probability = jnp.exp(scores - log_total)
            prob_grad = dot(value[:keys], grad_block, 1, 1)
            weighted = probability * prob_grad
            center = jnp.sum(weighted, axis=0, keepdims=True)
            score_grad = (weighted - probability * center).astype(low)
            d_sum = d1_sum if head else d0_sum
            d_sum[:keys] += dot(probability.astype(low), grad_block, 1, 0)
            dk_sum[:keys] += dot(score_grad, q_block, 1, 0)
            query_grads.append(dot(score_grad, k_ref[:keys], 0, 0))
        cosine, sine = cos_ref[here, :] * scale, sin_ref[here, :] * scale
        zero, one = query_grads
        left_here = left[:BLK]
        straight = jnp.where(left_here, zero, pltpu.roll(one, HEAD_DIM, 1))
        turned = jnp.where(left_here, pltpu.roll(zero, HEAD_DIM, 1), one)
        dq_ref[here, :] = (straight * cosine - turned * sine).astype(low)
    dk_all = dk_sum[...]
    dk_rot = dk_all * cos_ref[...] - pltpu.roll(dk_all, HEAD_DIM, 1) * sin_ref[...]
    dv_all = pltpu.roll(d0_sum[...], HEAD_DIM, 1) + d1_sum[...]
    dkv_ref[...] = jnp.where(left, dk_rot, dv_all).astype(low)


def whole(shape):
    return pl.BlockSpec(shape, lambda h: (0,) * len(shape))


def columns(rows, width):
    return pl.BlockSpec((rows, width), lambda h: (0, h))


def attention_forward(length, normed, w_qkv, cosine, sine):
    rows = normed.shape[0]
    kv_here = w_qkv.shape[1] // 256
    low = jnp.bfloat16
    return pl.pallas_call(
        attention_forward_kernel,
        grid=(kv_here,),
        in_specs=[
            pl.BlockSpec(memory_space=pltpu.SMEM),
            whole((rows, D)),
            columns(D, 256),
            whole((rows, LANES)),
            whole((rows, LANES)),
        ],
        out_specs=[
            columns(rows, 256),
            columns(rows, LANES),
            columns(rows, LANES),
            columns(rows, LANES),
            pl.BlockSpec((16, rows), lambda h: (h, 0)),
        ],
        out_shape=[
            jax.ShapeDtypeStruct((rows, kv_here * 256), low),
            jax.ShapeDtypeStruct((rows, kv_here * LANES), low),
            jax.ShapeDtypeStruct((rows, kv_here * LANES), low),
            jax.ShapeDtypeStruct((rows, kv_here * LANES), low),
            jax.ShapeDtypeStruct((kv_here * 16, rows), jnp.float32),
        ],
        compiler_params=pltpu.CompilerParams(vmem_limit_bytes=50 * MIB),
        cost_estimate=pl.CostEstimate(
            flops=8_000_000_000, bytes_accessed=12_000_000, transcendentals=5_000_000
        ),
        name="attention_forward",
    )(length, normed, w_qkv, cosine, sine)


def attention_backward(length, branch_low, w_output, q2, k2, v, lse, cosine, sine):
    rows = branch_low.shape[0]
    kv_here = k2.shape[1] // LANES
    low = jnp.bfloat16
    return pl.pallas_call(
        attention_backward_kernel,
        grid=(kv_here,),
        in_specs=[
            pl.BlockSpec(memory_space=pltpu.SMEM),
            whole((rows, D)),
            columns(D, LANES),
            columns(rows, 256),
            columns(rows, LANES),
            columns(rows, LANES),
            pl.BlockSpec((16, rows), lambda h: (h, 0)),
            whole((rows, LANES)),
            whole((rows, LANES)),
        ],
        out_specs=[columns(rows, LANES), columns(rows, LANES)],
        out_shape=[
            jax.ShapeDtypeStruct((rows, kv_here * LANES), low),
            jax.ShapeDtypeStruct((rows, kv_here * LANES), low),
        ],
        scratch_shapes=[pltpu.VMEM((rows, LANES), jnp.float32)] * 3,
        compiler_params=pltpu.CompilerParams(vmem_limit_bytes=50 * MIB),
        cost_estimate=pl.CostEstimate(
            flops=20_000_000_000, bytes_accessed=12_000_000, transcendentals=5_000_000
        ),
        name="attention_backward",
    )(length, branch_low, w_output, q2, k2, v, lse, cosine, sine)


CHUNK = 256
TILE = 512


def chunk_weights(shard_refs, chunk, kind):
    units = shard_refs[0].shape[0]
    per_shard = units // 4
    ref = shard_refs[chunk // per_shard]
    start = (chunk % per_shard) * 4
    return ref[start : start + 4, kind].reshape(CHUNK, D)


def spread_weights(route_ref, chunk, per_chunk):
    if per_chunk == 1:
        return route_ref[:, chunk : chunk + 1]
    rows = route_ref.shape[0]
    pieces = [
        jnp.broadcast_to(route_ref[:, chunk * 4 + j : chunk * 4 + j + 1], (rows, CHUNK // 4))
        for j in range(4)
    ]
    return jnp.concatenate(pieces, axis=1)


def expert_forward_kernel(
    chunks, per_chunk, x_ref, route_ref, s0, s1, s2, s3, mixed_ref, slope_ref, silu_ref, inner_ref
):
    shards = (s0, s1, s2, s3)
    low = jnp.bfloat16
    x = x_ref[...]
    total = None
    for chunk in range(chunks):
        here = slice(chunk * CHUNK, (chunk + 1) * CHUNK)
        gate = dot(x, chunk_weights(shards, chunk, 0), 1, 1)
        upper = dot(x, chunk_weights(shards, chunk, 1), 1, 1)
        weight = spread_weights(route_ref, chunk, per_chunk)
        sigmoid = 0.5 * jnp.tanh(0.5 * gate) + 0.5
        silu = gate * sigmoid
        weighted_upper = weight * upper
        slope_ref[:, here] = (weighted_upper * (sigmoid + silu * (1.0 - sigmoid))).astype(low)
        silu_ref[:, here] = (weight * silu).astype(low)
        inner = (silu * weighted_upper).astype(low)
        inner_ref[:, here] = inner
        part = dot(inner, chunk_weights(shards, chunk, 2), 1, 0)
        total = part if total is None else total + part
    mixed_ref[...] = total.astype(low)


def expert_backward_kernel(
    chunks, grad_ref, slope_ref, silu_ref, s0, s1, s2, s3, input_ref, gate_ref, upper_ref
):
    shards = (s0, s1, s2, s3)
    low = jnp.bfloat16
    grad = grad_ref[...]
    total = None
    for chunk in range(chunks):
        here = slice(chunk * CHUNK, (chunk + 1) * CHUNK)
        inner_grad = dot(grad, chunk_weights(shards, chunk, 2), 1, 1)
        gate_grad = (inner_grad * slope_ref[:, here].astype(jnp.float32)).astype(low)
        upper_grad = (inner_grad * silu_ref[:, here].astype(jnp.float32)).astype(low)
        gate_ref[:, here] = gate_grad
        upper_ref[:, here] = upper_grad
        part = dot(gate_grad, chunk_weights(shards, chunk, 0), 1, 0)
        part = part + dot(upper_grad, chunk_weights(shards, chunk, 1), 1, 0)
        total = part if total is None else total + part
    input_ref[...] = total.astype(low)


def token_rows(width):
    return pl.BlockSpec((TILE, width), lambda i: (i, 0))


def shard_spec(shard):
    return pl.BlockSpec(shard.shape, lambda i: (0, 0, 0, 0), pipeline_mode=pl.Buffered(1))


def expert_forward(x, route_columns, shards):
    rows = x.shape[0]
    hidden_width = sum(s.shape[0] * s.shape[2] for s in shards)
    chunks = hidden_width // CHUNK
    per_chunk = route_columns.shape[1] // chunks
    low = jnp.bfloat16
    wide = jax.ShapeDtypeStruct((rows, hidden_width), low)
    return pl.pallas_call(
        functools.partial(expert_forward_kernel, chunks, per_chunk),
        grid=(rows // TILE,),
        in_specs=[token_rows(D), token_rows(route_columns.shape[1])]
        + [shard_spec(s) for s in shards],
        out_specs=[token_rows(D)] + [token_rows(hidden_width)] * 3,
        out_shape=[jax.ShapeDtypeStruct((rows, D), low), wide, wide, wide],
        compiler_params=pltpu.CompilerParams(vmem_limit_bytes=58 * MIB),
        cost_estimate=pl.CostEstimate(
            flops=6 * rows * hidden_width * D,
            bytes_accessed=80_000_000,
            transcendentals=rows * hidden_width,
        ),
        name="expert_forward",
    )(x, route_columns, *shards)


def expert_backward(grad, slope, silu, shards):
    rows, hidden_width = slope.shape
    low = jnp.bfloat16
    wide = jax.ShapeDtypeStruct((rows, hidden_width), low)
    return pl.pallas_call(
        functools.partial(expert_backward_kernel, hidden_width // CHUNK),
        grid=(rows // TILE,),
        in_specs=[token_rows(D), token_rows(hidden_width), token_rows(hidden_width)]
        + [shard_spec(s) for s in shards],
        out_specs=[token_rows(D)] + [token_rows(hidden_width)] * 2,
        out_shape=[jax.ShapeDtypeStruct((rows, D), low), wide, wide],
        compiler_params=pltpu.CompilerParams(vmem_limit_bytes=58 * MIB),
        cost_estimate=pl.CostEstimate(
            flops=6 * rows * hidden_width * D, bytes_accessed=100_000_000, transcendentals=0
        ),
        name="expert_backward",
    )(grad, slope, silu, *shards)


def spread_tokens(own):
    parts = jnp.stack([own] + [swap_dp(own, mask) for mask in TOKEN_MASKS[1:]])
    return jnp.concatenate([parts, swap_core(parts)], axis=0).reshape(-1, own.shape[-1])


def collect_tokens(partial, own_rows):
    partial = partial.reshape(2, len(TOKEN_MASKS), own_rows, -1)
    mine = partial[0].astype(jnp.float32) + swap_core(partial[1]).astype(jnp.float32)
    total = mine[0]
    for place, mask in enumerate(TOKEN_MASKS[1:], 1):
        total = total + swap_dp(mine[place].astype(jnp.bfloat16), mask).astype(jnp.float32)
    return total


def extra_masks():
    count = lax.axis_size("dp")
    used = sum(WEIGHT_BITS) + TOKEN_MASKS[-1]
    masks = []
    mask = 1
    while mask < count:
        if not mask & used:
            masks.append(mask)
        mask *= 2
    return masks


def gather_weights(own):
    for mask in extra_masks():
        own = jnp.concatenate([own, swap_dp(own, mask)], axis=0)
    first, second = WEIGHT_BITS
    far = swap_dp(own, second)
    return [own, swap_dp(own, first), far, swap_dp(far, first)]


def unit_owners():
    masks = [0]
    for mask in extra_masks():
        masks = masks + [m ^ mask for m in masks]
    first, second = WEIGHT_BITS
    masks = [m ^ k for k in (0, first, second, first ^ second) for m in masks]
    return lax.axis_index("dp") ^ jnp.array(masks, jnp.int32)


def scatter_grads(parts):
    first, second = WEIGHT_BITS
    far = parts[2] + swap_dp(parts[3].astype(jnp.bfloat16), first).astype(jnp.float32)
    near = parts[0] + swap_dp(parts[1].astype(jnp.bfloat16), first).astype(jnp.float32)
    total = near + swap_dp(far.astype(jnp.bfloat16), second).astype(jnp.float32)
    for mask in reversed(extra_masks()):
        half = total.shape[0] // 2
        total = total[:half] + swap_dp(total[half:].astype(jnp.bfloat16), mask).astype(jnp.float32)
    return total


def on_device(
    activations,
    targets,
    lengths,
    token_mask,
    routes,
    route_weights,
    norm_gains,
    attention_master,
    expert_master,
    attention_left,
    attention_right,
    attention_left_root,
    attention_right_root,
    expert_left,
    expert_right,
    expert_left_root,
    expert_right_root,
):
    low = jnp.bfloat16
    own_rows = activations.shape[0]
    tensor_size = lax.axis_size("tensor")
    core = lax.axis_index("tensor")
    tokens_total = own_rows * tensor_size * lax.axis_size("dp")
    seq_length = lengths[0]
    position = core * own_rows + jnp.arange(own_rows, dtype=jnp.int32)
    valid_rows = ((token_mask == 1) & (position < seq_length)).astype(jnp.float32)
    valid_total = sum_everywhere(jnp.sum(valid_rows).reshape(1, 1))[0, 0]

    heads_here = HEADS // tensor_size
    kv_here = KV_HEADS // tensor_size
    query_cols = heads_here * HEAD_DIM
    key_cols = kv_here * HEAD_DIM
    qkv_cols = query_cols + 2 * key_cols
    rows_here = attention_master.shape[0]

    def by_head(values):
        rows = values.shape[0]
        query = values[:, :query_cols].reshape(rows, kv_here, LANES)
        key = values[:, query_cols : query_cols + key_cols].reshape(rows, kv_here, HEAD_DIM)
        value = values[:, query_cols + key_cols : qkv_cols].reshape(rows, kv_here, HEAD_DIM)
        return jnp.concatenate([query, key, value], axis=2).reshape(rows, qkv_cols)

    def from_heads(values):
        rows = values.shape[0]
        values = values.reshape(rows, kv_here, 256)
        return jnp.concatenate(
            [
                values[:, :, :LANES].reshape(rows, query_cols),
                values[:, :, LANES : LANES + HEAD_DIM].reshape(rows, key_cols),
                values[:, :, LANES + HEAD_DIM :].reshape(rows, key_cols),
            ],
            axis=1,
        )

    attention_low = attention_master.astype(low)
    w_qkv = lax.all_gather(by_head(attention_low), "dp", axis=0, tiled=True)
    w_output = lax.all_gather(attention_low[:, qkv_cols:], "dp", axis=0, tiled=True)
    hidden = activations.astype(jnp.float32)
    normed_own, attention_scaling = normalize(hidden, norm_gains[0])
    normed_own = normed_own.astype(low)
    normed = in_order(normed_own, swap_core(normed_own))

    shards = gather_weights(expert_master.astype(low))

    seq_rows = normed.shape[0]
    half_width = HEAD_DIM // 2
    frequency = theta_base ** (-jnp.arange(half_width, dtype=jnp.float32) * 2.0 / HEAD_DIM)
    angles = jnp.arange(seq_rows, dtype=jnp.float32)[:, None] * frequency[None, :]
    cosine = jnp.tile(jnp.cos(angles), (1, LANES // half_width))
    sine = jnp.tile(jnp.sin(angles), (1, LANES // half_width))
    q2, k2, v_high, attended, log_totals = attention_forward(
        lengths, normed, w_qkv, cosine, sine
    )
    branch = dot(attended, w_output, 1, 1)
    branch = own_half(branch) + swap_core(other_half(branch).astype(low)).astype(jnp.float32)
    middle = hidden + branch
    mix_own, mix_scaling = normalize(middle, norm_gains[1])
    mix = spread_tokens(mix_own.astype(low))

    routing = jnp.concatenate([routes.astype(jnp.float32), route_weights], axis=1)
    routing = jnp.stack([routing] + [swap_dp(routing, mask) for mask in TOKEN_MASKS[1:]])
    routing = routing.reshape(len(TOKEN_MASKS), 2, own_rows, 2 * TOPK)
    routing = jnp.concatenate(
        [
            lax.dynamic_index_in_dim(routing, core, 1, keepdims=False),
            lax.dynamic_index_in_dim(routing, 1 - core, 1, keepdims=False),
        ],
        axis=0,
    ).reshape(-1, 2 * TOPK)
    unit_here = expert_master.shape[0]
    slice_rows = expert_master.shape[2]
    unit_ids = (unit_owners()[:, None] * unit_here + jnp.arange(unit_here)[None, :]).reshape(-1)
    expert_of = unit_ids // GROUPS
    if unit_here % 4 == 0:
        expert_of = expert_of[::4]
    named = routing[:, None, :TOPK] == expert_of.astype(jnp.float32)[None, :, None]
    route_columns = jnp.sum(jnp.where(named, routing[:, None, TOPK:], 0.0), axis=2)

    mixed, slope, silu, inner = expert_forward(mix, route_columns, shards)
    output = middle + collect_tokens(mixed, own_rows)
    residual_error = output - targets
    loss_part = jnp.sum(valid_rows[:, None] * residual_error * residual_error)
    output_grad = 2.0 / valid_total * valid_rows[:, None] * residual_error
    output_low = spread_tokens(output_grad.astype(low))
    mix_part, gate_grad, upper_grad = expert_backward(output_low, slope, silu, shards)
    shard_units = shards[0].shape[0]

    def weight_grad(left, right):
        full = dot(left, right, 0, 0).reshape(4, shard_units, slice_rows, D)
        return scatter_grads([full[k] for k in range(4)])

    down_grad = weight_grad(inner, output_low)
    gate_weight_grad = weight_grad(gate_grad, mix)
    upper_weight_grad = weight_grad(upper_grad, mix)
    expert_grad = jnp.stack([gate_weight_grad, upper_weight_grad, down_grad], axis=1)

    mix_back, gain_mix = normalize_back(
        middle, mix_scaling, norm_gains[1], collect_tokens(mix_part, own_rows)
    )
    middle_grad = output_grad + mix_back
    branch_own = middle_grad.astype(low)
    branch_low = in_order(branch_own, swap_core(branch_own))
    dq, dkv = attention_backward(
        lengths, branch_low, w_output, q2, k2, v_high, log_totals, cosine, sine
    )
    qkv_grad = jnp.concatenate(
        [dq.reshape(seq_rows, kv_here, LANES), dkv.reshape(seq_rows, kv_here, LANES)], axis=2
    ).reshape(seq_rows, qkv_cols)
    normed_grad = dot(qkv_grad, w_qkv, 1, 1)
    normed_grad = own_half(normed_grad) + swap_core(
        other_half(normed_grad).astype(low)
    ).astype(jnp.float32)
    attention_back, gain_attention = normalize_back(
        hidden, attention_scaling, norm_gains[0], normed_grad
    )
    input_grad = middle_grad + attention_back
    qkv_part = dot(normed, qkv_grad, 0, 0).astype(low)
    output_part = dot(branch_low, attended, 0, 0).astype(low)
    qkv_part = lax.psum_scatter(qkv_part, "dp", scatter_dimension=0, tiled=True)
    output_part = lax.psum_scatter(output_part, "dp", scatter_dimension=0, tiled=True)
    attention_grad = jnp.concatenate([from_heads(qkv_part), output_part], axis=1).astype(
        jnp.float32
    )

    loss_row = jnp.full((1, D), loss_part)
    sums = sum_everywhere(jnp.concatenate([gain_attention[None], gain_mix[None], loss_row], axis=0))
    gain_grad = sums[:2]
    mean_loss = sums[2, 0] / valid_total
    gains_new = norm_gains - gain_rate * tokens_total**0.5 * gain_grad

    attention_blocks = attention_grad.reshape(rows_here, -1, BLOCK).transpose(1, 0, 2)
    attention_left_new = stat_decay * attention_left[0] + jnp.einsum(
        "bik,bjk->bij", attention_blocks, attention_blocks
    )
    attention_right_new = stat_decay * attention_right[0] + jnp.einsum(
        "bki,bkj->bij", attention_blocks, attention_blocks
    )
    attention_step = jnp.einsum("bij,bjk->bik", attention_left_root[0], attention_blocks)
    attention_step = jnp.einsum("bik,bkl->bil", attention_step, attention_right_root[0])
    attention_new = attention_master - D ** (-0.5) * attention_step.transpose(1, 0, 2).reshape(
        rows_here, -1
    )
    block_count = D // BLOCK
    expert_blocks = expert_grad.reshape(unit_here, 3, slice_rows, block_count, BLOCK).transpose(
        0, 1, 3, 2, 4
    )
    expert_left_new = stat_decay * expert_left + jnp.einsum(
        "...ik,...jk->...ij", expert_blocks, expert_blocks
    )
    expert_right_new = stat_decay * expert_right + jnp.einsum(
        "...ki,...kj->...ij", expert_blocks, expert_blocks
    )
    expert_step = jnp.einsum("...ij,...jk->...ik", expert_left_root, expert_blocks)
    expert_step = jnp.einsum("...ik,...kl->...il", expert_step, expert_right_root)
    expert_new = expert_master - D ** (-0.5) * expert_step.transpose(0, 1, 3, 2, 4).reshape(
        expert_master.shape
    )
    return (
        output,
        mean_loss,
        input_grad,
        gain_grad,
        gains_new,
        attention_grad,
        attention_left_new[None],
        attention_right_new[None],
        attention_new,
        expert_grad,
        expert_left_new,
        expert_right_new,
        expert_new,
    )


def solution(mesh):
    return jax.shard_map(
        on_device,
        mesh=mesh,
        in_specs=(
            P(("dp", "tensor"), None),
            P(("dp", "tensor"), None),
            P("dp"),
            P(("dp", "tensor")),
            P("dp", None),
            P("dp", None),
            P(),
            P("dp", "tensor"),
            P("dp", None, "tensor", None),
            P("dp", "tensor", None, None),
            P("dp", "tensor", None, None),
            P("dp", "tensor", None, None),
            P("dp", "tensor", None, None),
            P("dp", None, None, "tensor", None),
            P("dp", None, "tensor", None, None),
            P("dp", None, None, "tensor", None),
            P("dp", None, "tensor", None, None),
        ),
        out_specs=(
            P(("dp", "tensor"), None),
            P(),
            P(("dp", "tensor"), None),
            P(),
            P(),
            P("dp", "tensor"),
            P("dp", "tensor", None, None),
            P("dp", "tensor", None, None),
            P("dp", "tensor"),
            P("dp", None, "tensor", None),
            P("dp", None, None, "tensor", None),
            P("dp", None, "tensor", None, None),
            P("dp", None, "tensor", None),
        ),
        check_vma=False,
    )
```

time: 4040 us -> 1240 us (0.31)
  waiting for transfers between devices: 1730 us -> 586 us
  other arithmetic: 1100 us -> 85.3 us
  matrix products: 575 us -> 137 us
  local copies, waits for them, and re-layouts: 511 us -> 105 us
  Pallas kernels: 0 us -> 216 us
  blocking collectives: 82.7 us -> 0 us
  starting transfers between devices: 0.9 us -> 81.2 us
    unnamed x14 -> x4, waiting for transfers between devices: 1280 us -> 0.07 us
    scatter-add x2 -> x0, other arithmetic: 822 us -> none  [the longest x1 411 us: on_device(): input_slots.at[owner_ids]]
    dot_general x34 -> x13, matrix products: 575 us -> 137 us  [the longest x7 87.4 us: dot(): lax.dot_general(left, right, (((left_dim,), (right_dim,)), ((), ())), pre...]
    ppermute x0 -> x45, waiting for transfers between devices: none -> 434 us  [the longest x35 419 us: swap_dp(): return lax.ppermute(values, 'dp', [(i, i ^ mask) for i in range(count)])]
    all_gather x6 -> x2, waiting for transfers between devices: 424 us -> 77.3 us  [the longest x1 46.7 us: on_device(): w_qkv = lax.all_gather(by_head(attention_low), 'dp', axis=0, tiled=True)]
    gather x6 -> x0, local copies, waits for them, and re-layouts: 331 us -> none  [the longest x1 62.4 us: on_device(): jnp.take(output_low, source_row, axis=0)]
    pallas_call x0 -> x4, Pallas kernels: none -> 216 us  [the longest x1 91.7 us: expert_backward(): pl.pallas_call(functools.partial(expert_backward_kernel, hidden_width //...]
    psum x2 -> x0, blocking collectives: 82.7 us -> none  [the longest x1 43.9 us: on_device(): lax.psum((loss_part, jnp.stack([gain_attention, gain_mix])), ('dp', 'tens...]
  transfers between devices with their start and end apart: 12 -> 49, of which waited for: 7 -> 25; matrix products, arithmetic and copies ran while one was open for 11% -> 18% of each run, Pallas kernels for 0% -> 2%
where the time goes in v1:
time: 1240 us; the launch traced here: 1230 us
  waiting for transfers between devices  586 us (47%)
  Pallas kernels  216 us (17%)
  matrix products  137 us (11%)
  local copies, waits for them, and re-layouts  105 us (8%)
  other arithmetic  85.3 us (7%)
  starting transfers between devices  81.2 us (7%)
  between operations  21.3 us (2%)
    ppermute x35, waiting for transfers between devices, swap_dp(): return lax.ppermute(values, 'dp', [(i, i ^ mask) for i in range(count)])  419 us
    pallas_call x1, Pallas kernels, expert_backward(): pl.pallas_call(functools.partial(expert_backward_kernel, hidden_width //...  91.7 us
    dot_general x7, matrix products, dot(): lax.dot_general(left, right, (((left_dim,), (right_dim,)), ((), ())), pre...  87.4 us
    ppermute x35, starting transfers between devices, swap_dp(): return lax.ppermute(values, 'dp', [(i, i ^ mask) for i in range(count)])  79.8 us
    reduce_scatter x1, waiting for transfers between devices, on_device(): lax.psum_scatter(output_part, 'dp', scatter_dimension=0, tiled=True)  75.2 us
    pallas_call x1, Pallas kernels, expert_forward(): pl.pallas_call(functools.partial(expert_forward_kernel, chunks, per_chunk...  74.7 us
    all_gather x1, waiting for transfers between devices, on_device(): w_qkv = lax.all_gather(by_head(attention_low), 'dp', axis=0, tiled=True)  46.7 us
    unnamed x147, local copies, waits for them, and re-layouts  30.6 us
  transfers between devices with their start and end apart: 49, of which 25 were waited for; matrix products, arithmetic and copies ran while one was open for 18% of the time, Pallas kernels for 2%

profile of v1, /device:TPU:0, one launch (start us, length us, event | category | flops | bytes accessed | tf_op | source)
XLA Modules:
  0.0 1231.7 jit_solution(1493890583597406961)
XLA Ops:
  28.1 46.7 %all-gather.3.cloned.1.call-done.w_ref = bf16[1024,1024]{1,0:T(8,128)(2,1)} async-done(((bf16[64,1024]{1,0:T(8,128)(2,1)}), bf16[1024,1024]{1,0:T(8,128)(2,1)}) %all-gather.3.cloned.1.call-update) | async-done | bytes 2097168 | tf_op jit(solution)/shard_map/all_gather | solution.py:507
  76.9 22.7 %attention_forward.1 = (bf16[1024,1024]{1,0:T(8,128)(2,1)}, bf16[1024,512]{1,0:T(8,128)(2,1)S(1)}, bf16[1024,512]{1,0:T(8,128)(2,1)S(1)}, bf16[1024,512]{1,0:T(8,128)(2,1)}, f32[64,1024]{1,0:T(8,128)S(1)}) custom-call(s32[1]{0:T(128)} %copy.96.length_ref, bf16[1024,1024]{1,0:T(8,128)(2,1)} %pad_maximum_fusion.3.x_ref, ...), custom_call_target="tpu_custom_call" | custom-call | flops 8000000000 | bytes 12000000 | tf_op jit(solution)/shard_map/attention_forward/pallas_call | solution.py:215
  101.6 30.5 %all-gather.5.cloned.1.call-done.wo_ref = bf16[1024,512]{1,0:T(8,128)(2,1)} async-done(((bf16[64,512]{1,0:T(8,128)(2,1)}), bf16[1024,512]{1,0:T(8,128)(2,1)}) %all-gather.5.cloned.1.call-update) | async-done | bytes 1048592 | tf_op jit(solution)/shard_map/all_gather | solution.py:508
  149.3 23.5 %collective-permute-done.4 = bf16[512,1024]{1,0:T(8,128)(2,1)S(1)} collective-permute-done((bf16[512,1024]{1,0:T(8,128)(2,1)S(1)}, bf16[512,1024]{1,0:T(8,128)(2,1)S(1)}, u32[]{:S(2)}, u32[]{:S(2)}) %collective-permute-start.4) | collective-permute-done | bytes 1048608 | tf_op jit(solution)/shard_map/ppermute | solution.py:52
  172.7 21.6 %collective-permute-done.3 = bf16[512,1024]{1,0:T(8,128)(2,1)S(1)} collective-permute-done((bf16[512,1024]{1,0:T(8,128)(2,1)S(1)}, bf16[512,1024]{1,0:T(8,128)(2,1)S(1)}, u32[]{:S(2)}, u32[]{:S(2)}) %collective-permute-start.3) | collective-permute-done | bytes 1048608 | tf_op jit(solution)/shard_map/ppermute | solution.py:52
  202.3 77.4 %collective-permute-done.10.s2 = bf16[8,3,64,1024]{3,2,1,0:T(8,128)(2,1)} collective-permute-done((bf16[8,3,64,1024]{3,2,1,0:T(8,128)(2,1)}, bf16[8,3,64,1024]{3,2,1,0:T(8,128)(2,1)}, u32[]{:S(2)}, u32[]{:S(2)}) %collective-permute-start.10) | collective-permute-done | bytes 3145760 | tf_op jit(solution)/shard_map/ppermute | solution.py:52
  297.7 4.6 constant_dynamic-update-slice_fusion
  302.3 36.4 %collective-permute-done.9.s1 = bf16[8,3,64,1024]{3,2,1,0:T(8,128)(2,1)} collective-permute-done((bf16[8,3,64,1024]{3,2,1,0:T(8,128)(2,1)}, bf16[8,3,64,1024]{3,2,1,0:T(8,128)(2,1)}, u32[]{:S(2)}, u32[]{:S(2)}) %collective-permute-start.9) | collective-permute-done | bytes 3145760 | tf_op jit(solution)/shard_map/ppermute | solution.py:52
  338.7 66.5 %collective-permute-done.11.s3 = bf16[8,3,64,1024]{3,2,1,0:T(8,128)(2,1)} collective-permute-done((bf16[8,3,64,1024]{3,2,1,0:T(8,128)(2,1)}, bf16[8,3,64,1024]{3,2,1,0:T(8,128)(2,1)}, u32[]{:S(2)}, u32[]{:S(2)}) %collective-permute-start.11) | collective-permute-done | bytes 3145760 | tf_op jit(solution)/shard_map/ppermute | solution.py:52
  405.2 74.7 %expert_forward.1 = (bf16[4096,1024]{1,0:T(8,128)(2,1)}, bf16[4096,2048]{1,0:T(8,128)(2,1)}, bf16[4096,2048]{1,0:T(8,128)(2,1)}, bf16[4096,2048]{1,0:T(8,128)(2,1)}) custom-call(bf16[4096,1024]{1,0:T(8,128)(2,1)} %bitcast.220, f32[4096,8]{1,0:T(8,128)} %copy.50.route_ref, bf16[8,3,64,1024]{3,2,1,0:T(8,128)(2,1)} %convert_element_type.179.s0, ...), custom_call_target="tpu_custom_call" | custom-call | flops 51539607552 | bytes 80000000 | tf_op jit(solution)/shard_map/expert_forward/pallas_call | solution.py:361
  483.9 7.1 collective-permute-done.12
  493.1 7.8 convert_add_fusion.1
  508.0 39.1 %collective-permute-start.17 = (f32[1,1]{1,0:T(1,128)}, f32[1,1]{1,0:T(1,128)}, u32[]{:S(2)}, u32[]{:S(2)}) collective-permute-start(f32[1,1]{1,0:T(1,128)} %add.196), channel_id=1, source_target_pairs={{0,2},{2,0},{4,6},{6,4},{8,10},{10,8},{12,14},{14,12},{16,18},{18,... | collective-permute-start | bytes 20 | tf_op jit(solution)/shard_map/ppermute | solution.py:52
  571.9 23.5 %collective-permute-done.23 = bf16[512,1024]{1,0:T(8,128)(2,1)S(1)} collective-permute-done((bf16[512,1024]{1,0:T(8,128)(2,1)S(1)}, bf16[512,1024]{1,0:T(8,128)(2,1)S(1)}, u32[]{:S(2)}, u32[]{:S(2)}) %collective-permute-start.23) | collective-permute-done | bytes 1048608 | tf_op jit(solution)/shard_map/ppermute | solution.py:52
  595.4 16.7 %collective-permute-done.22 = bf16[512,1024]{1,0:T(8,128)(2,1)S(1)} collective-permute-done((bf16[512,1024]{1,0:T(8,128)(2,1)S(1)}, bf16[512,1024]{1,0:T(8,128)(2,1)S(1)}, u32[]{:S(2)}, u32[]{:S(2)}) %collective-permute-start.22) | collective-permute-done | bytes 1048608 | tf_op jit(solution)/shard_map/ppermute | solution.py:52
  614.3 5.7 collective-permute-done.24
  620.5 24.9 %fusion.76 = (bf16[2048,1024]{1,0:T(8,128)(2,1)S(1)}, f32[2048,1024]{1,0:T(8,128)}) fusion(bf16[4096,2048]{1,0:T(8,128)(2,1)} %get-tuple-element.40, bf16[4096,1024]{1,0:T(8,128)(2,1)S(1)} %bitcast.223), kind=kOutput, calls=%fused_computation.151 | convolution fusion | flops 17181966336 | bytes 37748736 | tf_op jit(solution)/shard_map/dot_general | solution.py:33
  646.8 91.7 %expert_backward.1 = (bf16[4096,1024]{1,0:T(8,128)(2,1)}, bf16[4096,2048]{1,0:T(8,128)(2,1)}, bf16[4096,2048]{1,0:T(8,128)(2,1)}) custom-call(bf16[4096,1024]{1,0:T(8,128)(2,1)} %bitcast.224, bf16[4096,2048]{1,0:T(8,128)(2,1)} %get-tuple-element.29.slope_ref, bf16[4096,2048]{1,0:T(8,128)(2,1)} %get-tuple-element.30.silu_ref, ...), custom_call_target="tpu_custom_call" | custom-call | flops 51539607552 | bytes 100000000 | tf_op jit(solution)/shard_map/expert_backward/pallas_call | solution.py:382
  742.8 24.4 %fusion.78 = (bf16[2048,1024]{1,0:T(8,128)(2,1)S(1)}, f32[2048,1024]{1,0:T(8,128)}) fusion(bf16[4096,2048]{1,0:T(8,128)(2,1)} %get-tuple-element.38, bf16[4096,1024]{1,0:T(8,128)(2,1)} %bitcast.221), kind=kOutput, calls=%fused_computation.153 | convolution fusion | flops 17181966336 | bytes 37748736 | tf_op jit(solution)/shard_map/dot_general | solution.py:33
  770.6 24.5 %fusion.77 = (bf16[2048,1024]{1,0:T(8,128)(2,1)}, f32[2048,1024]{1,0:T(8,128)}) fusion(bf16[4096,2048]{1,0:T(8,128)(2,1)} %get-tuple-element.39, bf16[4096,1024]{1,0:T(8,128)(2,1)} %bitcast.222), kind=kOutput, calls=%fused_computation.152 | convolution fusion | flops 17181966336 | bytes 37748736 | tf_op jit(solution)/shard_map/dot_general | solution.py:33
  807.7 7.8 convert_add_fusion
  832.8 9.1 collective-permute-done.26
  843.7 20.2 %collective-permute-done.28 = bf16[512,1024]{1,0:T(8,128)(2,1)S(1)} collective-permute-done((bf16[512,1024]{1,0:T(8,128)(2,1)S(1)}, bf16[512,1024]{1,0:T(8,128)(2,1)S(1)}, u32[]{:S(2)}, u32[]{:S(2)}) %collective-permute-start.28) | collective-permute-done | bytes 1048608 | tf_op jit(solution)/shard_map/ppermute | solution.py:52
  874.2 44.0 %collective-permute-done.44 = bf16[8,64,1024]{2,1,0:T(8,128)(2,1)S(1)} collective-permute-done((bf16[8,64,1024]{2,1,0:T(8,128)(2,1)S(1)}, bf16[8,64,1024]{2,1,0:T(8,128)(2,1)S(1)}, u32[]{:S(2)}, u32[]{:S(2)}) %collective-permute-start.44) | collective-permute-done | bytes 1048608 | tf_op jit(solution)/shard_map/ppermute | solution.py:52
  925.3 55.6 %collective-permute-done.38 = bf16[8,64,1024]{2,1,0:T(8,128)(2,1)} collective-permute-done((bf16[8,64,1024]{2,1,0:T(8,128)(2,1)}, bf16[8,64,1024]{2,1,0:T(8,128)(2,1)}, u32[]{:S(2)}, u32[]{:S(2)}) %collective-permute-start.38) | collective-permute-done | bytes 1048608 | tf_op jit(solution)/shard_map/ppermute | solution.py:52
  989.3 12.3 %collective-permute-done.41 = bf16[8,64,1024]{2,1,0:T(8,128)(2,1)} collective-permute-done((bf16[8,64,1024]{2,1,0:T(8,128)(2,1)}, bf16[8,64,1024]{2,1,0:T(8,128)(2,1)}, u32[]{:S(2)}, u32[]{:S(2)}) %collective-permute-start.41) | collective-permute-done | bytes 1048608 | tf_op jit(solution)/shard_map/ppermute | solution.py:52
  1013.7 26.6 %attention_backward.1 = (bf16[1024,512]{1,0:T(8,128)(2,1)S(1)}, bf16[1024,512]{1,0:T(8,128)(2,1)S(1)}) custom-call(s32[1]{0:T(128)} %copy.96.length_ref, bf16[1024,1024]{1,0:T(8,128)(2,1)} %pad_maximum_fusion.4.branch_ref, bf16[1024,512]{1,0:T(8,128)(2,1)} %all-gather.5.cloned.1.call-done.wo_ref, bf16[1024,1024]{1,0:T(8,128)(2,1)} %get-tuple-element.32.q_ref, ...), custom_call_target="tpu_custom_call" | custom-call | flops 20000000000 | bytes 12000000 | tf_op jit(solution)/shard_map/attention_backward/pallas_call | solution.py:251
  1054.9 19.7 %multiply_add_fusion = f32[8,3,4,256,256]{4,3,2,1,0:T(8,128)} fusion(f32[8,3,4,256,256]{4,3,2,1,0:T(8,128)} %param.32, bf16[8,1,64,4,256]{4,2,3,1,0:T(8,128)(2,1)} %copy.57, bf16[8,1,64,4,256]{4,2,3,1,0:T(8,128)(2,1)} %copy.56, bf16[8,1,64,4,256]{4,2,3,1,0:T(8,128)(2,1)} %copy.55), kind=kOutput, calls=%fused_computation | convolution fusion | flops 821035008 | bytes 53477376 | tf_op jit(solution)/shard_map/...ki,...kj->...ij/dot_general | solution.py:621
  1074.6 4.6 fusion.83
  1082.3 15.1 %multiply_bitcast_fusion = f32[8,3,4,8,8,256]{5,4,3,2,1,0:T(8,128)} fusion(f32[8,3,4,256,256]{4,3,2,1,0:T(8,128)} %param.34, f32[8,3,4,64,64]{4,3,2,1,0:T(8,128)S(1)} %copy-done, bf16[8,1,64,4,256]{4,2,3,1,0:T(8,128)(2,1)} %copy.57, bf16[8,1,64,4,256]{4,2,3,1,0:T(8,128)(2,1)} %copy.56, bf16[8,1,64,4,256]{4,2,3,1,0:T(8,128)(2,1)} %copy.55), kind=kOutput, calls=%fused_computation.5 | convolution fusion | flops 1011351552 | bytes 36175872 | tf_op jit(solution)/shard_map/...ik,...kl->...il/dot_general | solution.py:625
  1105.0 7.4 multiply_add_fusion.1
  1136.7 75.2 %reduce-scatter.5.cloned.1.call-done = bf16[64,512]{1,0:T(8,128)(2,1)} async-done(((bf16[1024,512]{1,0:T(8,128)(2,1)}), bf16[64,512]{1,0:T(8,128)(2,1)}) %reduce-scatter.5.cloned.1.call-update) | async-done | bytes 65552 | tf_op jit(solution)/shard_map/reduce_scatter | solution.py:591
  (345 shorter events, 242.8 us)
Async XLA Ops:
  7.2 67.6 %all-gather.3.cloned.1.call-start = ((), (), s32[]{:S(2)}) async-start(), calls=%async_computation.2 | async-start | bytes 2228224 | tf_op jit(solution)/shard_map/all_gather | solution.py:507
  10.1 122.0 %all-gather.5.cloned.1.call-start = ((), (), s32[]{:S(2)}) async-start(), calls=%async_computation.3 | async-start | bytes 1114112 | tf_op jit(solution)/shard_map/all_gather | solution.py:508
  16.1 1119.2 %reduce-scatter.3.cloned.1.call-start = ((), (), s32[]{:S(2)}) async-start(), calls=%async_computation.4 | async-start | bytes 2228224 | tf_op jit(solution)/shard_map/reduce_scatter | solution.py:590
  140.4 139.2 %collective-permute-start.10 = (bf16[8,3,64,1024]{3,2,1,0:T(8,128)(2,1)}, bf16[8,3,64,1024]{3,2,1,0:T(8,128)(2,1)}, u32[]{:S(2)}, u32[]{:S(2)}) collective-permute-start(bf16[8,3,64,1024]{3,2,1,0:T(8,128)(2,1)} %convert_element_type.179.s0), channel_id=1, source_target_pairs={{0,16},{2,18},{4,20},{6,22},{8,24},{10,26},{12,28},{14,30},{16,0},... | collective-permute-start | bytes 9437192 | tf_op jit(solution)/shard_map/ppermute | solution.py:52
  147.5 46.8 %collective-permute-start.3 = (bf16[512,1024]{1,0:T(8,128)(2,1)S(1)}, bf16[512,1024]{1,0:T(8,128)(2,1)S(1)}, u32[]{:S(2)}, u32[]{:S(2)}) collective-permute-start(bf16[512,1024]{1,0:T(8,128)(2,1)S(1)} %get-tuple-element.57), channel_id=1, source_target_pairs={{0,4},{2,6},{4,0},{6,2},{8,12},{10,14},{12,8},{14,10},{16,20},{18,... | collective-permute-start | bytes 3145736 | tf_op jit(solution)/shard_map/ppermute | solution.py:52
  148.7 45.7 %collective-permute-start.2 = (bf16[512,1024]{1,0:T(8,128)(2,1)S(1)}, bf16[512,1024]{1,0:T(8,128)(2,1)S(1)}, u32[]{:S(2)}, u32[]{:S(2)}) collective-permute-start(bf16[512,1024]{1,0:T(8,128)(2,1)S(1)} %get-tuple-element.57), channel_id=1, source_target_pairs={{0,2},{2,0},{4,6},{6,4},{8,10},{10,8},{12,14},{14,12},{16,18},{18,... | collective-permute-start | bytes 3145736 | tf_op jit(solution)/shard_map/ppermute | solution.py:52
  197.0 100.7 %collective-permute-start.5 = (bf16[4,512,1024]{2,1,0:T(8,128)(2,1)}, bf16[4,512,1024]{2,1,0:T(8,128)(2,1)}, u32[]{:S(2)}, u32[]{:S(2)}) collective-permute-start(bf16[4,512,1024]{2,1,0:T(8,128)(2,1)} %pad_maximum_fusion.1), channel_id=1, source_target_pairs={{0,1},{1,0},{2,3},{3,2},{4,5},{5,4},{6,7},{7,6},{8,9},{9,8},{10,11... | collective-permute-start | bytes 12582920 | tf_op jit(solution)/shard_map/ppermute | solution.py:57
  197.1 82.7 %collective-permute-start.8 = (f32[1024,16]{0,1:T(8,128)S(1)}, f32[1024,16]{0,1:T(8,128)}, u32[]{:S(2)}, u32[]{:S(2)}) collective-permute-start(f32[1024,16]{0,1:T(8,128)S(1)} %pad_maximum_fusion.8), channel_id=1, source_target_pairs={{0,6},{2,4},{4,2},{6,0},{8,14},{10,12},{12,10},{14,8},{16,22},{18,... | collective-permute-start | bytes 196616 | tf_op jit(solution)/shard_map/ppermute | solution.py:52
  198.9 84.0 %collective-permute-start.7 = (f32[1024,16]{0,1:T(8,128)S(1)}, f32[1024,16]{0,1:T(8,128)}, u32[]{:S(2)}, u32[]{:S(2)}) collective-permute-start(f32[1024,16]{0,1:T(8,128)S(1)} %pad_maximum_fusion.8), channel_id=1, source_target_pairs={{0,4},{2,6},{4,0},{6,2},{8,12},{10,14},{12,8},{14,10},{16,20},{18,... | collective-permute-start | bytes 196616 | tf_op jit(solution)/shard_map/ppermute | solution.py:52
  200.1 138.6 %collective-permute-start.9 = (bf16[8,3,64,1024]{3,2,1,0:T(8,128)(2,1)}, bf16[8,3,64,1024]{3,2,1,0:T(8,128)(2,1)}, u32[]{:S(2)}, u32[]{:S(2)}) collective-permute-start(bf16[8,3,64,1024]{3,2,1,0:T(8,128)(2,1)} %convert_element_type.179.s0), channel_id=1, source_target_pairs={{0,8},{2,10},{4,12},{6,14},{8,0},{10,2},{12,4},{14,6},{16,24},{18,... | collective-permute-start | bytes 9437192 | tf_op jit(solution)/shard_map/ppermute | solution.py:52
  279.6 125.6 %collective-permute-start.11 = (bf16[8,3,64,1024]{3,2,1,0:T(8,128)(2,1)}, bf16[8,3,64,1024]{3,2,1,0:T(8,128)(2,1)}, u32[]{:S(2)}, u32[]{:S(2)}) collective-permute-start(bf16[8,3,64,1024]{3,2,1,0:T(8,128)(2,1)} %collective-permute-done.10.s2), channel_id=1, source_target_pairs={{0,8},{2,10},{4,12},{6,14},{8,0},{10,2},{12,4},{14,6},{16,24},{18,... | collective-permute-start | bytes 9437192 | tf_op jit(solution)/shard_map/ppermute | solution.py:52
  501.2 62.5 %collective-permute-start.13 = (bf16[512,1024]{1,0:T(8,128)(2,1)S(1)}, bf16[512,1024]{1,0:T(8,128)(2,1)S(1)}, u32[]{:S(2)}, u32[]{:S(2)}) collective-permute-start(bf16[512,1024]{1,0:T(8,128)(2,1)S(1)} %get-tuple-element.83), channel_id=1, source_target_pairs={{0,2},{2,0},{4,6},{6,4},{8,10},{10,8},{12,14},{14,12},{16,18},{18,... | collective-permute-start | bytes 3145736 | tf_op jit(solution)/shard_map/ppermute | solution.py:52
  501.9 61.8 %collective-permute-start.15 = (bf16[512,1024]{1,0:T(8,128)(2,1)S(1)}, bf16[512,1024]{1,0:T(8,128)(2,1)S(1)}, u32[]{:S(2)}, u32[]{:S(2)}) collective-permute-start(bf16[512,1024]{1,0:T(8,128)(2,1)S(1)} %get-tuple-element.84), channel_id=1, source_target_pairs={{0,6},{2,4},{4,2},{6,0},{8,14},{10,12},{12,10},{14,8},{16,22},{18,... | collective-permute-start | bytes 3145736 | tf_op jit(solution)/shard_map/ppermute | solution.py:52
  503.4 60.4 %collective-permute-start.14 = (bf16[512,1024]{1,0:T(8,128)(2,1)S(1)}, bf16[512,1024]{1,0:T(8,128)(2,1)S(1)}, u32[]{:S(2)}, u32[]{:S(2)}) collective-permute-start(bf16[512,1024]{1,0:T(8,128)(2,1)S(1)} %get-tuple-element.85), channel_id=1, source_target_pairs={{0,4},{2,6},{4,0},{6,2},{8,12},{10,14},{12,8},{14,10},{16,20},{18,... | collective-permute-start | bytes 3145736 | tf_op jit(solution)/shard_map/ppermute | solution.py:52
  508.0 41.0 %collective-permute-start.17 = (f32[1,1]{1,0:T(1,128)}, f32[1,1]{1,0:T(1,128)}, u32[]{:S(2)}, u32[]{:S(2)}) collective-permute-start(f32[1,1]{1,0:T(1,128)} %add.196), channel_id=1, source_target_pairs={{0,2},{2,0},{4,6},{6,4},{8,10},{10,8},{12,14},{14,12},{16,18},{18,... | collective-permute-start | bytes 20 | tf_op jit(solution)/shard_map/ppermute | solution.py:52
  568.4 27.0 %collective-permute-start.23 = (bf16[512,1024]{1,0:T(8,128)(2,1)S(1)}, bf16[512,1024]{1,0:T(8,128)(2,1)S(1)}, u32[]{:S(2)}, u32[]{:S(2)}) collective-permute-start(bf16[512,1024]{1,0:T(8,128)(2,1)S(1)} %get-tuple-element.55), channel_id=1, source_target_pairs={{0,6},{2,4},{4,2},{6,0},{8,14},{10,12},{12,10},{14,8},{16,22},{18,... | collective-permute-start | bytes 3145736 | tf_op jit(solution)/shard_map/ppermute | solution.py:52
  569.8 42.4 %collective-permute-start.22 = (bf16[512,1024]{1,0:T(8,128)(2,1)S(1)}, bf16[512,1024]{1,0:T(8,128)(2,1)S(1)}, u32[]{:S(2)}, u32[]{:S(2)}) collective-permute-start(bf16[512,1024]{1,0:T(8,128)(2,1)S(1)} %get-tuple-element.55), channel_id=1, source_target_pairs={{0,4},{2,6},{4,0},{6,2},{8,12},{10,14},{12,8},{14,10},{16,20},{18,... | collective-permute-start | bytes 3145736 | tf_op jit(solution)/shard_map/ppermute | solution.py:52
  570.5 41.6 %collective-permute-start.21 = (bf16[512,1024]{1,0:T(8,128)(2,1)S(1)}, bf16[512,1024]{1,0:T(8,128)(2,1)S(1)}, u32[]{:S(2)}, u32[]{:S(2)}) collective-permute-start(bf16[512,1024]{1,0:T(8,128)(2,1)S(1)} %get-tuple-element.55), channel_id=1, source_target_pairs={{0,2},{2,0},{4,6},{6,4},{8,10},{10,8},{12,14},{14,12},{16,18},{18,... | collective-permute-start | bytes 3145736 | tf_op jit(solution)/shard_map/ppermute | solution.py:52
  742.4 75.6 %collective-permute-start.43 = (bf16[8,64,1024]{2,1,0:T(8,128)(2,1)}, bf16[8,64,1024]{2,1,0:T(8,128)(2,1)}, u32[]{:S(2)}, u32[]{:S(2)}) collective-permute-start(bf16[8,64,1024]{2,1,0:T(8,128)(2,1)} %bitcast.55), channel_id=1, source_target_pairs={{0,8},{2,10},{4,12},{6,14},{8,0},{10,2},{12,4},{14,6},{16,24},{18,... | collective-permute-start | bytes 3145736 | tf_op jit(solution)/shard_map/ppermute | solution.py:52
  742.8 62.9 %collective-permute-start.25 = (bf16[4,512,1024]{2,1,0:T(8,128)(2,1)S(1)}, bf16[4,512,1024]{2,1,0:T(8,128)(2,1)S(1)}, u32[]{:S(2)}, u32[]{:S(2)}) collective-permute-start(bf16[4,512,1024]{2,1,0:T(8,128)(2,1)S(1)} %bitcast.194), channel_id=1, source_target_pairs={{0,1},{1,0},{2,3},{3,2},{4,5},{5,4},{6,7},{7,6},{8,9},{9,8},{10,11... | collective-permute-start | bytes 12582920 | tf_op jit(solution)/shard_map/ppermute | solution.py:57
  768.8 56.5 %collective-permute-start.37 = (bf16[8,64,1024]{2,1,0:T(8,128)(2,1)}, bf16[8,64,1024]{2,1,0:T(8,128)(2,1)}, u32[]{:S(2)}, u32[]{:S(2)}) collective-permute-start(bf16[8,64,1024]{2,1,0:T(8,128)(2,1)} %bitcast.45), channel_id=1, source_target_pairs={{0,8},{2,10},{4,12},{6,14},{8,0},{10,2},{12,4},{14,6},{16,24},{18,... | collective-permute-start | bytes 3145736 | tf_op jit(solution)/shard_map/ppermute | solution.py:52
  798.1 31.6 %collective-permute-start.40 = (bf16[8,64,1024]{2,1,0:T(8,128)(2,1)}, bf16[8,64,1024]{2,1,0:T(8,128)(2,1)}, u32[]{:S(2)}, u32[]{:S(2)}) collective-permute-start(bf16[8,64,1024]{2,1,0:T(8,128)(2,1)} %bitcast.50), channel_id=1, source_target_pairs={{0,8},{2,10},{4,12},{6,14},{8,0},{10,2},{12,4},{14,6},{16,24},{18,... | collective-permute-start | bytes 3145736 | tf_op jit(solution)/shard_map/ppermute | solution.py:52
  816.6 47.3 %collective-permute-start.28 = (bf16[512,1024]{1,0:T(8,128)(2,1)S(1)}, bf16[512,1024]{1,0:T(8,128)(2,1)S(1)}, u32[]{:S(2)}, u32[]{:S(2)}) collective-permute-start(bf16[512,1024]{1,0:T(8,128)(2,1)S(1)} %get-tuple-element.81), channel_id=1, source_target_pairs={{0,6},{2,4},{4,2},{6,0},{8,14},{10,12},{12,10},{14,8},{16,22},{18,... | collective-permute-start | bytes 3145736 | tf_op jit(solution)/shard_map/ppermute | solution.py:52
  818.0 47.9 %collective-permute-start.27 = (bf16[512,1024]{1,0:T(8,128)(2,1)S(1)}, bf16[512,1024]{1,0:T(8,128)(2,1)S(1)}, u32[]{:S(2)}, u32[]{:S(2)}) collective-permute-start(bf16[512,1024]{1,0:T(8,128)(2,1)S(1)} %get-tuple-element.82), channel_id=1, source_target_pairs={{0,4},{2,6},{4,0},{6,2},{8,12},{10,14},{12,8},{14,10},{16,20},{18,... | collective-permute-start | bytes 3145736 | tf_op jit(solution)/shard_map/ppermute | solution.py:52
  825.3 44.8 %collective-permute-start.42 = (bf16[8,64,1024]{2,1,0:T(8,128)(2,1)S(1)}, bf16[8,64,1024]{2,1,0:T(8,128)(2,1)S(1)}, u32[]{:S(2)}, u32[]{:S(2)}) collective-permute-start(bf16[8,64,1024]{2,1,0:T(8,128)(2,1)S(1)} %bitcast.216), channel_id=1, source_target_pairs={{0,8},{2,10},{4,12},{6,14},{8,0},{10,2},{12,4},{14,6},{16,24},{18,... | collective-permute-start | bytes 3145736 | tf_op jit(solution)/shard_map/ppermute | solution.py:52
  829.7 95.6 %collective-permute-start.36 = (bf16[8,64,1024]{2,1,0:T(8,128)(2,1)}, bf16[8,64,1024]{2,1,0:T(8,128)(2,1)}, u32[]{:S(2)}, u32[]{:S(2)}) collective-permute-start(bf16[8,64,1024]{2,1,0:T(8,128)(2,1)} %bitcast.43), channel_id=1, source_target_pairs={{0,8},{2,10},{4,12},{6,14},{8,0},{10,2},{12,4},{14,6},{16,24},{18,... | collective-permute-start | bytes 3145736 | tf_op jit(solution)/shard_map/ppermute | solution.py:52
  841.9 147.4 %collective-permute-start.39 = (bf16[8,64,1024]{2,1,0:T(8,128)(2,1)}, bf16[8,64,1024]{2,1,0:T(8,128)(2,1)}, u32[]{:S(2)}, u32[]{:S(2)}) collective-permute-start(bf16[8,64,1024]{2,1,0:T(8,128)(2,1)} %bitcast.48), channel_id=1, source_target_pairs={{0,8},{2,10},{4,12},{6,14},{8,0},{10,2},{12,4},{14,6},{16,24},{18,... | collective-permute-start | bytes 3145736 | tf_op jit(solution)/shard_map/ppermute | solution.py:52
  863.9 54.3 %collective-permute-start.44 = (bf16[8,64,1024]{2,1,0:T(8,128)(2,1)S(1)}, bf16[8,64,1024]{2,1,0:T(8,128)(2,1)S(1)}, u32[]{:S(2)}, u32[]{:S(2)}) collective-permute-start(bf16[8,64,1024]{2,1,0:T(8,128)(2,1)S(1)} %add_convert_fusion), channel_id=1, source_target_pairs={{0,16},{2,18},{4,20},{6,22},{8,24},{10,26},{12,28},{14,30},{16,0},... | collective-permute-start | bytes 3145736 | tf_op jit(solution)/shard_map/ppermute | solution.py:52
  865.9 114.9 %collective-permute-start.38 = (bf16[8,64,1024]{2,1,0:T(8,128)(2,1)}, bf16[8,64,1024]{2,1,0:T(8,128)(2,1)}, u32[]{:S(2)}, u32[]{:S(2)}) collective-permute-start(bf16[8,64,1024]{2,1,0:T(8,128)(2,1)} %add_convert_fusion.2), channel_id=1, source_target_pairs={{0,16},{2,18},{4,20},{6,22},{8,24},{10,26},{12,28},{14,30},{16,0},... | collective-permute-start | bytes 3145736 | tf_op jit(solution)/shard_map/ppermute | solution.py:52
  870.1 131.5 %collective-permute-start.41 = (bf16[8,64,1024]{2,1,0:T(8,128)(2,1)}, bf16[8,64,1024]{2,1,0:T(8,128)(2,1)}, u32[]{:S(2)}, u32[]{:S(2)}) collective-permute-start(bf16[8,64,1024]{2,1,0:T(8,128)(2,1)} %add_convert_fusion.1), channel_id=1, source_target_pairs={{0,16},{2,18},{4,20},{6,22},{8,24},{10,26},{12,28},{14,30},{16,0},... | collective-permute-start | bytes 3145736 | tf_op jit(solution)/shard_map/ppermute | solution.py:52
  918.2 91.8 %collective-permute-start.29 = (bf16[512,1024]{1,0:T(8,128)(2,1)}, bf16[512,1024]{1,0:T(8,128)(2,1)}, u32[]{:S(2)}, u32[]{:S(2)}) collective-permute-start(bf16[512,1024]{1,0:T(8,128)(2,1)} %get-tuple-element.51), channel_id=1, source_target_pairs={{0,1},{1,0},{2,3},{3,2},{4,5},{5,4},{6,7},{7,6},{8,9},{9,8},{10,11... | collective-permute-start | bytes 3145736 | tf_op jit(solution)/shard_map/ppermute | solution.py:57
  1054.8 157.0 %reduce-scatter.5.cloned.1.call-start = ((), (), s32[]{:S(2)}) async-start(), calls=%async_computation.5 | async-start | bytes 1114112 | tf_op jit(solution)/shard_map/reduce_scatter | solution.py:591
  (83 other events, 2109.0 us)
Sparse Core Ops, SparseCore 0:
  11.4 63.3 all-gather.2
  78.1 53.9 all-gather.4
  1055.0 79.6 reduce-scatter.2
  1137.3 74.4 reduce-scatter.4

commit v2 on v1

v2 whole, which is shorter than its diff:
```python
import functools

import jax
import jax.numpy as jnp
from jax import lax
from jax.experimental import pallas as pl
from jax.experimental.pallas import tpu as pltpu
from jax.sharding import PartitionSpec as P

D = 1024
HEADS = 16
KV_HEADS = 8
HEAD_DIM = 64
EXPERTS = 32
TOPK = 8
BLK = 256
GROUPS = 4
BLOCK = 256
LANES = 128

epsilon = 1e-05
stat_decay = 0.9
gain_rate = 0.02
theta_base = 10000.0
masked_score = -1e30
MIB = 1 << 20
SMALL = pl.CostEstimate(flops=1000, bytes_accessed=1000, transcendentals=0)


def cost(flops):
    return pl.CostEstimate(flops=int(flops), bytes_accessed=1000, transcendentals=0)


ANYWHERE = pl.BlockSpec(memory_space=pl.ANY)
SCALARS = pl.BlockSpec(memory_space=pltpu.SMEM)

TOKEN_MASKS = (0, 1, 4, 5)
WEIGHT_BITS = (2, 8)


def dot(left, right, left_dim, right_dim):
    return lax.dot_general(
        left, right, (((left_dim,), (right_dim,)), ((), ())), preferred_element_type=jnp.float32
    )


def normalize(hidden, gain):
    scaling = lax.rsqrt(jnp.mean(hidden * hidden, axis=-1, keepdims=True) + epsilon)
    return (hidden * scaling * gain, scaling)


def normalize_back(hidden, scaling, gain, upstream):
    weighted = upstream * gain
    center = jnp.mean(weighted * hidden, axis=-1, keepdims=True)
    input_part = scaling * weighted - hidden * (scaling * scaling * scaling) * center
    return (input_part, jnp.sum(upstream * hidden * scaling, axis=0))


def swap_dp(values, mask):
    count = lax.axis_size("dp")
    return lax.ppermute(values, "dp", [(i, i ^ mask) for i in range(count)])


def swap_core(values):
    count = lax.axis_size("tensor")
    return lax.ppermute(values, "tensor", [(i, i ^ 1) for i in range(count)])


def sum_everywhere(values):
    values = values + swap_core(values)
    own = sum(values if mask == 0 else swap_dp(values, mask) for mask in TOKEN_MASKS)
    masks = [m for m in range(1, lax.axis_size("dp")) if not m & TOKEN_MASKS[-1]]
    return own + sum(swap_dp(own, mask) for mask in masks)


def in_order(own, other):
    first = lax.axis_index("tensor") == 0
    return jnp.concatenate([jnp.where(first, own, other), jnp.where(first, other, own)], axis=0)


def own_half(values):
    half = values.shape[0] // 2
    return lax.dynamic_slice_in_dim(values, lax.axis_index("tensor") * half, half, 0)


def other_half(values):
    half = values.shape[0] // 2
    return lax.dynamic_slice_in_dim(values, (1 - lax.axis_index("tensor")) * half, half, 0)


def turn(values):
    lane = lax.broadcasted_iota(jnp.int32, values.shape, 1)
    half = HEAD_DIM // 2
    return jnp.where(
        lane % HEAD_DIM < half,
        -pltpu.roll(values, LANES - half, 1),
        pltpu.roll(values, half, 1),
    )


def place_rows(starts_ref, source_refs, target_ref):
    for group, source_ref in enumerate(source_refs):
        count = starts_ref.shape[1]
        slot_rows = source_ref.shape[0] // count
        rows = target_ref.shape[0] // count // len(source_refs)
        for slot in range(count):
            start = pl.multiple_of(starts_ref[group, slot], rows)
            begin = slot * slot_rows
            target_ref[pl.ds(start, rows), :] = source_ref[begin : begin + rows, :]


def attention_forward_kernel(*refs):
    length_ref, starts_ref, x_ref, w0_ref, w1_ref, w2_ref, w3_ref, cos_ref, sin_ref = refs[:9]
    q_ref, k_ref, v_ref, att_ref, w_ref, lse_ref = refs[-6:]
    rows = x_ref.shape[0]
    place_rows(starts_ref, (w0_ref, w1_ref, w2_ref, w3_ref), w_ref)
    low = jnp.bfloat16
    cosine, sine = cos_ref[...], sin_ref[...]
    lane = lax.broadcasted_iota(jnp.int32, (rows, LANES), 1)
    left = lane < HEAD_DIM
    projected = dot(x_ref[...], w_ref[...], 1, 0)
    q_raw = projected[:, :LANES]
    q_turn = turn(q_raw)
    scale = HEAD_DIM ** (-0.5)
    q_rot = (q_raw * cosine + q_turn * sine) * scale
    q_rot_turn = (q_turn * cosine - q_raw * sine) * scale
    q_ref[:, :LANES] = jnp.where(left, q_rot, pltpu.roll(q_rot_turn, HEAD_DIM, 1)).astype(low)
    q_ref[:, LANES:] = jnp.where(left, pltpu.roll(q_rot, HEAD_DIM, 1), q_rot_turn).astype(low)
    kv_raw = projected[:, LANES:]
    k_turn = turn(kv_raw)
    k_rot = kv_raw * cosine + k_turn * sine
    k_rot_turn = k_turn * cosine - kv_raw * sine
    k_ref[...] = jnp.where(left, k_rot, pltpu.roll(k_rot_turn, HEAD_DIM, 1)).astype(low)
    v_high = jnp.where(left, 0.0, kv_raw)
    v_ref[...] = v_high.astype(low)
    v_low = pltpu.roll(v_high, HEAD_DIM, 1).astype(low)
    v_high = v_high.astype(low)
    k_only = jnp.where(left, k_rot, 0.0).astype(low)
    place = lax.broadcasted_iota(jnp.int32, (1, rows), 1)
    bias = jnp.where(place < length_ref[0], 0.0, masked_score)
    for block in range(rows // BLK):
        here = pl.ds(block * BLK, BLK)
        keys = (block + 1) * BLK
        total = None
        for head in range(2):
            q_block = q_ref[here, head * LANES : (head + 1) * LANES]
            scores = dot(q_block, k_only[:keys], 1, 1) + bias[:, :keys]
            top = jnp.max(scores, axis=1, keepdims=True)
            exponent = jnp.exp(scores - top)
            denominator = jnp.sum(exponent, axis=1, keepdims=True)
            weights = (exponent * (1.0 / denominator)).astype(low)
            value = v_high if head else v_low
            part = dot(weights, value[:keys], 1, 0)
            total = part if total is None else total + part
            log_total = jnp.broadcast_to(top + jnp.log(denominator), (BLK, LANES))
            lse_ref[head * 8 : (head + 1) * 8, here] = log_total.T[:8]
        att_ref[here, :] = total.astype(low)


def attention_backward_kernel(*refs):
    length_ref, branch_ref, wo_ref, q_ref, k_ref, v_ref, lse_ref, cos_ref, sin_ref = refs[:9]
    dq_ref, dkv_ref, dk_sum, d0_sum, d1_sum = refs[-5:]
    rows = branch_ref.shape[0]
    low = jnp.bfloat16
    lane = lax.broadcasted_iota(jnp.int32, (rows, LANES), 1)
    left = lane < HEAD_DIM
    grad = dot(branch_ref[...], wo_ref[...], 1, 0).astype(low)
    k_only = jnp.where(left, k_ref[...].astype(jnp.float32), 0.0).astype(low)
    v_high = v_ref[...]
    v_low = pltpu.roll(v_high.astype(jnp.float32), HEAD_DIM, 1).astype(low)
    place = lax.broadcasted_iota(jnp.int32, (rows, BLK), 0)
    seen = place < length_ref[0]
    dk_sum[...] = jnp.zeros_like(dk_sum)
    d0_sum[...] = jnp.zeros_like(d0_sum)
    d1_sum[...] = jnp.zeros_like(d1_sum)
    scale = HEAD_DIM ** (-0.5)
    for block in range(rows // BLK):
        here = pl.ds(block * BLK, BLK)
        keys = (block + 1) * BLK
        grad_block = grad[block * BLK : keys]
        query_grads = []
        for head in range(2):
            q_block = q_ref[here, head * LANES : (head + 1) * LANES]
            value = v_high if head else v_low
            scores = dot(k_only[:keys], q_block, 1, 1)
            log_total = lse_ref[head * 8 : head * 8 + 1, here]
            scores = jnp.where(seen[:keys], scores, masked_score)
            probability = jnp.exp(scores - log_total)
            prob_grad = dot(value[:keys], grad_block, 1, 1)
            weighted = probability * prob_grad
            center = jnp.sum(weighted, axis=0, keepdims=True)
            score_grad = (weighted - probability * center).astype(low)
            d_sum = d1_sum if head else d0_sum
            d_sum[:keys] += dot(probability.astype(low), grad_block, 1, 0)
            dk_sum[:keys] += dot(score_grad, q_block, 1, 0)
            query_grads.append(dot(score_grad, k_ref[:keys], 0, 0))
        cosine, sine = cos_ref[here, :] * scale, sin_ref[here, :] * scale
        zero, one = query_grads
        left_here = left[:BLK]
        straight = jnp.where(left_here, zero, pltpu.roll(one, HEAD_DIM, 1))
        turned = jnp.where(left_here, pltpu.roll(zero, HEAD_DIM, 1), one)
        dq_ref[here, :] = (straight * cosine - turned * sine).astype(low)
    dk_all = dk_sum[...]
    dk_rot = dk_all * cos_ref[...] - pltpu.roll(dk_all, HEAD_DIM, 1) * sin_ref[...]
    dv_all = pltpu.roll(d0_sum[...], HEAD_DIM, 1) + d1_sum[...]
    dkv_ref[...] = jnp.where(left, dk_rot, dv_all).astype(low)


def whole(shape):
    return pl.BlockSpec(shape, lambda h: (0,) * len(shape))


def columns(rows, width):
    return pl.BlockSpec((rows, width), lambda h: (0, h))


def attention_forward(length, starts, normed, w_groups, cosine, sine, deps=()):
    rows = normed.shape[0]
    kv_here = w_groups[0].shape[1] // 256
    low = jnp.bfloat16
    return pl.pallas_call(
        attention_forward_kernel,
        grid=(kv_here,),
        in_specs=[SCALARS, SCALARS, whole((rows, D))]
        + [columns(w.shape[0], 256) for w in w_groups]
        + [whole((rows, LANES))] * 2
        + [ANYWHERE] * len(deps),
        out_specs=[
            columns(rows, 256),
            columns(rows, LANES),
            columns(rows, LANES),
            columns(rows, LANES),
            columns(D, 256),
            pl.BlockSpec((16, rows), lambda h: (h, 0)),
        ],
        out_shape=[
            jax.ShapeDtypeStruct((rows, kv_here * 256), low),
            jax.ShapeDtypeStruct((rows, kv_here * LANES), low),
            jax.ShapeDtypeStruct((rows, kv_here * LANES), low),
            jax.ShapeDtypeStruct((rows, kv_here * LANES), low),
            jax.ShapeDtypeStruct((D, kv_here * 256), low),
            jax.ShapeDtypeStruct((kv_here * 16, rows), jnp.float32),
        ],
        compiler_params=pltpu.CompilerParams(vmem_limit_bytes=50 * MIB),
        cost_estimate=SMALL,
        name="attention_forward",
    )(length, starts, normed, *w_groups, cosine, sine, *deps)


def output_projection_kernel(*refs):
    starts_ref, core_ref, att_ref, w0_ref, w1_ref, w2_ref, w3_ref = refs[:7]
    own_ref, other_ref, w_ref = refs[-3:]
    place_rows(starts_ref, (w0_ref, w1_ref, w2_ref, w3_ref), w_ref)
    half = own_ref.shape[0]
    mine = pl.multiple_of(core_ref[0] * half, half)
    others = pl.multiple_of((1 - core_ref[0]) * half, half)
    other_ref[...] = dot(att_ref[pl.ds(others, half), :], w_ref[...], 1, 1).astype(jnp.bfloat16)
    own_ref[...] = dot(att_ref[pl.ds(mine, half), :], w_ref[...], 1, 1)


def output_projection(starts, core, attended, w_groups, deps=()):
    rows, width = attended.shape
    inside = pl.BlockSpec(memory_space=pltpu.VMEM)
    return pl.pallas_call(
        output_projection_kernel,
        in_specs=[SCALARS, SCALARS] + [inside] * 5 + [ANYWHERE] * len(deps),
        out_specs=[inside] * 3,
        out_shape=[
            jax.ShapeDtypeStruct((rows // 2, D), jnp.float32),
            jax.ShapeDtypeStruct((rows // 2, D), jnp.bfloat16),
            jax.ShapeDtypeStruct((D, width), jnp.bfloat16),
        ],
        compiler_params=pltpu.CompilerParams(vmem_limit_bytes=32 * MIB),
        cost_estimate=SMALL,
        name="output_projection",
    )(starts, core, attended, *w_groups, *deps)


def nothing(*refs):
    return None


def after(values, *deps):
    return pl.pallas_call(
        nothing,
        in_specs=[ANYWHERE] * (1 + len(deps)),
        out_specs=ANYWHERE,
        out_shape=jax.ShapeDtypeStruct(values.shape, values.dtype),
        input_output_aliases={0: 0},
        cost_estimate=SMALL,
        name="after",
    )(values, *deps)


def round_kernel(bounds, values_ref, whole_ref, *piece_refs):
    step = pl.program_id(0)
    rounded = values_ref[...].astype(jnp.bfloat16)
    whole_ref[...] = rounded
    for (begin, end), piece_ref in zip(bounds, piece_refs):

        @pl.when((step >= begin) & (step < end))
        def _(piece_ref=piece_ref):
            piece_ref[...] = rounded


def round_units(values, bounds):
    units = values.shape[0]
    shape = (None,) + values.shape[1:]

    def piece_spec(begin, end):
        return pl.BlockSpec(shape, lambda i: (jnp.clip(i - begin, 0, end - begin - 1), 0, 0, 0))

    return pl.pallas_call(
        functools.partial(round_kernel, bounds),
        grid=(units,),
        in_specs=[pl.BlockSpec(shape, lambda i: (i, 0, 0, 0))],
        out_specs=[pl.BlockSpec(shape, lambda i: (i, 0, 0, 0))]
        + [piece_spec(begin, end) for begin, end in bounds],
        out_shape=[jax.ShapeDtypeStruct(values.shape, jnp.bfloat16)]
        + [
            jax.ShapeDtypeStruct((end - begin,) + values.shape[1:], jnp.bfloat16)
            for begin, end in bounds
        ],
        cost_estimate=SMALL,
        name="round_units",
    )(values)


def attention_backward(length, branch_low, w_output, q2, k2, v, lse, cosine, sine, deps=()):
    rows = branch_low.shape[0]
    kv_here = k2.shape[1] // LANES
    low = jnp.bfloat16
    return pl.pallas_call(
        attention_backward_kernel,
        grid=(kv_here,),
        in_specs=[
            SCALARS,
            whole((rows, D)),
            columns(D, LANES),
            columns(rows, 256),
            columns(rows, LANES),
            columns(rows, LANES),
            pl.BlockSpec((16, rows), lambda h: (h, 0)),
            whole((rows, LANES)),
            whole((rows, LANES)),
        ]
        + [pl.BlockSpec(memory_space=pl.ANY)] * len(deps),
        out_specs=[columns(rows, LANES), columns(rows, LANES)],
        out_shape=[
            jax.ShapeDtypeStruct((rows, kv_here * LANES), low),
            jax.ShapeDtypeStruct((rows, kv_here * LANES), low),
        ],
        scratch_shapes=[pltpu.VMEM((rows, LANES), jnp.float32)] * 3,
        compiler_params=pltpu.CompilerParams(vmem_limit_bytes=50 * MIB),
        cost_estimate=SMALL,
        name="attention_backward",
    )(length, branch_low, w_output, q2, k2, v, lse, cosine, sine, *deps)


CHUNK = 512
UNIT_ROWS = 64


def first_unit(piece_refs, piece):
    return sum(p.shape[0] for p in piece_refs[:piece])


def piece_copy(piece_refs, weights, arrived, piece, kind):
    units = piece_refs[piece].shape[0]
    return pltpu.make_async_copy(
        piece_refs[piece].at[:, kind],
        weights.at[kind, pl.ds(first_unit(piece_refs, piece), units)],
        arrived.at[piece, kind],
    )


def row_copy(row_refs, rows_all, landed, index):
    count = len(row_refs) - 1
    rows = row_refs[0].shape[0]
    source = row_refs[index // 2]
    if index % 2:
        source = row_refs[count].at[pl.ds(index // 2 * rows, rows)]
    return pltpu.make_async_copy(
        source, rows_all.at[pl.ds(index * rows, rows)], landed.at[index]
    )


def fetch(kinds, piece_refs, weights, arrived, row_refs=(None,), rows_all=None, landed=None):
    @pl.when(pl.program_id(0) == 0)
    def _():
        for index in range(2 * len(row_refs) - 2):
            row_copy(row_refs, rows_all, landed, index).start()
        for early in kinds:
            for piece in range(len(piece_refs)):
                for kind in early:
                    piece_copy(piece_refs, weights, arrived, piece, kind).start()


def await_weights(kinds, piece_refs, weights, arrived, chunk=None):
    places = range(len(piece_refs))
    if chunk is not None:
        per_chunk = CHUNK // UNIT_ROWS
        places = [p for p in places if first_unit(piece_refs, p) // per_chunk == chunk]

    @pl.when(pl.program_id(0) == 0)
    def _():
        for piece in places:
            for kind in kinds:
                piece_copy(piece_refs, weights, arrived, piece, kind).wait()


def await_rows(row_refs, rows_all, landed):
    step = pl.program_id(0)
    for index in range(2 * len(row_refs) - 2):

        @pl.when(step == index)
        def _(index=index):
            row_copy(row_refs, rows_all, landed, index).wait()


def chunk_weights(weights, kind, chunk):
    units = CHUNK // UNIT_ROWS
    return weights[kind, chunk * units : (chunk + 1) * units].reshape(CHUNK, D)


def spread_weights(route_ref, column, per_unit):
    rows = route_ref.shape[0]
    units = CHUNK // UNIT_ROWS
    count = units if per_unit else units // 4
    width = CHUNK // count
    pieces = [
        jnp.broadcast_to(route_ref[:, column * count + j : column * count + j + 1], (rows, width))
        for j in range(count)
    ]
    return jnp.concatenate(pieces, axis=1)


def store_step(out_refs, values):
    step = pl.program_id(0)
    for index, out_ref in enumerate(out_refs):

        @pl.when(step == index)
        def _(out_ref=out_ref):
            out_ref[...] = values


def expert_hidden(x, route_ref, weights, piece_refs, arrived, first_column, per_unit, outs):
    low = jnp.bfloat16
    slope_ref, silu_ref, inner_ref = outs
    for chunk in range(slope_ref.shape[1] // CHUNK):
        here = slice(chunk * CHUNK, (chunk + 1) * CHUNK)
        await_weights((0, 1), piece_refs, weights, arrived, chunk)
        gate = dot(x, chunk_weights(weights, 0, chunk), 1, 1)
        upper = dot(x, chunk_weights(weights, 1, chunk), 1, 1)
        sigmoid = 0.5 * jnp.tanh(0.5 * gate) + 0.5
        silu = gate * sigmoid
        weight = spread_weights(route_ref, first_column + chunk, per_unit)
        weighted_upper = weight * upper
        slope_ref[:, here] = (weighted_upper * (sigmoid + silu * (1.0 - sigmoid))).astype(low)
        silu_ref[:, here] = (weight * silu).astype(low)
        inner_ref[:, here] = (silu * weighted_upper).astype(low)
    await_weights((2,), piece_refs, weights, arrived)
    return dot(inner_ref[...], weights[2].reshape(-1, D), 1, 0)


def expert_first_kernel(count, pieces, per_unit, *refs):
    parts = count // 2 + 1
    row_refs, route_ref = refs[:parts], refs[parts]
    piece_refs = refs[parts + 1 : parts + 1 + pieces]
    x_ref, mixed_ref, slope_ref, silu_ref, inner_ref = refs[-9:-4]
    weights, arrived, rows_all, landed = refs[-4:]
    fetch(((0, 1), (2,)), piece_refs, weights, arrived, row_refs, rows_all, landed)
    await_rows(row_refs, rows_all, landed)
    rows = x_ref.shape[0]
    x = rows_all[pl.ds(pl.multiple_of(pl.program_id(0) * rows, rows), rows), :]
    x_ref[...] = x
    outs = (slope_ref, silu_ref, inner_ref)
    mixed_ref[...] = expert_hidden(
        x, route_ref, weights, piece_refs, arrived, 0, per_unit, outs
    ).astype(jnp.bfloat16)


def expert_second_kernel(count, pieces, per_unit, first_column, *refs):
    x_ref, mixed_ref, route_ref = refs[:3]
    piece_refs = refs[3 : 3 + pieces]
    out_refs = refs[-5 - count : -5]
    weights, arrived = refs[-2:]
    fetch(((0, 1), (2,)), piece_refs, weights, arrived)
    part = expert_hidden(
        x_ref[...], route_ref, weights, piece_refs, arrived, first_column, per_unit, refs[-5:-2]
    )
    store_step(out_refs, (part + mixed_ref[...].astype(jnp.float32)).astype(jnp.bfloat16))


def expert_backward_kernel(count, pieces, *refs):
    parts = count // 2 + 1
    row_refs = refs[:parts]
    slope_refs, silu_refs = refs[parts : parts + 2], refs[parts + 2 : parts + 4]
    piece_refs = refs[parts + 4 : parts + 4 + pieces]
    out_refs = refs[-9 - count : -9]
    grad_ref = refs[-9]
    gate_refs, upper_refs = refs[-8:-6], refs[-6:-4]
    weights, arrived, rows_all, landed = refs[-4:]
    low = jnp.bfloat16
    fetch(((2,), (0,), (1,)), piece_refs, weights, arrived, row_refs, rows_all, landed)
    await_rows(row_refs, rows_all, landed)
    rows = grad_ref.shape[0]
    grad = rows_all[pl.ds(pl.multiple_of(pl.program_id(0) * rows, rows), rows), :]
    grad_ref[...] = grad
    chunks = slope_refs[0].shape[1] // CHUNK
    for chunk in range(2 * chunks):
        half, place = chunk // chunks, chunk % chunks
        here = slice(place * CHUNK, (place + 1) * CHUNK)
        await_weights((2,), piece_refs, weights, arrived, chunk)
        inner_grad = dot(grad, chunk_weights(weights, 2, chunk), 1, 1)
        slope, silu = slope_refs[half][:, here], silu_refs[half][:, here]
        gate_refs[half][:, here] = (inner_grad * slope.astype(jnp.float32)).astype(low)
        upper_refs[half][:, here] = (inner_grad * silu.astype(jnp.float32)).astype(low)
    units = weights.shape[1] // 2
    await_weights((0, 1), piece_refs, weights, arrived)
    total = None
    for half in range(2):
        mine = pl.ds(half * units, units)
        part = dot(gate_refs[half][...], weights[0, mine].reshape(-1, D), 1, 0)
        part = part + dot(upper_refs[half][...], weights[1, mine].reshape(-1, D), 1, 0)
        total = part if total is None else total + part
    store_step(out_refs, total.astype(low))


def fixed(shape):
    return pl.BlockSpec(shape, lambda i: (0,) * len(shape))


def token_block(rows, width, first=0):
    return pl.BlockSpec((rows, width), lambda i: (first + i, 0))


def expert_scratch(pieces, count=0, rows=0):
    units = sum(p.shape[0] for p in pieces)
    scratch = [
        pltpu.VMEM((3, units, UNIT_ROWS, D), jnp.bfloat16),
        pltpu.SemaphoreType.DMA((len(pieces), 3)),
    ]
    if count:
        scratch += [
            pltpu.VMEM((count * rows, D), jnp.bfloat16),
            pltpu.SemaphoreType.DMA((count,)),
        ]
    return scratch


def expert_call(
    kernel, name, steps, operands, specs, out_specs, widths, singles, kept, scratch, estimate=SMALL
):
    rows, total_rows = singles[1], singles[2]
    low = jnp.bfloat16
    operands, specs = list(operands), list(specs)
    aliases = {}
    if kept is not None:
        for index, buffer in enumerate(kept):
            aliases[len(operands)] = singles[0] + index
            operands.append(buffer)
            specs.append(ANYWHERE)
    outs = pl.pallas_call(
        kernel,
        grid=(steps,),
        in_specs=specs,
        out_specs=[fixed((rows, D))] * singles[0] + out_specs,
        out_shape=[jax.ShapeDtypeStruct((rows, D), low)] * singles[0]
        + [jax.ShapeDtypeStruct((total_rows, w), low) for w in widths],
        scratch_shapes=scratch,
        input_output_aliases=aliases,
        compiler_params=pltpu.CompilerParams(vmem_limit_bytes=60 * MIB),
        cost_estimate=estimate,
        name=name,
    )(*operands)
    return outs[: singles[0]], outs[singles[0] :]


def expert_first(row_parts, route_columns, per_unit, pieces, deps):
    count, rows = 2 * len(row_parts) - 2, row_parts[0].shape[0]
    width = sum(p.shape[0] for p in pieces) * UNIT_ROWS
    widths = [D, D, width, width, width]
    return expert_call(
        functools.partial(expert_first_kernel, count, len(pieces), per_unit),
        "expert_first",
        count,
        list(row_parts) + [route_columns] + list(pieces) + list(deps),
        [ANYWHERE] * len(row_parts)
        + [token_block(rows, route_columns.shape[1])]
        + [ANYWHERE] * (len(pieces) + len(deps)),
        [token_block(rows, w) for w in widths],
        widths,
        (0, rows, count * rows),
        None,
        expert_scratch(pieces, count, rows),
        cost(6 * count * rows * width * D),
    )[1]


def expert_second(count, rows, x, mixed, route_columns, per_unit, pieces, deps):
    width = sum(p.shape[0] for p in pieces) * UNIT_ROWS
    return expert_call(
        functools.partial(expert_second_kernel, count, len(pieces), per_unit, width // CHUNK),
        "expert_second",
        count,
        [x, mixed, route_columns] + list(pieces) + list(deps),
        [
            token_block(rows, D),
            token_block(rows, D),
            token_block(rows, route_columns.shape[1]),
        ]
        + [ANYWHERE] * (len(pieces) + len(deps)),
        [token_block(rows, width)] * 3,
        [width] * 3,
        (count, rows, x.shape[0]),
        None,
        expert_scratch(pieces),
    )


def expert_backward(first, row_parts, slopes, silus, pieces, kept):
    count, rows = 2 * len(row_parts) - 2, row_parts[0].shape[0]
    width = slopes[0].shape[1]
    widths = [D] + [width] * 4
    return expert_call(
        functools.partial(expert_backward_kernel, count, len(pieces)),
        "expert_backward",
        count,
        list(row_parts) + list(slopes) + list(silus) + list(pieces),
        [ANYWHERE] * len(row_parts)
        + [token_block(rows, width, first)] * 4
        + [ANYWHERE] * len(pieces),
        [token_block(rows, w, first) for w in widths],
        widths,
        (count, rows, slopes[0].shape[0]),
        kept,
        expert_scratch(pieces, count, rows),
    )


def weight_grad_kernel(count, *refs):
    right_ref = refs[count]
    outs = refs[-2 * count :]
    step = pl.program_id(0)
    for index in range(count):
        for slot in range(2):

            @pl.when(step == 2 * index + slot)
            def _(index=index, slot=slot):
                outs[2 * index + slot][...] = dot(refs[index][...], right_ref[...], 0, 0).astype(
                    jnp.bfloat16
                )


def weight_grads(lefts, right, deps=(), estimate=SMALL):
    rows = right.shape[0]
    columns_here = lefts[0].shape[1] // 2
    count = len(lefts)

    def left_spec(index):
        return pl.BlockSpec(
            (rows, columns_here), lambda i: (0, 1 - jnp.clip(i - 2 * index, 0, 1))
        )

    return pl.pallas_call(
        functools.partial(weight_grad_kernel, count),
        grid=(2 * count,),
        in_specs=[left_spec(index) for index in range(count)]
        + [pl.BlockSpec((rows, D), lambda i: (0, 0), pipeline_mode=pl.Buffered(1))]
        + [ANYWHERE] * len(deps),
        out_specs=[fixed((columns_here, D))] * (2 * count),
        out_shape=[jax.ShapeDtypeStruct((columns_here, D), jnp.bfloat16)] * (2 * count),
        compiler_params=pltpu.CompilerParams(vmem_limit_bytes=56 * MIB),
        cost_estimate=estimate,
        name="weight_grads",
    )(*lefts, right, *deps)


def update_blocks(grads, lefts, rights, left_roots, right_roots, left_outs, right_outs, step_outs):
    low = jnp.bfloat16
    grads = [grad.astype(low) for grad in grads]
    firsts = [
        dot(root[...].astype(low), grad, 1, 0).astype(low) for root, grad in zip(left_roots, grads)
    ]
    for grad, left, out in zip(grads, lefts, left_outs):
        out[...] = stat_decay * left[...] + dot(grad, grad, 1, 1)
    for first, root, (out, master) in zip(firsts, right_roots, step_outs):
        out[...] = master[...] - D ** (-0.5) * dot(first, root[...].astype(low), 1, 0)
    for grad, right, out in zip(grads, rights, right_outs):
        out[...] = stat_decay * right[...] + dot(grad, grad, 0, 0)


def expert_update_kernel(count, *refs):
    parts = refs[:count]
    master, left, right, left_root, right_root = refs[count : count + 5]
    grad_out, left_out, right_out, new_out = refs[-4:]
    units, rows, _ = grad_out.shape
    grad = parts[0][...].astype(jnp.float32)
    for part in parts[1:]:
        grad = grad + part[...].astype(jnp.float32)
    grad = grad.reshape(units, rows, D)
    grad_out[...] = grad
    blocks = [(u, b) for u in range(units) for b in range(D // BLOCK)]

    def wide(ref):
        return [ref.at[u, :, b * BLOCK : (b + 1) * BLOCK] for u, b in blocks]

    def square(ref):
        return [ref.at[u, b] for u, b in blocks]

    update_blocks(
        [grad[u, :, b * BLOCK : (b + 1) * BLOCK] for u, b in blocks],
        square(left),
        square(right),
        square(left_root),
        square(right_root),
        square(left_out),
        square(right_out),
        list(zip(wide(new_out), wide(master))),
    )


def expert_update(kind, parts, state, kept, deps=()):
    master, left, right, left_root, right_root = state
    units, _, rows, _ = master.shape
    step = min(units, 2)
    flat = pl.BlockSpec((step, None, rows, D), lambda i: (i, kind, 0, 0))
    lefts = pl.BlockSpec((step, None) + left.shape[2:], lambda i: (i, kind, 0, 0, 0))
    rights = pl.BlockSpec((step, None) + right.shape[2:], lambda i: (i, kind, 0, 0, 0))
    operands = list(parts) + list(state) + list(deps)
    specs = [pl.BlockSpec((step * rows, D), lambda i: (i, 0))] * len(parts)
    specs += [flat, lefts, rights, lefts, rights] + [ANYWHERE] * len(deps)
    aliases = {}
    if kept is not None:
        for index, buffer in enumerate(kept):
            aliases[len(operands)] = index
            operands.append(buffer)
            specs.append(ANYWHERE)
    return pl.pallas_call(
        functools.partial(expert_update_kernel, len(parts)),
        grid=(units // step,),
        in_specs=specs,
        out_specs=[flat, lefts, rights, flat],
        out_shape=[jax.ShapeDtypeStruct(a.shape, jnp.float32) for a in (master, left, right, master)],
        input_output_aliases=aliases,
        compiler_params=pltpu.CompilerParams(vmem_limit_bytes=56 * MIB),
        cost_estimate=cost(12e9),
        name="expert_update",
    )(*operands)


def attention_update_kernel(qkv_ref, wo_ref, master, left, right, left_root, right_root, *outs):
    grad_out, left_out, right_out, new_out = outs
    heads = qkv_ref.shape[1] // 256
    rows = qkv_ref.shape[0]
    low_lanes = lax.broadcasted_iota(jnp.int32, (rows, LANES), 1) < HEAD_DIM
    grad = qkv_ref[...].astype(jnp.float32)
    queries = heads * LANES
    keys = queries // 2
    for head in range(heads):
        grad_out[:, head * LANES : (head + 1) * LANES] = grad[:, head * 256 : head * 256 + LANES]
    for pair in range(heads // 2):
        begin = pair * 512 + LANES
        one, two = grad[:, begin : begin + LANES], grad[:, begin + 256 : begin + 256 + LANES]
        place = queries + pair * LANES
        grad_out[:, place : place + LANES] = jnp.where(low_lanes, one, pltpu.roll(two, HEAD_DIM, 1))
        place = place + keys
        grad_out[:, place : place + LANES] = jnp.where(low_lanes, pltpu.roll(one, HEAD_DIM, 1), two)
    grad_out[:, queries + 2 * keys :] = wo_ref[...].astype(jnp.float32)
    blocks = range(grad_out.shape[1] // BLOCK)

    def wide(ref):
        return [ref.at[:, b * BLOCK : (b + 1) * BLOCK] for b in blocks]

    def square(ref):
        return [ref.at[b] for b in blocks]

    update_blocks(
        [part[...] for part in wide(grad_out)],
        square(left),
        square(right),
        square(left_root),
        square(right_root),
        square(left_out),
        square(right_out),
        list(zip(wide(new_out), wide(master))),
    )


def attention_update(qkv_part, output_part, state):
    inside = pl.BlockSpec(memory_space=pltpu.VMEM)
    master, left, right = state[:3]
    return pl.pallas_call(
        attention_update_kernel,
        in_specs=[inside] * 7,
        out_specs=[inside] * 4,
        out_shape=[jax.ShapeDtypeStruct(a.shape, jnp.float32) for a in (master, left, right, master)],
        compiler_params=pltpu.CompilerParams(vmem_limit_bytes=40 * MIB),
        cost_estimate=SMALL,
        name="attention_update",
    )(qkv_part, output_part, *state)


def spread_tokens(own, relay):
    beside, across, both = TOKEN_MASKS[1:]
    rows = [own, swap_dp(own, beside), swap_dp(own, across)]
    return rows + [swap_dp(rows[2], beside) if relay else swap_dp(own, both)]


def with_other(own_rows):
    return list(own_rows) + [swap_core(jnp.concatenate(own_rows, axis=0))]


def sum_cores(place, parts):
    own, other = parts
    total = own.astype(jnp.float32) + swap_core(other).astype(jnp.float32)
    return total if place == 0 else total.astype(jnp.bfloat16)


def return_tokens(sums):
    total = sums[0]
    for rows, mask in zip(sums[1:], TOKEN_MASKS[1:]):
        total = total + swap_dp(rows, mask).astype(jnp.float32)
    return total


def extra_masks():
    count = lax.axis_size("dp")
    used = sum(WEIGHT_BITS) + TOKEN_MASKS[-1]
    masks = []
    mask = 1
    while mask < count:
        if not mask & used:
            masks.append(mask)
        mask *= 2
    return masks


def gather_attention(own, count, qkv_cols, deps):
    low = jnp.bfloat16
    high_digit = jnp.floor(count / 64.0)
    digits = jnp.stack([high_digit, count - 64.0 * high_digit]).astype(low)
    digits = jnp.pad(digits[None, :], ((0, 7), (0, own.shape[1] - 2)))
    own = jnp.concatenate([own, digits], axis=0)
    slot_rows = own.shape[0]
    masks = list(range(0, lax.axis_size("dp"), 4))
    line = jnp.concatenate([own] + [swap_dp(own, mask) for mask in masks[1:]], axis=0)
    line = after(line, *deps)
    inner, outer = line[:, :qkv_cols], line[:, qkv_cols:]
    inner = [inner] + [swap_dp(inner, mask) for mask in (1, 2, 3)]
    outer = [outer] + [swap_dp(outer, mask) for mask in (1, 2, 3)]
    table = jnp.array([[group ^ mask for mask in masks] for group in range(4)], jnp.int32)
    total = 0.0
    for group in inner:
        digits = group.reshape(len(masks), slot_rows, -1)[:, slot_rows - 8, :2]
        digits = jnp.sum(digits.astype(jnp.float32), axis=0)
        total = total + 64.0 * digits[0] + digits[1]
    total = total.reshape(1, 1)
    return line, inner, outer, lax.axis_index("dp") ^ table, (total + swap_core(total))[0, 0]


FAR_PIECES = ((0, 4), (4, 8))
NEAR_PIECES = ((0, 3), (3, 8))


def round_weights(master):
    bounds = FAR_PIECES + NEAR_PIECES
    extra = extra_masks()
    if not extra:
        shard, *pieces = round_units(master, bounds)
    else:
        shard = round_units(master, ())[0]
        for mask in extra:
            shard = jnp.concatenate([shard, swap_dp(shard, mask)], axis=0)
        pieces = [shard[begin:end] for begin, end in bounds]
    return shard, pieces[: len(FAR_PIECES)], pieces[len(FAR_PIECES) :]


def unit_owners():
    masks = [0]
    for mask in extra_masks():
        masks = masks + [m ^ mask for m in masks]
    first, second = WEIGHT_BITS
    masks = [m ^ k for k in (0, first, second, first ^ second) for m in masks]
    return lax.axis_index("dp") ^ jnp.array(masks, jnp.int32)


def add_grads(far, both):
    return (far.astype(jnp.float32) + swap_dp(both, WEIGHT_BITS[0]).astype(jnp.float32)).astype(
        jnp.bfloat16
    )


def grad_terms(own, near, far):
    parts = [own, swap_dp(near, WEIGHT_BITS[0]), far]
    masks = extra_masks()
    if not masks:
        return parts
    total = sum(p.astype(jnp.float32) for p in parts)
    for mask in reversed(masks):
        half = total.shape[0] // 2
        sent = swap_dp(total[half:].astype(jnp.bfloat16), mask)
        total = total[:half] + sent.astype(jnp.float32)
    return [total]


def on_device(
    activations,
    targets,
    lengths,
    token_mask,
    routes,
    route_weights,
    norm_gains,
    attention_master,
    expert_master,
    attention_left,
    attention_right,
    attention_left_root,
    attention_right_root,
    expert_left,
    expert_right,
    expert_left_root,
    expert_right_root,
):
    low = jnp.bfloat16
    own_rows = activations.shape[0]
    tensor_size = lax.axis_size("tensor")
    core = lax.axis_index("tensor")
    tokens_total = own_rows * tensor_size * lax.axis_size("dp")
    seq_length = lengths[0]
    position = core * own_rows + jnp.arange(own_rows, dtype=jnp.int32)
    valid_rows = ((token_mask == 1) & (position < seq_length)).astype(jnp.float32)
    valid_here = jnp.sum(valid_rows)

    routing = jnp.concatenate([routes.T.astype(jnp.float32), route_weights.T], axis=0)
    routing_parts = [routing] + [swap_dp(routing, mask) for mask in TOKEN_MASKS[1:]]
    heads_here = HEADS // tensor_size
    kv_here = KV_HEADS // tensor_size
    query_cols = heads_here * HEAD_DIM
    key_cols = kv_here * HEAD_DIM
    qkv_cols = query_cols + 2 * key_cols
    rows_here = attention_master.shape[0]

    def by_head(values):
        rows = values.shape[0]
        query = values[:, :query_cols].reshape(rows, kv_here, LANES)
        key = values[:, query_cols : query_cols + key_cols].reshape(rows, kv_here, HEAD_DIM)
        value = values[:, query_cols + key_cols : qkv_cols].reshape(rows, kv_here, HEAD_DIM)
        return jnp.concatenate([query, key, value], axis=2).reshape(rows, qkv_cols)

    attention_low = attention_master.astype(low)
    own_columns = jnp.concatenate([by_head(attention_low), attention_low[:, qkv_cols:]], axis=1)
    shard, for_far, for_near = round_weights(expert_master)
    line, w_inner, w_outer, devices, valid_total = gather_attention(
        own_columns, valid_here, qkv_cols, [shard] + routing_parts[1:]
    )
    starts = devices * rows_here
    hidden = activations.astype(jnp.float32)
    normed_own, attention_scaling = normalize(hidden, norm_gains[0])
    normed_own = normed_own.astype(low)
    normed = in_order(normed_own, swap_core(normed_own))

    near_bit, far_bit = WEIGHT_BITS
    for_near[0] = after(for_near[0], *w_inner[1:])
    near = [swap_dp(piece, near_bit) for piece in for_near]
    far = [swap_dp(after(piece, line), far_bit) for piece in for_far]

    seq_rows = normed.shape[0]
    half_width = HEAD_DIM // 2
    frequency = theta_base ** (-jnp.arange(half_width, dtype=jnp.float32) * 2.0 / HEAD_DIM)
    angles = jnp.arange(seq_rows, dtype=jnp.float32)[:, None] * frequency[None, :]
    cosine = jnp.tile(jnp.cos(angles), (1, LANES // half_width))
    sine = jnp.tile(jnp.sin(angles), (1, LANES // half_width))
    q2, k2, v_high, attended, w_qkv, log_totals = attention_forward(
        lengths,
        starts,
        normed,
        w_inner,
        cosine,
        sine,
    )
    branch, branch_other, w_output = output_projection(
        starts, core.reshape(1).astype(jnp.int32), attended, w_outer, far[:1] + near[:1]
    )
    branch = branch + swap_core(branch_other).astype(jnp.float32)
    middle = hidden + branch
    mix_own, mix_scaling = normalize(middle, norm_gains[1])

    routing = jnp.stack(routing_parts).reshape(len(TOKEN_MASKS), 2 * TOPK, 2, own_rows)
    routing = jnp.stack(
        [
            lax.dynamic_index_in_dim(routing, core, 2, keepdims=False),
            lax.dynamic_index_in_dim(routing, 1 - core, 2, keepdims=False),
        ],
        axis=1,
    )
    unit_here = expert_master.shape[0]
    unit_ids = (unit_owners()[:, None] * unit_here + jnp.arange(unit_here)[None, :]).reshape(-1)
    expert_of = unit_ids // GROUPS
    per_unit = unit_here % 4 != 0
    if not per_unit:
        expert_of = expert_of[::4]
    named = (
        routing[:, :, None, :TOPK] == expert_of.astype(jnp.float32)[None, None, :, None, None]
    )
    route_columns = jnp.sum(jnp.where(named, routing[:, :, None, TOPK:], 0.0), axis=3)
    route_columns = route_columns.transpose(0, 1, 3, 2).reshape(-1, expert_of.shape[0])

    spread = spread_tokens(mix_own.astype(low), True)
    both = [swap_dp(piece, near_bit) for piece in far]
    later = [after(spread[1], far[1], near[1]), spread[2], after(spread[3], both[0])]
    mix_rows = with_other(spread[:1] + later)
    mix, mixed, *firsts = expert_first(
        mix_rows, route_columns, per_unit, [shard] + near, []
    )
    pieces = [shard] + near + far + both
    mixed_parts, seconds = expert_second(
        2 * len(spread), own_rows, mix, mixed, route_columns, per_unit, far + both, []
    )
    slopes, silus, inners = ([firsts[i], seconds[i]] for i in range(3))
    sums = [sum_cores(i, mixed_parts[2 * i : 2 * i + 2]) for i in range(len(TOKEN_MASKS))]
    output = middle + return_tokens(sums)
    residual_error = output - targets
    loss_part = jnp.sum(valid_rows[:, None] * residual_error * residual_error)
    output_grad = 2.0 / valid_total * valid_rows[:, None] * residual_error

    spread = spread_tokens(output_grad.astype(low), False)
    backward = functools.partial(expert_backward, slopes=slopes, silus=silus, pieces=pieces)
    parts0, kept = backward(0, [spread[0], swap_core(spread[0])], kept=None)
    later = [after(rows, parts0[0]) for rows in spread[1:]]
    parts1, kept = backward(2, with_other(later), kept=kept)
    parts = list(parts0) + list(parts1)
    sums = [sum_cores(i, parts[2 * i : 2 * i + 2]) for i in range(len(TOKEN_MASKS))]
    sent = return_tokens(sums)
    output_low = kept[0]
    gates, uppers = kept[1:3], kept[3:5]
    full = cost(30e9)
    down_far = weight_grads([inners[1]], output_low, (), full)
    gate_far = weight_grads([gates[1]], mix, [down_far[0]] + sums[1:], full)
    down_sum = add_grads(down_far[1], down_far[0])
    upper_far = weight_grads([uppers[1]], mix, [gate_far[0], down_sum], full)
    gate_sum = add_grads(gate_far[1], gate_far[0])
    upper_sum = add_grads(upper_far[1], upper_far[0])
    far_gate, far_upper, far_down = (
        swap_dp(rows, far_bit) for rows in (gate_sum, upper_sum, down_sum)
    )
    mix_back, gain_mix = normalize_back(middle, mix_scaling, norm_gains[1], sent)
    middle_grad = output_grad + mix_back
    branch_own = middle_grad.astype(low)
    branch_low = in_order(branch_own, swap_core(branch_own))
    dq, dkv = attention_backward(
        lengths, branch_low, w_output, q2, k2, v_high, log_totals, cosine, sine,
        [upper_far[0], gate_sum],
    )
    qkv_grad = jnp.concatenate(
        [dq.reshape(seq_rows, kv_here, LANES), dkv.reshape(seq_rows, kv_here, LANES)], axis=2
    ).reshape(seq_rows, qkv_cols)
    qkv_part = dot(normed, qkv_grad, 0, 0).astype(low)
    output_part = dot(branch_low, attended, 0, 0).astype(low)
    down_near = weight_grads([inners[0]], output_low, [qkv_part, upper_sum, far_down], full)
    gate_up_near = weight_grads(
        [gates[0], uppers[0]], mix, [down_near[0], output_part], full
    )
    qkv_part = lax.psum_scatter(qkv_part, "dp", scatter_dimension=0, tiled=True)
    output_part = lax.psum_scatter(output_part, "dp", scatter_dimension=0, tiled=True)
    normed_grad_other = dot(other_half(qkv_grad), w_qkv, 1, 1).astype(low)
    normed_grad = dot(own_half(qkv_grad), w_qkv, 1, 1)
    normed_grad = normed_grad + swap_core(normed_grad_other).astype(jnp.float32)
    attention_back, gain_attention = normalize_back(
        hidden, attention_scaling, norm_gains[0], normed_grad
    )
    input_grad = middle_grad + attention_back
    parts = {
        2: grad_terms(down_near[1], down_near[0], far_down),
        0: grad_terms(gate_up_near[1], gate_up_near[0], far_gate),
        1: grad_terms(gate_up_near[3], gate_up_near[2], far_upper),
    }
    state = (expert_master, expert_left, expert_right, expert_left_root, expert_right_root)
    updated = expert_update(2, parts[2], state, None, [input_grad, far_gate])
    updated = expert_update(0, parts[0], state, updated, [far_upper])
    loss_row = jnp.full((1, D), loss_part)
    sums = jnp.concatenate([gain_attention[None], gain_mix[None], loss_row], axis=0)
    sums = sum_everywhere(after(sums, updated[0]))
    updated = expert_update(1, parts[1], state, updated, [sums])
    expert_grad, expert_left_new, expert_right_new, expert_new = updated
    gain_grad = sums[:2]
    mean_loss = sums[2, 0] / valid_total
    gains_new = norm_gains - gain_rate * tokens_total**0.5 * gain_grad

    attention_grad, attention_left_new, attention_right_new, attention_new = attention_update(
        qkv_part,
        output_part,
        (
            attention_master,
            attention_left[0],
            attention_right[0],
            attention_left_root[0],
            attention_right_root[0],
        ),
    )
    return (
        output,
        mean_loss,
        input_grad,
        gain_grad,
        gains_new,
        attention_grad,
        attention_left_new[None],
        attention_right_new[None],
        attention_new,
        expert_grad,
        expert_left_new,
        expert_right_new,
        expert_new,
    )


def solution(mesh):
    return jax.shard_map(
        on_device,
        mesh=mesh,
        in_specs=(
            P(("dp", "tensor"), None),
            P(("dp", "tensor"), None),
            P("dp"),
            P(("dp", "tensor")),
            P("dp", None),
            P("dp", None),
            P(),
            P("dp", "tensor"),
            P("dp", None, "tensor", None),
            P("dp", "tensor", None, None),
            P("dp", "tensor", None, None),
            P("dp", "tensor", None, None),
            P("dp", "tensor", None, None),
            P("dp", None, None, "tensor", None),
            P("dp", None, "tensor", None, None),
            P("dp", None, None, "tensor", None),
            P("dp", None, "tensor", None, None),
        ),
        out_specs=(
            P(("dp", "tensor"), None),
            P(),
            P(("dp", "tensor"), None),
            P(),
            P(),
            P("dp", "tensor"),
            P("dp", "tensor", None, None),
            P("dp", "tensor", None, None),
            P("dp", "tensor"),
            P("dp", None, "tensor", None),
            P("dp", None, None, "tensor", None),
            P("dp", None, "tensor", None, None),
            P("dp", None, "tensor", None),
        ),
        check_vma=False,
    )
```

time: 1240 us -> 837 us (0.68)
  waiting for transfers between devices: 586 us -> 272 us
  Pallas kernels: 216 us -> 362 us
  matrix products: 137 us -> 12.1 us
  local copies, waits for them, and re-layouts: 105 us -> 34.9 us
  other arithmetic: 85.3 us -> 55.8 us
  starting transfers between devices: 81.2 us -> 64.4 us
    ppermute x35 -> x45, waiting for transfers between devices: 419 us -> 257 us  [swap_dp(): return lax.ppermute(values, 'dp', [(i, i ^ mask) for i in range(count)])]
    pallas_call x4 -> x27, Pallas kernels: 216 us -> 362 us  [the longest x4 172 us: expert_call(): pl.pallas_call(kernel, grid=(steps,), in_specs=specs, out_specs=[fixed((r...]
    all_gather x2 -> x0, waiting for transfers between devices: 77.3 us -> none  [the longest x1 46.7 us: on_device(): w_qkv = lax.all_gather(by_head(attention_low), 'dp', axis=0, tiled=True)]
    dot_general x7 -> x4, matrix products: 87.4 us -> 12.1 us  [dot(): lax.dot_general(left, right, (((left_dim,), (right_dim,)), ((), ())), pre...]
    reduce_scatter x1, waiting for transfers between devices: 75.2 us -> 0.02 us  [on_device(): lax.psum_scatter(output_part, 'dp', scatter_dimension=0, tiled=True)]
    dot_general x6 -> x0, matrix products: 49.5 us -> none  [the longest x1 19.7 us: on_device(): jnp.einsum('...ki,...kj->...ij', expert_blocks, expert_blocks)]
    add x9 -> x2, other arithmetic: 24.4 us -> 0.02 us  [the longest x1 0.01 us: sum_everywhere(): sum((values if mask == 0 else swap_dp(values, mask) for mask in TOKEN_MAS...]
    slice x12 -> x7, local copies, waits for them, and re-layouts: 23.9 us -> 4.43 us  [the longest x4 2.34 us: gather_attention(): total = total + 64.0 * digits[0] + digits[1]]
  transfers between devices with their start and end apart: 49 -> 64, of which waited for: 25 -> 30; matrix products, arithmetic and copies ran while one was open for 18% -> 8% of each run, Pallas kernels for 2% -> 38%
where the time goes in v2:
time: 837 us; the launch traced here: 826 us
  Pallas kernels  362 us (43%)
  waiting for transfers between devices  272 us (32%)
  starting transfers between devices  64.4 us (8%)
  other arithmetic  55.8 us (7%)
  local copies, waits for them, and re-layouts  34.9 us (4%)
  between operations  25 us (3%)
  matrix products  12.1 us (1%)
    ppermute x45, waiting for transfers between devices, swap_dp(): return lax.ppermute(values, 'dp', [(i, i ^ mask) for i in range(count)])  257 us
    pallas_call x4, Pallas kernels, expert_call(): pl.pallas_call(kernel, grid=(steps,), in_specs=specs, out_specs=[fixed((r...  172 us
    pallas_call x5, Pallas kernels, weight_grads(): pl.pallas_call(functools.partial(weight_grad_kernel, count), grid=(2 * co...  87.6 us
    ppermute x45, starting transfers between devices, swap_dp(): return lax.ppermute(values, 'dp', [(i, i ^ mask) for i in range(count)])  60.9 us
    pallas_call x3, Pallas kernels, expert_update(): pl.pallas_call(functools.partial(expert_update_kernel, len(parts)), grid=...  40.3 us
    pallas_call x1, Pallas kernels, attention_backward(): pl.pallas_call(attention_backward_kernel, grid=(kv_here,), in_specs=[SCAL...  26.8 us
    pallas_call x1, Pallas kernels, attention_forward(): pl.pallas_call(attention_forward_kernel, grid=(kv_here,), in_specs=[SCALA...  23 us
    unnamed x162, local copies, waits for them, and re-layouts  19.1 us
  transfers between devices with their start and end apart: 64, of which 30 were waited for; matrix products, arithmetic and copies ran while one was open for 8% of the time, Pallas kernels for 38%

profile of v2, /device:TPU:0, one launch (start us, length us, event | category | flops | bytes accessed | tf_op | source)
XLA Modules:
  0.0 826.2 jit_solution(1153591065074894434)
XLA Ops:
  8.9 4.0 collective-permute-start.6
  18.2 4.0 collective-permute-start.3
  22.7 8.5 %round_units.1 = (bf16[8,3,64,1024]{3,2,1,0:T(8,128)(2,1)}, bf16[4,3,64,1024]{3,2,1,0:T(8,128)(2,1)}, bf16[4,3,64,1024]{3,2,1,0:T(8,128)(2,1)}, bf16[3,3,64,1024]{3,2,1,0:T(8,128)(2,1)}, bf16[5,3,64,1024]{3,2,1,0:T(8,128)(2,1)}) custom-call(f32[8,3,64,1024]{3,2,1,0:T(8,128)} %refs_3_.5), custom_call_target="tpu_custom_call" | custom-call | flops 1000 | bytes 1000 | tf_op jit(solution)/shard_map/round_units/pallas_call | solution.py:313
  32.4 12.1 %collective-permute-done.2 = bf16[72,1536]{1,0:T(8,128)(2,1)S(1)} collective-permute-done((bf16[72,1536]{1,0:T(8,128)(2,1)S(1)}, bf16[72,1536]{1,0:T(8,128)(2,1)S(1)}, u32[]{:S(2)}, u32[]{:S(2)}) %collective-permute-start.2) | collective-permute-done | bytes 221216 | tf_op jit(solution)/shard_map/ppermute | solution.py:61
  52.7 11.3 %collective-permute-done.9.refs_6_.refs_3_ = bf16[288,1024]{1,0:T(8,128)(2,1)} collective-permute-done((bf16[288,1024]{1,0:T(8,128)(2,1)S(1)}, bf16[288,1024]{1,0:T(8,128)(2,1)}, u32[]{:S(2)}, u32[]{:S(2)}) %collective-permute-start.9) | collective-permute-done | bytes 589856 | tf_op jit(solution)/shard_map/ppermute | solution.py:61
  64.0 11.4 %collective-permute-done.8.refs_5_.refs_2_ = bf16[288,1024]{1,0:T(8,128)(2,1)S(1)} collective-permute-done((bf16[288,1024]{1,0:T(8,128)(2,1)S(1)}, bf16[288,1024]{1,0:T(8,128)(2,1)S(1)}, u32[]{:S(2)}, u32[]{:S(2)}) %collective-permute-start.8) | collective-permute-done | bytes 589856 | tf_op jit(solution)/shard_map/ppermute | solution.py:61
  93.7 23.0 %attention_forward.1 = (bf16[1024,1024]{1,0:T(8,128)(2,1)}, bf16[1024,512]{1,0:T(8,128)(2,1)}, bf16[1024,512]{1,0:T(8,128)(2,1)}, bf16[1024,512]{1,0:T(8,128)(2,...) custom-call(s32[1]{0:T(128)} %copy.100.refs_0_, s32[4,4]{1,0:T(4,128)S(1)} %xor_multiply_fusion.refs_1_.refs_0_, ...), custom_call_target="tpu_custom_call" | custom-call | flops 1000 | bytes 1000 | tf_op jit(solution)/shard_map/attention_forward/pallas_call | solution.py:221
  134.0 39.5 %collective-permute-done.19.refs_2_ = bf16[512,1024]{1,0:T(8,128)(2,1)} collective-permute-done((bf16[512,1024]{1,0:T(8,128)(2,1)}, bf16[512,1024]{1,0:T(8,128)(2,1)}, u32[]{:S(2)}, u32[]{:S(2)}) %collective-permute-start.19) | collective-permute-done | bytes 1048608 | tf_op jit(solution)/shard_map/ppermute | solution.py:61
  175.2 24.9 %collective-permute-done.17.refs_1_.refs_4_.refs_10_.refs_12_ = bf16[4,3,64,1024]{3,2,1,0:T(8,128)(2,1)} collective-permute-done((bf16[4,3,64,1024]{3,2,1,0:T(8,128)(2,1)}, bf16[4,3,64,1024]{3,2,1,0:T(8,128)(2,1)}, u32[]{:S(2)}, u32[]{:S(2)}) %collective-permute-start.17) | collective-permute-done | bytes 1572896 | tf_op jit(solution)/shard_map/ppermute | solution.py:61
  200.2 5.8 collective-permute-done.21.refs_1_.refs_5_.refs_11_.refs_13_
  218.3 41.1 %expert_first.1 = (bf16[4096,1024]{1,0:T(8,128)(2,1)}, bf16[4096,1024]{1,0:T(8,128)(2,1)}, bf16[4096,1024]{1,0:T(8,128)(2,1)}, bf16[4096,1024]{1,0:T(8,128)(2,1)}, bf16[4096,1024]{1,0:T(8,128)(2,1)}) custom-call(bf16[512,1024]{1,0:T(8,128)(2,1)} %multiply_convert_fusion.refs_0_, bf16[512,1024]{1,0:T(8,128)(2,1)} %after.14.refs_1_, ...), custom_call_target="tpu_custom_call" | custom-call | flops 25769803776 | bytes 1000 | tf_op jit(solution)/shard_map/expert_first/pallas_call | solution.py:564
  260.5 44.9 %expert_second.1 = (bf16[512,1024]{1,0:T(8,128)(2,1)}, bf16[512,1024]{1,0:T(8,128)(2,1)}, bf16[512,1024]{1,0:T(8,128)(2,1)}, bf16[512,1024]{1,0:T(8,128)(2,1)}, ...) custom-call(bf16[4096,1024]{1,0:T(8,128)(2,1)} %get-tuple-element.99, ...), custom_call_target="tpu_custom_call" | custom-call | flops 1000 | bytes 1000 | tf_op jit(solution)/shard_map/expert_second/pallas_call | solution.py:564
  327.0 8.3 %collective-permute-done.26 = bf16[512,1024]{1,0:T(8,128)(2,1)S(1)} collective-permute-done((bf16[512,1024]{1,0:T(8,128)(2,1)S(1)}, bf16[512,1024]{1,0:T(8,128)(2,1)S(1)}, u32[]{:S(2)}, u32[]{:S(2)}) %collective-permute-start.26) | collective-permute-done | bytes 1048608 | tf_op jit(solution)/shard_map/ppermute | solution.py:61
  338.3 21.2 %collective-permute-done.30 = bf16[512,1024]{1,0:T(8,128)(2,1)S(1)} collective-permute-done((bf16[512,1024]{1,0:T(8,128)(2,1)S(1)}, bf16[512,1024]{1,0:T(8,128)(2,1)S(1)}, u32[]{:S(2)}, u32[]{:S(2)}) %collective-permute-start.30) | collective-permute-done | bytes 1048608 | tf_op jit(solution)/shard_map/ppermute | solution.py:61
  367.0 26.4 %expert_backward.2 = (bf16[512,1024]{1,0:T(8,128)(2,1)}, bf16[512,1024]{1,0:T(8,128)(2,1)}, bf16[4096,1024]{1,0:T(8,128)(2,1)}, bf16[4096,1024]{1,0:T(8,128)(2,1...) custom-call(bf16[512,1024]{1,0:T(8,128)(2,1)} %multiply_convert_fusion.1.refs_0_, ...), custom_call_target="tpu_custom_call" | custom-call | flops 1000 | bytes 1000 | tf_op jit(solution)/shard_map/expert_backward/pallas_call | solution.py:564
  393.5 19.5 %collective-permute-done.35.refs_0_ = bf16[512,1024]{1,0:T(8,128)(2,1)} collective-permute-done((bf16[512,1024]{1,0:T(8,128)(2,1)}, bf16[512,1024]{1,0:T(8,128)(2,1)}, u32[]{:S(2)}, u32[]{:S(2)}) %collective-permute-start.35) | collective-permute-done | bytes 1048608 | tf_op jit(solution)/shard_map/ppermute | solution.py:61
  415.6 6.8 collective-permute-done.37.refs_3_
  422.4 59.1 %expert_backward.3 = (bf16[512,1024]{1,0:T(8,128)(2,1)}, bf16[512,1024]{1,0:T(8,128)(2,1)}, bf16[512,1024]{1,0:T(8,128)(2,1)}, bf16[512,1024]{1,0:T(8,128)(2,1)}...) custom-call(bf16[512,1024]{1,0:T(8,128)(2,1)} %after.16.refs_0_, ...), custom_call_target="tpu_custom_call", output_to_operand_aliasing={{6}: (15, {}), {7}: (16, {}), {8}: (17, {}), {9}: (18, {}),... | custom-call | flops 1000 | bytes 1000 | tf_op jit(solution)/shard_map/expert_backward/pallas_call | solution.py:564
  482.2 15.4 %weight_grads.5 = (bf16[512,1024]{1,0:T(8,128)(2,1)}, bf16[512,1024]{1,0:T(8,128)(2,1)}) custom-call(bf16[4096,1024]{1,0:T(8,128)(2,1)} %get-tuple-element.133.refs_0_, bf16[4096,1024]{1,0:T(8,128)(2,1)} %get-tuple-element.134.refs_1_), custom_call_target="tpu_custom_call" | custom-call | flops 30000001024 | bytes 1000 | tf_op jit(solution)/shard_map/weight_grads/pallas_call | solution.py:666
  508.1 15.1 %weight_grads.6 = (bf16[512,1024]{1,0:T(8,128)(2,1)}, bf16[512,1024]{1,0:T(8,128)(2,1)}) custom-call(bf16[4096,1024]{1,0:T(8,128)(2,1)} %get-tuple-element.132.refs_0_, bf16[4096,1024]{1,0:T(8,128)(2,1)} %get-tuple-element.99.refs_0_.refs_1_.refs_2_, bf16[512,1024]{1,0:T(8,128)(2,1)} %get-tuple-element.135.refs_2_, ...), custom_call_target="tpu_custom_call" | custom-call | flops 30000001024 | bytes 1000 | tf_op jit(solution)/shard_map/weight_grads/pallas_call | solution.py:666
  530.9 21.4 %collective-permute-done.43 = bf16[512,1024]{1,0:T(8,128)(2,1)} collective-permute-done((bf16[512,1024]{1,0:T(8,128)(2,1)}, bf16[512,1024]{1,0:T(8,128)(2,1)}, u32[]{:S(2)}, u32[]{:S(2)}) %collective-permute-start.43) | collective-permute-done | bytes 1048608 | tf_op jit(solution)/shard_map/ppermute | solution.py:61
  557.7 15.4 %weight_grads.7 = (bf16[512,1024]{1,0:T(8,128)(2,1)}, bf16[512,1024]{1,0:T(8,128)(2,1)}) custom-call(bf16[4096,1024]{1,0:T(8,128)(2,1)} %get-tuple-element.131.refs_0_, bf16[4096,1024]{1,0:T(8,128)(2,1)} %get-tuple-element.99.refs_0_.refs_1_.refs_2_, bf16[512,1024]{1,0:T(8,128)(2,1)} %get-tuple-element.136.refs_2_, bf16[512,1024]{1,0:T(8,128)(2,1)} %add_convert_fusion.2.refs_3_), custom_call_target="tpu_custom_call" | custom-call | flops 30000001024 | bytes 1000 | tf_op jit(solution)/shard_map/weight_grads/pallas_call | solution.py:666
  583.4 18.2 %collective-permute-done.48 = bf16[512,1024]{1,0:T(8,128)(2,1)} collective-permute-done((bf16[512,1024]{1,0:T(8,128)(2,1)}, bf16[512,1024]{1,0:T(8,128)(2,1)}, u32[]{:S(2)}, u32[]{:S(2)}) %collective-permute-start.48) | collective-permute-done | bytes 1048608 | tf_op jit(solution)/shard_map/ppermute | solution.py:61
  607.5 26.8 %attention_backward.1 = (bf16[1024,512]{1,0:T(8,128)(2,1)S(1)}, bf16[1024,512]{1,0:T(8,128)(2,1)S(1)}) custom-call(s32[1]{0:T(128)} %copy.100.refs_0_, bf16[1024,1024]{1,0:T(8,128)(2,1)} %pad_maximum_fusion.3.refs_1_, bf16[1024,512]{1,0:T(8,128)(2,1)} %copy-done.15, bf16[1024,1024]{1,0:T(8,128)(2,1)} %get-tuple-element.127.refs_3_, ...), custom_call_target="tpu_custom_call" | custom-call | flops 1000 | bytes 1000 | tf_op jit(solution)/shard_map/attention_backward/pallas_call | solution.py:333
  647.1 32.8 %collective-permute-done.49.refs_4_.refs_2_ = bf16[512,1024]{1,0:T(8,128)(2,1)} collective-permute-done((bf16[512,1024]{1,0:T(8,128)(2,1)}, bf16[512,1024]{1,0:T(8,128)(2,1)}, u32[]{:S(2)}, u32[]{:S(2)}) %collective-permute-start.49) | collective-permute-done | bytes 1048608 | tf_op jit(solution)/shard_map/ppermute | solution.py:61
  679.9 15.3 %weight_grads.8 = (bf16[512,1024]{1,0:T(8,128)(2,1)}, bf16[512,1024]{1,0:T(8,128)(2,1)}) custom-call(bf16[4096,1024]{1,0:T(8,128)(2,1)} %get-tuple-element.145.refs_0_, bf16[4096,1024]{1,0:T(8,128)(2,1)} %get-tuple-element.134.refs_1_, bf16[1024,1024]{1,0:T(8,128)(2,1)} %convolution_convert_fusion.refs_2_, bf16[512,1024]{1,0:T(8,128)(2,1)} %add_convert_fusion.refs_3_, ...), custom_call_target="tpu_custom_call" | custom-call | flops 30000001024 | bytes 1000 | tf_op jit(solution)/shard_map/weight_grads/pallas_call | solution.py:666
  695.2 26.4 %weight_grads.9 = (bf16[512,1024]{1,0:T(8,128)(2,1)}, bf16[512,1024]{1,0:T(8,128)(2,1)}, bf16[512,1024]{1,0:T(8,128)(2,1)}, bf16[512,1024]{1,0:T(8,128)(2,1)}) custom-call(bf16[4096,1024]{1,0:T(8,128)(2,1)} %get-tuple-element.143.refs_0_, bf16[4096,1024]{1,0:T(8,128)(2,1)} %get-tuple-element.144.refs_1_, ...), custom_call_target="tpu_custom_call" | custom-call | flops 30000001024 | bytes 1000 | tf_op jit(solution)/shard_map/weight_grads/pallas_call | solution.py:666
  731.4 13.2 %expert_update.3 = (f32[8,3,64,1024]{3,2,1,0:T(8,128)}, f32[8,3,4,64,64]{4,3,2,1,0:T(8,128)}, f32[8,3,4,256,256]{4,3,2,1,0:T(8,128)}, f32[8,3,64,1024]{3,2,1,0:T(8,128)}) custom-call(bf16[512,1024]{1,0:T(8,128)(2,1)} %get-tuple-element.150.refs_0_, bf16[512,1024]{1,0:T(8,128)(2,1)} %copy-done.41, bf16[512,1024]{1,0:T(8,128)(2,1)} %collective-permute-done.49.refs_4_.refs_2_, ...), custom_call_target="tpu_custom_call" | custom-call | flops 12000000000 | bytes 1000 | tf_op jit(solution)/shard_map/expert_update/pallas_call | solution.py:740
  744.6 14.4 %collective-permute-done.50.refs_1_ = bf16[512,1024]{1,0:T(8,128)(2,1)S(1)} collective-permute-done((bf16[512,1024]{1,0:T(8,128)(2,1)}, bf16[512,1024]{1,0:T(8,128)(2,1)S(1)}, u32[]{:S(2)}, u32[]{:S(2)}) %collective-permute-start.50) | collective-permute-done | bytes 1048608 | tf_op jit(solution)/shard_map/ppermute | solution.py:61
  760.0 13.2 %expert_update.4 = (f32[8,3,64,1024]{3,2,1,0:T(8,128)}, f32[8,3,4,64,64]{4,3,2,1,0:T(8,128)}, f32[8,3,4,256,256]{4,3,2,1,0:T(8,128)}, f32[8,3,64,1024]{3,2,1,0:T(8,128)}) custom-call(bf16[512,1024]{1,0:T(8,128)(2,1)} %get-tuple-element.148.refs_0_, ...), custom_call_target="tpu_custom_call", output_to_operand_aliasing={{0}: (9, {}), {1}: (10, {}), {2}: (11, {}), {3}: (12, {})} | custom-call | flops 12000000000 | bytes 1000 | tf_op jit(solution)/shard_map/expert_update/pallas_call | solution.py:740
  787.9 3.9 collective-permute-start.59
  798.3 14.0 %expert_update.5 = (f32[8,3,64,1024]{3,2,1,0:T(8,128)}, f32[8,3,4,64,64]{4,3,2,1,0:T(8,128)}, f32[8,3,4,256,256]{4,3,2,1,0:T(8,128)}, f32[8,3,64,1024]{3,2,1,0:T(8,128)}) custom-call(bf16[512,1024]{1,0:T(8,128)(2,1)} %get-tuple-element.160.refs_0_, ...), custom_call_target="tpu_custom_call", output_to_operand_aliasing={{0}: (9, {}), {1}: (10, {}), {2}: (11, {}), {3}: (12, {})} | custom-call | flops 12000000000 | bytes 1000 | tf_op jit(solution)/shard_map/expert_update/pallas_call | solution.py:740
  (379 shorter events, 183.9 us)
Async XLA Ops:
  7.2 805.0 %reduce-scatter.5.cloned.1.call-start = ((), (), s32[]{:S(2)}) async-start(), calls=%async_computation.3 | async-start | bytes 1114112 | tf_op jit(solution)/shard_map/reduce_scatter | solution.py:1067
  8.9 35.7 %collective-permute-start.6 = (f32[16,1024]{1,0:T(8,128)S(1)}, f32[16,1024]{1,0:T(8,128)S(1)}, u32[]{:S(2)}, u32[]{:S(2)}) collective-permute-start(f32[16,1024]{1,0:T(8,128)S(1)} %pad_maximum_fusion.8), channel_id=1, source_target_pairs={{0,10},{2,8},{4,14},{6,12},{8,2},{10,0},{12,6},{14,4},{16,26},{18,... | collective-permute-start | bytes 196616 | tf_op jit(solution)/shard_map/ppermute | solution.py:61
  12.8 31.8 %collective-permute-start.5 = (f32[16,1024]{1,0:T(8,128)S(1)}, f32[16,1024]{1,0:T(8,128)S(1)}, u32[]{:S(2)}, u32[]{:S(2)}) collective-permute-start(f32[16,1024]{1,0:T(8,128)S(1)} %pad_maximum_fusion.8), channel_id=1, source_target_pairs={{0,8},{2,10},{4,12},{6,14},{8,0},{10,2},{12,4},{14,6},{16,24},{18,... | collective-permute-start | bytes 196616 | tf_op jit(solution)/shard_map/ppermute | solution.py:61
  13.3 31.4 %collective-permute-start.4 = (f32[16,1024]{1,0:T(8,128)S(1)}, f32[16,1024]{1,0:T(8,128)S(1)}, u32[]{:S(2)}, u32[]{:S(2)}) collective-permute-start(f32[16,1024]{1,0:T(8,128)S(1)} %pad_maximum_fusion.8), channel_id=1, source_target_pairs={{0,2},{2,0},{4,6},{6,4},{8,10},{10,8},{12,14},{14,12},{16,18},{18,... | collective-permute-start | bytes 196616 | tf_op jit(solution)/shard_map/ppermute | solution.py:61
  50.2 67.2 %collective-permute-start.13 = (bf16[4,3,64,1024]{3,2,1,0:T(8,128)(2,1)}, bf16[4,3,64,1024]{3,2,1,0:T(8,128)(2,1)S(1)}, u32[]{:S(2)}, u32[]{:S(2)}) collective-permute-start(bf16[4,3,64,1024]{3,2,1,0:T(8,128)(2,1)} %after.11), channel_id=1, source_target_pairs={{0,16},{2,18},{4,20},{6,22},{8,24},{10,26},{12,28},{14,30},{16,0},... | collective-permute-start | bytes 4718600 | tf_op jit(solution)/shard_map/ppermute | solution.py:61
  52.7 34.8 %collective-permute-start = (bf16[512,1024]{1,0:T(8,128)(2,1)}, bf16[512,1024]{1,0:T(8,128)(2,1)}, u32[]{:S(2)}, u32[]{:S(2)}) collective-permute-start(bf16[512,1024]{1,0:T(8,128)(2,1)} %fusion.3), channel_id=1, source_target_pairs={{0,1},{1,0},{2,3},{3,2},{4,5},{5,4},{6,7},{7,6},{8,9},{9,8},{10,11... | collective-permute-start | bytes 3145736 | tf_op jit(solution)/shard_map/ppermute | solution.py:66
  76.4 41.0 %collective-permute-start.14 = (bf16[3,3,64,1024]{3,2,1,0:T(8,128)(2,1)}, bf16[3,3,64,1024]{3,2,1,0:T(8,128)(2,1)S(1)}, u32[]{:S(2)}, u32[]{:S(2)}) collective-permute-start(bf16[3,3,64,1024]{3,2,1,0:T(8,128)(2,1)} %after.12), channel_id=1, source_target_pairs={{0,4},{2,6},{4,0},{6,2},{8,12},{10,14},{12,8},{14,10},{16,20},{18,... | collective-permute-start | bytes 3538952 | tf_op jit(solution)/shard_map/ppermute | solution.py:61
  84.7 32.0 %collective-permute-start.12 = (bf16[288,512]{1,0:T(8,128)(2,1)S(1)}, bf16[288,512]{1,0:T(8,128)(2,1)S(1)}, u32[]{:S(2)}, u32[]{:S(2)}) collective-permute-start(bf16[288,512]{1,0:T(8,128)(2,1)S(1)} %slice.107.refs_3_), channel_id=1, source_target_pairs={{0,6},{2,4},{4,2},{6,0},{8,14},{10,12},{12,10},{14,8},{16,22},{18,... | collective-permute-start | bytes 884744 | tf_op jit(solution)/shard_map/ppermute | solution.py:61
  86.2 30.9 %collective-permute-start.11 = (bf16[288,512]{1,0:T(8,128)(2,1)S(1)}, bf16[288,512]{1,0:T(8,128)(2,1)S(1)}, u32[]{:S(2)}, u32[]{:S(2)}) collective-permute-start(bf16[288,512]{1,0:T(8,128)(2,1)S(1)} %slice.107.refs_3_), channel_id=1, source_target_pairs={{0,4},{2,6},{4,0},{6,2},{8,12},{10,14},{12,8},{14,10},{16,20},{18,... | collective-permute-start | bytes 884744 | tf_op jit(solution)/shard_map/ppermute | solution.py:61
  87.5 29.7 %collective-permute-start.10 = (bf16[288,512]{1,0:T(8,128)(2,1)S(1)}, bf16[288,512]{1,0:T(8,128)(2,1)S(1)}, u32[]{:S(2)}, u32[]{:S(2)}) collective-permute-start(bf16[288,512]{1,0:T(8,128)(2,1)S(1)} %slice.107.refs_3_), channel_id=1, source_target_pairs={{0,2},{2,0},{4,6},{6,4},{8,10},{10,8},{12,14},{14,12},{16,18},{18,... | collective-permute-start | bytes 884744 | tf_op jit(solution)/shard_map/ppermute | solution.py:61
  127.1 46.4 %collective-permute-start.19 = (bf16[512,1024]{1,0:T(8,128)(2,1)}, bf16[512,1024]{1,0:T(8,128)(2,1)}, u32[]{:S(2)}, u32[]{:S(2)}) collective-permute-start(bf16[512,1024]{1,0:T(8,128)(2,1)} %multiply_convert_fusion.refs_0_), channel_id=1, source_target_pairs={{0,8},{2,10},{4,12},{6,14},{8,0},{10,2},{12,4},{14,6},{16,24},{18,... | collective-permute-start | bytes 3145736 | tf_op jit(solution)/shard_map/ppermute | solution.py:61
  127.1 73.1 %collective-permute-start.18 = (bf16[5,3,64,1024]{3,2,1,0:T(8,128)(2,1)}, bf16[5,3,64,1024]{3,2,1,0:T(8,128)(2,1)}, u32[]{:S(2)}, u32[]{:S(2)}) collective-permute-start(bf16[5,3,64,1024]{3,2,1,0:T(8,128)(2,1)} %get-tuple-element.98), channel_id=1, source_target_pairs={{0,4},{2,6},{4,0},{6,2},{8,12},{10,14},{12,8},{14,10},{16,20},{18,... | collective-permute-start | bytes 5898248 | tf_op jit(solution)/shard_map/ppermute | solution.py:61
  128.8 71.4 %collective-permute-start.17 = (bf16[4,3,64,1024]{3,2,1,0:T(8,128)(2,1)}, bf16[4,3,64,1024]{3,2,1,0:T(8,128)(2,1)}, u32[]{:S(2)}, u32[]{:S(2)}) collective-permute-start(bf16[4,3,64,1024]{3,2,1,0:T(8,128)(2,1)} %after.13), channel_id=1, source_target_pairs={{0,16},{2,18},{4,20},{6,22},{8,24},{10,26},{12,28},{14,30},{16,0},... | collective-permute-start | bytes 4718600 | tf_op jit(solution)/shard_map/ppermute | solution.py:61
  132.0 74.0 %collective-permute-start.21 = (bf16[4,3,64,1024]{3,2,1,0:T(8,128)(2,1)S(1)}, bf16[4,3,64,1024]{3,2,1,0:T(8,128)(2,1)}, u32[]{:S(2)}, u32[]{:S(2)}) collective-permute-start(bf16[4,3,64,1024]{3,2,1,0:T(8,128)(2,1)S(1)} %collective-permute-done.13.refs_7_.refs_3_.refs_9_.refs_11_), channel_id=1, source_target_pairs={{0,4},{2,6},{4,0},{6,2},{8,12},{10,14},{12,8},{14,10},{16,20},{18,... | collective-permute-start | bytes 4718600 | tf_op jit(solution)/shard_map/ppermute | solution.py:61
  132.4 67.8 %collective-permute-start.16 = (bf16[512,1024]{1,0:T(8,128)(2,1)}, bf16[512,1024]{1,0:T(8,128)(2,1)}, u32[]{:S(2)}, u32[]{:S(2)}) collective-permute-start(bf16[512,1024]{1,0:T(8,128)(2,1)} %multiply_convert_fusion.refs_0_), channel_id=1, source_target_pairs={{0,2},{2,0},{4,6},{6,4},{8,10},{10,8},{12,14},{14,12},{16,18},{18,... | collective-permute-start | bytes 3145736 | tf_op jit(solution)/shard_map/ppermute | solution.py:61
  173.5 32.5 %collective-permute-start.20 = (bf16[512,1024]{1,0:T(8,128)(2,1)}, bf16[512,1024]{1,0:T(8,128)(2,1)S(1)}, u32[]{:S(2)}, u32[]{:S(2)}) collective-permute-start(bf16[512,1024]{1,0:T(8,128)(2,1)} %collective-permute-done.19.refs_2_), channel_id=1, source_target_pairs={{0,2},{2,0},{4,6},{6,4},{8,10},{10,8},{12,14},{14,12},{16,18},{18,... | collective-permute-start | bytes 3145736 | tf_op jit(solution)/shard_map/ppermute | solution.py:61
  214.1 45.3 %collective-permute-start.23 = (bf16[4,3,64,1024]{3,2,1,0:T(8,128)(2,1)}, bf16[4,3,64,1024]{3,2,1,0:T(8,128)(2,1)S(1)}, u32[]{:S(2)}, u32[]{:S(2)}) collective-permute-start(bf16[4,3,64,1024]{3,2,1,0:T(8,128)(2,1)} %collective-permute-done.17.refs_1_.refs_4_.refs_10_.refs_12_), channel_id=1, source_target_pairs={{0,4},{2,6},{4,0},{6,2},{8,12},{10,14},{12,8},{14,10},{16,20},{18,... | collective-permute-start | bytes 4718600 | tf_op jit(solution)/shard_map/ppermute | solution.py:61
  314.4 45.1 %collective-permute-start.30 = (bf16[512,1024]{1,0:T(8,128)(2,1)S(1)}, bf16[512,1024]{1,0:T(8,128)(2,1)S(1)}, u32[]{:S(2)}, u32[]{:S(2)}) collective-permute-start(bf16[512,1024]{1,0:T(8,128)(2,1)S(1)} %add_convert_fusion.6), channel_id=1, source_target_pairs={{0,10},{2,8},{4,14},{6,12},{8,2},{10,0},{12,6},{14,4},{16,26},{18,... | collective-permute-start | bytes 3145736 | tf_op jit(solution)/shard_map/ppermute | solution.py:61
  363.5 29.9 %collective-permute-start.36 = (bf16[512,1024]{1,0:T(8,128)(2,1)}, bf16[512,1024]{1,0:T(8,128)(2,1)}, u32[]{:S(2)}, u32[]{:S(2)}) collective-permute-start(bf16[512,1024]{1,0:T(8,128)(2,1)} %multiply_convert_fusion.1.refs_0_), channel_id=1, source_target_pairs={{0,10},{2,8},{4,14},{6,12},{8,2},{10,0},{12,6},{14,4},{16,26},{18,... | collective-permute-start | bytes 3145736 | tf_op jit(solution)/shard_map/ppermute | solution.py:61
  366.3 46.7 %collective-permute-start.35 = (bf16[512,1024]{1,0:T(8,128)(2,1)}, bf16[512,1024]{1,0:T(8,128)(2,1)}, u32[]{:S(2)}, u32[]{:S(2)}) collective-permute-start(bf16[512,1024]{1,0:T(8,128)(2,1)} %multiply_convert_fusion.1.refs_0_), channel_id=1, source_target_pairs={{0,8},{2,10},{4,12},{6,14},{8,0},{10,2},{12,4},{14,6},{16,24},{18,... | collective-permute-start | bytes 3145736 | tf_op jit(solution)/shard_map/ppermute | solution.py:61
  366.6 46.4 %collective-permute-start.34 = (bf16[512,1024]{1,0:T(8,128)(2,1)}, bf16[512,1024]{1,0:T(8,128)(2,1)}, u32[]{:S(2)}, u32[]{:S(2)}) collective-permute-start(bf16[512,1024]{1,0:T(8,128)(2,1)} %multiply_convert_fusion.1.refs_0_), channel_id=1, source_target_pairs={{0,2},{2,0},{4,6},{6,4},{8,10},{10,8},{12,14},{14,12},{16,18},{18,... | collective-permute-start | bytes 3145736 | tf_op jit(solution)/shard_map/ppermute | solution.py:61
  415.1 111.1 %collective-permute-start.33 = (bf16[512,1024]{1,0:T(8,128)(2,1)}, bf16[512,1024]{1,0:T(8,128)(2,1)}, u32[]{:S(2)}, u32[]{:S(2)}) collective-permute-start(bf16[512,1024]{1,0:T(8,128)(2,1)} %get-tuple-element.114), channel_id=1, source_target_pairs={{0,1},{1,0},{2,3},{3,2},{4,5},{5,4},{6,7},{7,6},{8,9},{9,8},{10,11... | collective-permute-start | bytes 3145736 | tf_op jit(solution)/shard_map/ppermute | solution.py:66
  507.7 44.6 %collective-permute-start.43 = (bf16[512,1024]{1,0:T(8,128)(2,1)}, bf16[512,1024]{1,0:T(8,128)(2,1)}, u32[]{:S(2)}, u32[]{:S(2)}) collective-permute-start(bf16[512,1024]{1,0:T(8,128)(2,1)} %add_convert_fusion.3.refs_5_), channel_id=1, source_target_pairs={{0,10},{2,8},{4,14},{6,12},{8,2},{10,0},{12,6},{14,4},{16,26},{18,... | collective-permute-start | bytes 3145736 | tf_op jit(solution)/shard_map/ppermute | solution.py:61
  523.3 57.1 %collective-permute-start.46 = (bf16[512,1024]{1,0:T(8,128)(2,1)}, bf16[512,1024]{1,0:T(8,128)(2,1)}, u32[]{:S(2)}, u32[]{:S(2)}) collective-permute-start(bf16[512,1024]{1,0:T(8,128)(2,1)} %get-tuple-element.136.refs_2_), channel_id=1, source_target_pairs={{0,4},{2,6},{4,0},{6,2},{8,12},{10,14},{12,8},{14,10},{16,20},{18,... | collective-permute-start | bytes 3145736 | tf_op jit(solution)/shard_map/ppermute | solution.py:61
  576.6 235.6 %reduce-scatter.3.cloned.1.call-start = ((), (), s32[]{:S(2)}) async-start(), calls=%async_computation.2 | async-start | bytes 2228224 | tf_op jit(solution)/shard_map/reduce_scatter | solution.py:1066
  577.5 102.4 %collective-permute-start.49 = (bf16[512,1024]{1,0:T(8,128)(2,1)}, bf16[512,1024]{1,0:T(8,128)(2,1)}, u32[]{:S(2)}, u32[]{:S(2)}) collective-permute-start(bf16[512,1024]{1,0:T(8,128)(2,1)} %add_convert_fusion.2.refs_3_), channel_id=1, source_target_pairs={{0,16},{2,18},{4,20},{6,22},{8,24},{10,26},{12,28},{14,30},{16,0},... | collective-permute-start | bytes 3145736 | tf_op jit(solution)/shard_map/ppermute | solution.py:61
  583.4 147.0 %collective-permute-start.51 = (bf16[512,1024]{1,0:T(8,128)(2,1)}, bf16[512,1024]{1,0:T(8,128)(2,1)}, u32[]{:S(2)}, u32[]{:S(2)}) collective-permute-start(bf16[512,1024]{1,0:T(8,128)(2,1)} %add_convert_fusion.1.refs_10_), channel_id=1, source_target_pairs={{0,16},{2,18},{4,20},{6,22},{8,24},{10,26},{12,28},{14,30},{16,0},... | collective-permute-start | bytes 3145736 | tf_op jit(solution)/shard_map/ppermute | solution.py:61
  604.3 140.4 %collective-permute-start.52 = (bf16[512,1024]{1,0:T(8,128)(2,1)}, bf16[512,1024]{1,0:T(8,128)(2,1)}, u32[]{:S(2)}, u32[]{:S(2)}) collective-permute-start(bf16[512,1024]{1,0:T(8,128)(2,1)} %add_convert_fusion.refs_3_), channel_id=1, source_target_pairs={{0,16},{2,18},{4,20},{6,22},{8,24},{10,26},{12,28},{14,30},{16,0},... | collective-permute-start | bytes 3145736 | tf_op jit(solution)/shard_map/ppermute | solution.py:61
  643.2 80.5 %collective-permute-start.47 = (bf16[512,1024]{1,0:T(8,128)(2,1)}, bf16[512,1024]{1,0:T(8,128)(2,1)S(1)}, u32[]{:S(2)}, u32[]{:S(2)}) collective-permute-start(bf16[512,1024]{1,0:T(8,128)(2,1)} %convolution_convert_fusion.2), channel_id=1, source_target_pairs={{0,1},{1,0},{2,3},{3,2},{4,5},{5,4},{6,7},{7,6},{8,9},{9,8},{10,11... | collective-permute-start | bytes 3145736 | tf_op jit(solution)/shard_map/ppermute | solution.py:66
  695.2 35.3 %collective-permute-start.53 = (bf16[512,1024]{1,0:T(8,128)(2,1)}, bf16[512,1024]{1,0:T(8,128)(2,1)S(1)}, u32[]{:S(2)}, u32[]{:S(2)}) collective-permute-start(bf16[512,1024]{1,0:T(8,128)(2,1)} %get-tuple-element.147.refs_3_), channel_id=1, source_target_pairs={{0,4},{2,6},{4,0},{6,2},{8,12},{10,14},{12,8},{14,10},{16,20},{18,... | collective-permute-start | bytes 3145736 | tf_op jit(solution)/shard_map/ppermute | solution.py:61
  721.6 37.4 %collective-permute-start.50 = (bf16[512,1024]{1,0:T(8,128)(2,1)}, bf16[512,1024]{1,0:T(8,128)(2,1)S(1)}, u32[]{:S(2)}, u32[]{:S(2)}) collective-permute-start(bf16[512,1024]{1,0:T(8,128)(2,1)} %get-tuple-element.149), channel_id=1, source_target_pairs={{0,4},{2,6},{4,0},{6,2},{8,12},{10,14},{12,8},{14,10},{16,20},{18,... | collective-permute-start | bytes 3145736 | tf_op jit(solution)/shard_map/ppermute | solution.py:61
  724.7 72.6 %collective-permute-start.61 = (bf16[512,1024]{1,0:T(8,128)(2,1)}, bf16[512,1024]{1,0:T(8,128)(2,1)S(1)}, u32[]{:S(2)}, u32[]{:S(2)}) collective-permute-start(bf16[512,1024]{1,0:T(8,128)(2,1)} %get-tuple-element.161), channel_id=1, source_target_pairs={{0,4},{2,6},{4,0},{6,2},{8,12},{10,14},{12,8},{14,10},{16,20},{18,... | collective-permute-start | bytes 3145736 | tf_op jit(solution)/shard_map/ppermute | solution.py:61
  (109 other events, 1429.2 us)
Sparse Core Ops, SparseCore 0:
  576.7 120.8 reduce-scatter.4
  700.0 80.5 reduce-scatter.2

commit v3 on v2

--- a/solution.py
+++ b/solution.py
@@ -385,37 +385,21 @@
     )
 
 
-def fetch(kinds, piece_refs, weights, arrived, row_refs=(None,), rows_all=None, landed=None):
+def fetch(piece_refs, weights, arrived, row_refs=(None,), rows_all=None, landed=None):
     @pl.when(pl.program_id(0) == 0)
     def _():
-        for index in range(2 * len(row_refs) - 2):
-            row_copy(row_refs, rows_all, landed, index).start()
-        for early in kinds:
-            for piece in range(len(piece_refs)):
-                for kind in early:
-                    piece_copy(piece_refs, weights, arrived, piece, kind).start()
-
-
-def await_weights(kinds, piece_refs, weights, arrived, chunk=None):
-    places = range(len(piece_refs))
-    if chunk is not None:
-        per_chunk = CHUNK // UNIT_ROWS
-        places = [p for p in places if first_unit(piece_refs, p) // per_chunk == chunk]
-
-    @pl.when(pl.program_id(0) == 0)
-    def _():
-        for piece in places:
-            for kind in kinds:
-                piece_copy(piece_refs, weights, arrived, piece, kind).wait()
-
-
-def await_rows(row_refs, rows_all, landed):
-    step = pl.program_id(0)
-    for index in range(2 * len(row_refs) - 2):
-
-        @pl.when(step == index)
-        def _(index=index):
-            row_copy(row_refs, rows_all, landed, index).wait()
+        copies = [
+            row_copy(row_refs, rows_all, landed, index) for index in range(2 * len(row_refs) - 2)
+        ]
+        copies += [
+            piece_copy(piece_refs, weights, arrived, piece, kind)
+            for piece in range(len(piece_refs))
+            for kind in range(3)
+        ]
+        for copy in copies:
+            copy.start()
+        for copy in copies:
+            copy.wait()
 
 
 def chunk_weights(weights, kind, chunk):
@@ -444,12 +428,11 @@
             out_ref[...] = values
 
 
-def expert_hidden(x, route_ref, weights, piece_refs, arrived, first_column, per_unit, outs):
+def expert_hidden(x, route_ref, weights, first_column, per_unit, outs):
     low = jnp.bfloat16
     slope_ref, silu_ref, inner_ref = outs
     for chunk in range(slope_ref.shape[1] // CHUNK):
         here = slice(chunk * CHUNK, (chunk + 1) * CHUNK)
-        await_weights((0, 1), piece_refs, weights, arrived, chunk)
         gate = dot(x, chunk_weights(weights, 0, chunk), 1, 1)
         upper = dot(x, chunk_weights(weights, 1, chunk), 1, 1)
         sigmoid = 0.5 * jnp.tanh(0.5 * gate) + 0.5
@@ -459,7 +442,6 @@
         slope_ref[:, here] = (weighted_upper * (sigmoid + silu * (1.0 - sigmoid))).astype(low)
         silu_ref[:, here] = (weight * silu).astype(low)
         inner_ref[:, here] = (silu * weighted_upper).astype(low)
-    await_weights((2,), piece_refs, weights, arrived)
     return dot(inner_ref[...], weights[2].reshape(-1, D), 1, 0)
 
 
@@ -469,14 +451,13 @@
     piece_refs = refs[parts + 1 : parts + 1 + pieces]
     x_ref, mixed_ref, slope_ref, silu_ref, inner_ref = refs[-9:-4]
     weights, arrived, rows_all, landed = refs[-4:]
-    fetch(((0, 1), (2,)), piece_refs, weights, arrived, row_refs, rows_all, landed)
-    await_rows(row_refs, rows_all, landed)
+    fetch(piece_refs, weights, arrived, row_refs, rows_all, landed)
     rows = x_ref.shape[0]
     x = rows_all[pl.ds(pl.multiple_of(pl.program_id(0) * rows, rows), rows), :]
     x_ref[...] = x
     outs = (slope_ref, silu_ref, inner_ref)
     mixed_ref[...] = expert_hidden(
-        x, route_ref, weights, piece_refs, arrived, 0, per_unit, outs
+        x, route_ref, weights, 0, per_unit, outs
     ).astype(jnp.bfloat16)
 
 
@@ -485,9 +466,9 @@
     piece_refs = refs[3 : 3 + pieces]
     out_refs = refs[-5 - count : -5]
     weights, arrived = refs[-2:]
-    fetch(((0, 1), (2,)), piece_refs, weights, arrived)
+    fetch(piece_refs, weights, arrived)
     part = expert_hidden(
-        x_ref[...], route_ref, weights, piece_refs, arrived, first_column, per_unit, refs[-5:-2]
+        x_ref[...], route_ref, weights, first_column, per_unit, refs[-5:-2]
     )
     store_step(out_refs, (part + mixed_ref[...].astype(jnp.float32)).astype(jnp.bfloat16))
 
@@ -502,8 +483,7 @@
     gate_refs, upper_refs = refs[-8:-6], refs[-6:-4]
     weights, arrived, rows_all, landed = refs[-4:]
     low = jnp.bfloat16
-    fetch(((2,), (0,), (1,)), piece_refs, weights, arrived, row_refs, rows_all, landed)
-    await_rows(row_refs, rows_all, landed)
+    fetch(piece_refs, weights, arrived, row_refs, rows_all, landed)
     rows = grad_ref.shape[0]
     grad = rows_all[pl.ds(pl.multiple_of(pl.program_id(0) * rows, rows), rows), :]
     grad_ref[...] = grad
@@ -511,13 +491,11 @@
     for chunk in range(2 * chunks):
         half, place = chunk // chunks, chunk % chunks
         here = slice(place * CHUNK, (place + 1) * CHUNK)
-        await_weights((2,), piece_refs, weights, arrived, chunk)
         inner_grad = dot(grad, chunk_weights(weights, 2, chunk), 1, 1)
         slope, silu = slope_refs[half][:, here], silu_refs[half][:, here]
         gate_refs[half][:, here] = (inner_grad * slope.astype(jnp.float32)).astype(low)
         upper_refs[half][:, here] = (inner_grad * silu.astype(jnp.float32)).astype(low)
     units = weights.shape[1] // 2
-    await_weights((0, 1), piece_refs, weights, arrived)
     total = None
     for half in range(2):
         mine = pl.ds(half * units, units)
@@ -819,10 +797,13 @@
 
 
 def return_tokens(sums):
-    total = sums[0]
-    for rows, mask in zip(sums[1:], TOKEN_MASKS[1:]):
-        total = total + swap_dp(rows, mask).astype(jnp.float32)
-    return total
+    return [swap_dp(rows, mask) for rows, mask in zip(sums[1:], TOKEN_MASKS[1:])]
+
+
+def add_all(first, others):
+    for rows in others:
+        first = first + rows.astype(jnp.float32)
+    return first
 
 
 def extra_masks():
@@ -844,8 +825,11 @@
     digits = jnp.pad(digits[None, :], ((0, 7), (0, own.shape[1] - 2)))
     own = jnp.concatenate([own, digits], axis=0)
     slot_rows = own.shape[0]
-    masks = list(range(0, lax.axis_size("dp"), 4))
-    line = jnp.concatenate([own] + [swap_dp(own, mask) for mask in masks[1:]], axis=0)
+    masks, line, mask = [0], own, lax.axis_size("dp") // 2
+    while mask > 2:
+        line = jnp.concatenate([line, swap_dp(line, mask)], axis=0)
+        masks = masks + [m ^ mask for m in masks]
+        mask //= 2
     line = after(line, *deps)
     inner, outer = line[:, :qkv_cols], line[:, qkv_cols:]
     inner = [inner] + [swap_dp(inner, mask) for mask in (1, 2, 3)]
@@ -951,21 +935,10 @@
         return jnp.concatenate([query, key, value], axis=2).reshape(rows, qkv_cols)
 
     attention_low = attention_master.astype(low)
-    own_columns = jnp.concatenate([by_head(attention_low), attention_low[:, qkv_cols:]], axis=1)
-    shard, for_far, for_near = round_weights(expert_master)
-    line, w_inner, w_outer, devices, valid_total = gather_attention(
-        own_columns, valid_here, qkv_cols, [shard] + routing_parts[1:]
-    )
-    starts = devices * rows_here
     hidden = activations.astype(jnp.float32)
     normed_own, attention_scaling = normalize(hidden, norm_gains[0])
     normed_own = normed_own.astype(low)
     normed = in_order(normed_own, swap_core(normed_own))
-
-    near_bit, far_bit = WEIGHT_BITS
-    for_near[0] = after(for_near[0], *w_inner[1:])
-    near = [swap_dp(piece, near_bit) for piece in for_near]
-    far = [swap_dp(after(piece, line), far_bit) for piece in for_far]
 
     seq_rows = normed.shape[0]
     half_width = HEAD_DIM // 2
@@ -973,6 +946,20 @@
     angles = jnp.arange(seq_rows, dtype=jnp.float32)[:, None] * frequency[None, :]
     cosine = jnp.tile(jnp.cos(angles), (1, LANES // half_width))
     sine = jnp.tile(jnp.sin(angles), (1, LANES // half_width))
+    own_columns = jnp.concatenate([by_head(attention_low), attention_low[:, qkv_cols:]], axis=1)
+    shard, for_far, for_near = round_weights(expert_master)
+    line, w_inner, w_outer, devices, valid_total = gather_attention(
+        own_columns,
+        valid_here,
+        qkv_cols,
+        [shard, normed, cosine, sine] + routing_parts[1:],
+    )
+    starts = devices * rows_here
+    near_bit, far_bit = WEIGHT_BITS
+    for_near[0] = after(for_near[0], *w_inner[1:])
+    near = [swap_dp(piece, near_bit) for piece in for_near]
+    far = [swap_dp(after(piece, line), far_bit) for piece in for_far]
+
     q2, k2, v_high, attended, w_qkv, log_totals = attention_forward(
         lengths,
         starts,
@@ -1021,7 +1008,7 @@
     )
     slopes, silus, inners = ([firsts[i], seconds[i]] for i in range(3))
     sums = [sum_cores(i, mixed_parts[2 * i : 2 * i + 2]) for i in range(len(TOKEN_MASKS))]
-    output = middle + return_tokens(sums)
+    output = middle + add_all(sums[0], return_tokens(sums))
     residual_error = output - targets
     loss_part = jnp.sum(valid_rows[:, None] * residual_error * residual_error)
     output_grad = 2.0 / valid_total * valid_rows[:, None] * residual_error
@@ -1033,7 +1020,7 @@
     parts1, kept = backward(2, with_other(later), kept=kept)
     parts = list(parts0) + list(parts1)
     sums = [sum_cores(i, parts[2 * i : 2 * i + 2]) for i in range(len(TOKEN_MASKS))]
-    sent = return_tokens(sums)
+    returned = return_tokens(sums)
     output_low = kept[0]
     gates, uppers = kept[1:3], kept[3:5]
     full = cost(30e9)
@@ -1043,6 +1030,8 @@
     upper_far = weight_grads([uppers[1]], mix, [gate_far[0], down_sum], full)
     gate_sum = add_grads(gate_far[1], gate_far[0])
     upper_sum = add_grads(upper_far[1], upper_far[0])
+    returned[2] = after(returned[2], upper_far[0], gate_sum)
+    sent = add_all(sums[0], returned)
     far_gate, far_upper, far_down = (
         swap_dp(rows, far_bit) for rows in (gate_sum, upper_sum, down_sum)
     )
@@ -1059,9 +1048,9 @@
     ).reshape(seq_rows, qkv_cols)
     qkv_part = dot(normed, qkv_grad, 0, 0).astype(low)
     output_part = dot(branch_low, attended, 0, 0).astype(low)
-    down_near = weight_grads([inners[0]], output_low, [qkv_part, upper_sum, far_down], full)
-    gate_up_near = weight_grads(
-        [gates[0], uppers[0]], mix, [down_near[0], output_part], full
+    gate_up_near = weight_grads([gates[0], uppers[0]], mix, [qkv_part, output_part, upper_sum])
+    down_near = weight_grads(
+        [inners[0]], output_low, [gate_up_near[0], far_down, far_gate]
     )
     qkv_part = lax.psum_scatter(qkv_part, "dp", scatter_dimension=0, tiled=True)
     output_part = lax.psum_scatter(output_part, "dp", scatter_dimension=0, tiled=True)
@@ -1078,17 +1067,13 @@
         1: grad_terms(gate_up_near[3], gate_up_near[2], far_upper),
     }
     state = (expert_master, expert_left, expert_right, expert_left_root, expert_right_root)
-    updated = expert_update(2, parts[2], state, None, [input_grad, far_gate])
-    updated = expert_update(0, parts[0], state, updated, [far_upper])
+    updated = expert_update(0, parts[0], state, None, [input_grad])
+    updated = expert_update(1, parts[1], state, updated)
     loss_row = jnp.full((1, D), loss_part)
     sums = jnp.concatenate([gain_attention[None], gain_mix[None], loss_row], axis=0)
     sums = sum_everywhere(after(sums, updated[0]))
-    updated = expert_update(1, parts[1], state, updated, [sums])
+    updated = expert_update(2, parts[2], state, updated, [sums])
     expert_grad, expert_left_new, expert_right_new, expert_new = updated
-    gain_grad = sums[:2]
-    mean_loss = sums[2, 0] / valid_total
-    gains_new = norm_gains - gain_rate * tokens_total**0.5 * gain_grad
-
     attention_grad, attention_left_new, attention_right_new, attention_new = attention_update(
         qkv_part,
         output_part,
@@ -1100,6 +1085,10 @@
             attention_right_root[0],
         ),
     )
+    gain_grad = sums[:2]
+    mean_loss = sums[2, 0] / valid_total
+    gains_new = norm_gains - gain_rate * tokens_total**0.5 * gain_grad
+
     return (
         output,
         mean_loss,

time: 837 us -> 796 us (0.951)
  waiting for transfers between devices: 272 us -> 245 us
  Pallas kernels: 362 us -> 353 us
    ppermute x45 -> x44, waiting for transfers between devices: 257 us -> 226 us  [swap_dp(): return lax.ppermute(values, 'dp', [(i, i ^ mask) for i in range(count)])]
    pallas_call x4, Pallas kernels: 172 us -> 162 us  [expert_call(): pl.pallas_call(kernel, grid=(steps,), in_specs=specs, out_specs=[fixed((r...]
    unnamed x162 -> x160, local copies, waits for them, and re-layouts: 19.1 us -> 20.1 us
    ppermute x45 -> x44, starting transfers between devices: 60.9 us -> 60.3 us  [swap_dp(): return lax.ppermute(values, 'dp', [(i, i ^ mask) for i in range(count)])]
  transfers between devices with their start and end apart: 64 -> 63, of which waited for: 30 -> 30; matrix products, arithmetic and copies ran while one was open for 8% -> 7% of each run, Pallas kernels for 38% -> 39%
where the time goes in v3:
time: 796 us; the launch traced here: 785 us
  Pallas kernels  353 us (44%)
  waiting for transfers between devices  245 us (31%)
  starting transfers between devices  63.7 us (8%)
  other arithmetic  51.2 us (6%)
  local copies, waits for them, and re-layouts  33.8 us (4%)
  between operations  25 us (3%)
  matrix products  13.6 us (2%)
    ppermute x44, waiting for transfers between devices, swap_dp(): return lax.ppermute(values, 'dp', [(i, i ^ mask) for i in range(count)])  226 us
    pallas_call x4, Pallas kernels, expert_call(): pl.pallas_call(kernel, grid=(steps,), in_specs=specs, out_specs=[fixed((r...  162 us
    pallas_call x5, Pallas kernels, weight_grads(): pl.pallas_call(functools.partial(weight_grad_kernel, count), grid=(2 * co...  88.1 us
    ppermute x44, starting transfers between devices, swap_dp(): return lax.ppermute(values, 'dp', [(i, i ^ mask) for i in range(count)])  60.3 us
    pallas_call x3, Pallas kernels, expert_update(): pl.pallas_call(functools.partial(expert_update_kernel, len(parts)), grid=...  40.3 us
    pallas_call x1, Pallas kernels, attention_backward(): pl.pallas_call(attention_backward_kernel, grid=(kv_here,), in_specs=[SCAL...  26.6 us
    pallas_call x1, Pallas kernels, attention_forward(): pl.pallas_call(attention_forward_kernel, grid=(kv_here,), in_specs=[SCALA...  23 us
    unnamed x160, local copies, waits for them, and re-layouts  20.1 us
  transfers between devices with their start and end apart: 63, of which 30 were waited for; matrix products, arithmetic and copies ran while one was open for 7% of the time, Pallas kernels for 39%

profile of v3, /device:TPU:0, one launch (start us, length us, event | category | flops | bytes accessed | tf_op | source)
XLA Modules:
  0.0 785.4 jit_solution(15797932200390390979)
XLA Ops:
  12.1 4.1 collective-permute-start.1
  18.4 8.0 %collective-permute-done.1 = bf16[72,1536]{1,0:T(8,128)(2,1)S(1)} collective-permute-done((bf16[72,1536]{1,0:T(8,128)(2,1)S(1)}, bf16[72,1536]{1,0:T(8,128)(2,1)S(1)}, u32[]{:S(2)}, u32[]{:S(2)}) %collective-permute-start.1) | collective-permute-done | bytes 221216 | tf_op jit(solution)/shard_map/ppermute | solution.py:61
  31.5 8.5 %round_units.1 = (bf16[8,3,64,1024]{3,2,1,0:T(8,128)(2,1)}, bf16[4,3,64,1024]{3,2,1,0:T(8,128)(2,1)}, bf16[4,3,64,1024]{3,2,1,0:T(8,128)(2,1)}, bf16[3,3,64,1024]{3,2,1,0:T(8,128)(2,1)}, bf16[5,3,64,1024]{3,2,1,0:T(8,128)(2,1)}) custom-call(f32[8,3,64,1024]{3,2,1,0:T(8,128)} %refs_3_.5), custom_call_target="tpu_custom_call" | custom-call | flops 1000 | bytes 1000 | tf_op jit(solution)/shard_map/round_units/pallas_call | solution.py:313
  56.0 10.4 %collective-permute-done.8.refs_6_.refs_3_ = bf16[288,1024]{1,0:T(8,128)(2,1)} collective-permute-done((bf16[288,1024]{1,0:T(8,128)(2,1)S(1)}, bf16[288,1024]{1,0:T(8,128)(2,1)}, u32[]{:S(2)}, u32[]{:S(2)}) %collective-permute-start.8) | collective-permute-done | bytes 589856 | tf_op jit(solution)/shard_map/ppermute | solution.py:61
  66.4 10.4 %collective-permute-done.7.refs_5_.refs_2_ = bf16[288,1024]{1,0:T(8,128)(2,1)S(1)} collective-permute-done((bf16[288,1024]{1,0:T(8,128)(2,1)S(1)}, bf16[288,1024]{1,0:T(8,128)(2,1)S(1)}, u32[]{:S(2)}, u32[]{:S(2)}) %collective-permute-start.7) | collective-permute-done | bytes 589856 | tf_op jit(solution)/shard_map/ppermute | solution.py:61
  89.4 23.0 %attention_forward.1 = (bf16[1024,1024]{1,0:T(8,128)(2,1)}, bf16[1024,512]{1,0:T(8,128)(2,1)}, bf16[1024,512]{1,0:T(8,128)(2,1)}, bf16[1024,512]{1,0:T(8,128)(2,...) custom-call(s32[1]{0:T(128)} %copy.102.refs_0_, s32[4,4]{1,0:T(4,128)S(1)} %xor_multiply_fusion.refs_1_.refs_0_, ...), custom_call_target="tpu_custom_call" | custom-call | flops 1000 | bytes 1000 | tf_op jit(solution)/shard_map/attention_forward/pallas_call | solution.py:221
  112.4 6.9 collective-permute-done.10.refs_5_
  139.4 39.9 %collective-permute-done.18.refs_2_ = bf16[512,1024]{1,0:T(8,128)(2,1)} collective-permute-done((bf16[512,1024]{1,0:T(8,128)(2,1)}, bf16[512,1024]{1,0:T(8,128)(2,1)}, u32[]{:S(2)}, u32[]{:S(2)}) %collective-permute-start.18) | collective-permute-done | bytes 1048608 | tf_op jit(solution)/shard_map/ppermute | solution.py:61
  180.7 25.0 %collective-permute-done.16.refs_1_.refs_4_.refs_10_.refs_12_ = bf16[4,3,64,1024]{3,2,1,0:T(8,128)(2,1)} collective-permute-done((bf16[4,3,64,1024]{3,2,1,0:T(8,128)(2,1)}, bf16[4,3,64,1024]{3,2,1,0:T(8,128)(2,1)}, u32[]{:S(2)}, u32[]{:S(2)}) %collective-permute-start.16) | collective-permute-done | bytes 1572896 | tf_op jit(solution)/shard_map/ppermute | solution.py:61
  205.7 6.0 collective-permute-done.20.refs_1_.refs_5_.refs_11_.refs_13_
  224.0 39.5 %expert_first.1 = (bf16[4096,1024]{1,0:T(8,128)(2,1)}, bf16[4096,1024]{1,0:T(8,128)(2,1)}, bf16[4096,1024]{1,0:T(8,128)(2,1)}, bf16[4096,1024]{1,0:T(8,128)(2,1)}, bf16[4096,1024]{1,0:T(8,128)(2,1)}) custom-call(bf16[512,1024]{1,0:T(8,128)(2,1)} %multiply_convert_fusion.refs_0_, bf16[512,1024]{1,0:T(8,128)(2,1)} %after.15.refs_1_, ...), custom_call_target="tpu_custom_call" | custom-call | flops 25769803776 | bytes 1000 | tf_op jit(solution)/shard_map/expert_first/pallas_call | solution.py:542
  264.7 41.5 %expert_second.1 = (bf16[512,1024]{1,0:T(8,128)(2,1)}, bf16[512,1024]{1,0:T(8,128)(2,1)}, bf16[512,1024]{1,0:T(8,128)(2,1)}, bf16[512,1024]{1,0:T(8,128)(2,1)}, ...) custom-call(bf16[4096,1024]{1,0:T(8,128)(2,1)} %get-tuple-element.99, ...), custom_call_target="tpu_custom_call" | custom-call | flops 1000 | bytes 1000 | tf_op jit(solution)/shard_map/expert_second/pallas_call | solution.py:542
  327.8 8.2 %collective-permute-done.25 = bf16[512,1024]{1,0:T(8,128)(2,1)S(1)} collective-permute-done((bf16[512,1024]{1,0:T(8,128)(2,1)S(1)}, bf16[512,1024]{1,0:T(8,128)(2,1)S(1)}, u32[]{:S(2)}, u32[]{:S(2)}) %collective-permute-start.25) | collective-permute-done | bytes 1048608 | tf_op jit(solution)/shard_map/ppermute | solution.py:61
  338.8 21.4 %collective-permute-done.29 = bf16[512,1024]{1,0:T(8,128)(2,1)S(1)} collective-permute-done((bf16[512,1024]{1,0:T(8,128)(2,1)S(1)}, bf16[512,1024]{1,0:T(8,128)(2,1)S(1)}, u32[]{:S(2)}, u32[]{:S(2)}) %collective-permute-start.29) | collective-permute-done | bytes 1048608 | tf_op jit(solution)/shard_map/ppermute | solution.py:61
  367.7 25.2 %expert_backward.2 = (bf16[512,1024]{1,0:T(8,128)(2,1)}, bf16[512,1024]{1,0:T(8,128)(2,1)}, bf16[4096,1024]{1,0:T(8,128)(2,1)}, bf16[4096,1024]{1,0:T(8,128)(2,1...) custom-call(bf16[512,1024]{1,0:T(8,128)(2,1)} %multiply_convert_fusion.1.refs_0_, ...), custom_call_target="tpu_custom_call" | custom-call | flops 1000 | bytes 1000 | tf_op jit(solution)/shard_map/expert_backward/pallas_call | solution.py:542
  392.9 20.5 %collective-permute-done.34.refs_0_ = bf16[512,1024]{1,0:T(8,128)(2,1)} collective-permute-done((bf16[512,1024]{1,0:T(8,128)(2,1)}, bf16[512,1024]{1,0:T(8,128)(2,1)}, u32[]{:S(2)}, u32[]{:S(2)}) %collective-permute-start.34) | collective-permute-done | bytes 1048608 | tf_op jit(solution)/shard_map/ppermute | solution.py:61
  416.2 6.8 collective-permute-done.36.refs_3_
  422.9 55.9 %expert_backward.3 = (bf16[512,1024]{1,0:T(8,128)(2,1)}, bf16[512,1024]{1,0:T(8,128)(2,1)}, bf16[512,1024]{1,0:T(8,128)(2,1)}, bf16[512,1024]{1,0:T(8,128)(2,1)}...) custom-call(bf16[512,1024]{1,0:T(8,128)(2,1)} %after.17.refs_0_, ...), custom_call_target="tpu_custom_call", output_to_operand_aliasing={{6}: (15, {}), {7}: (16, {}), {8}: (17, {}), {9}: (18, {}),... | custom-call | flops 1000 | bytes 1000 | tf_op jit(solution)/shard_map/expert_backward/pallas_call | solution.py:542
  479.6 15.3 %weight_grads.5 = (bf16[512,1024]{1,0:T(8,128)(2,1)}, bf16[512,1024]{1,0:T(8,128)(2,1)}) custom-call(bf16[4096,1024]{1,0:T(8,128)(2,1)} %get-tuple-element.128.refs_0_, bf16[4096,1024]{1,0:T(8,128)(2,1)} %get-tuple-element.129.refs_1_), custom_call_target="tpu_custom_call" | custom-call | flops 30000001024 | bytes 1000 | tf_op jit(solution)/shard_map/weight_grads/pallas_call | solution.py:644
  504.9 15.4 %weight_grads.6 = (bf16[512,1024]{1,0:T(8,128)(2,1)}, bf16[512,1024]{1,0:T(8,128)(2,1)}) custom-call(bf16[4096,1024]{1,0:T(8,128)(2,1)} %get-tuple-element.127.refs_0_, bf16[4096,1024]{1,0:T(8,128)(2,1)} %get-tuple-element.99.refs_0_.refs_1_.refs_2_, bf16[512,1024]{1,0:T(8,128)(2,1)} %get-tuple-element.130.refs_2_, ...), custom_call_target="tpu_custom_call" | custom-call | flops 30000001024 | bytes 1000 | tf_op jit(solution)/shard_map/weight_grads/pallas_call | solution.py:644
  523.4 15.3 %weight_grads.7 = (bf16[512,1024]{1,0:T(8,128)(2,1)}, bf16[512,1024]{1,0:T(8,128)(2,1)}) custom-call(bf16[4096,1024]{1,0:T(8,128)(2,1)} %get-tuple-element.126.refs_0_, bf16[4096,1024]{1,0:T(8,128)(2,1)} %get-tuple-element.99.refs_0_.refs_1_.refs_2_, bf16[512,1024]{1,0:T(8,128)(2,1)} %get-tuple-element.131.refs_2_, bf16[512,1024]{1,0:T(8,128)(2,1)} %add_convert_fusion.2.refs_3_), custom_call_target="tpu_custom_call" | custom-call | flops 30000001024 | bytes 1000 | tf_op jit(solution)/shard_map/weight_grads/pallas_call | solution.py:644
  538.7 6.7 collective-permute-done.44
  550.2 4.0 multiply_reduce_fusion.1
  566.6 26.6 %attention_backward.1 = (bf16[1024,512]{1,0:T(8,128)(2,1)S(1)}, bf16[1024,512]{1,0:T(8,128)(2,1)S(1)}) custom-call(s32[1]{0:T(128)} %copy.102.refs_0_, bf16[1024,1024]{1,0:T(8,128)(2,1)} %pad_maximum_fusion.3.refs_1_, bf16[1024,512]{1,0:T(8,128)(2,1)} %copy-done.16, bf16[1024,1024]{1,0:T(8,128)(2,1)} %get-tuple-element.136.refs_3_, ...), custom_call_target="tpu_custom_call" | custom-call | flops 1000 | bytes 1000 | tf_op jit(solution)/shard_map/attention_backward/pallas_call | solution.py:333
  608.2 5.3 convolution_convert_fusion.refs_3_
  613.6 26.6 %weight_grads.8 = (bf16[512,1024]{1,0:T(8,128)(2,1)}, bf16[512,1024]{1,0:T(8,128)(2,1)}, bf16[512,1024]{1,0:T(8,128)(2,1)}, bf16[512,1024]{1,0:T(8,128)(2,1)}) custom-call(bf16[4096,1024]{1,0:T(8,128)(2,1)} %get-tuple-element.143.refs_0_, bf16[4096,1024]{1,0:T(8,128)(2,1)} %get-tuple-element.144.refs_1_, ...), custom_call_target="tpu_custom_call" | custom-call | flops 1000 | bytes 1000 | tf_op jit(solution)/shard_map/weight_grads/pallas_call | solution.py:644
  641.7 23.1 %collective-permute-done.59.refs_3_.refs_2_ = bf16[512,1024]{1,0:T(8,128)(2,1)} collective-permute-done((bf16[512,1024]{1,0:T(8,128)(2,1)}, bf16[512,1024]{1,0:T(8,128)(2,1)}, u32[]{:S(2)}, u32[]{:S(2)}) %collective-permute-start.59) | collective-permute-done | bytes 1048608 | tf_op jit(solution)/shard_map/ppermute | solution.py:61
  664.7 25.1 %collective-permute-done.51.refs_2_.refs_4_ = bf16[512,1024]{1,0:T(8,128)(2,1)} collective-permute-done((bf16[512,1024]{1,0:T(8,128)(2,1)}, bf16[512,1024]{1,0:T(8,128)(2,1)}, u32[]{:S(2)}, u32[]{:S(2)}) %collective-permute-start.51) | collective-permute-done | bytes 1048608 | tf_op jit(solution)/shard_map/ppermute | solution.py:61
  689.8 15.5 %weight_grads.9 = (bf16[512,1024]{1,0:T(8,128)(2,1)}, bf16[512,1024]{1,0:T(8,128)(2,1)}) custom-call(bf16[4096,1024]{1,0:T(8,128)(2,1)} %get-tuple-element.159.refs_0_, bf16[4096,1024]{1,0:T(8,128)(2,1)} %get-tuple-element.129.refs_1_, bf16[512,1024]{1,0:T(8,128)(2,1)} %get-tuple-element.149.refs_2_, ...), custom_call_target="tpu_custom_call" | custom-call | flops 1000 | bytes 1000 | tf_op jit(solution)/shard_map/weight_grads/pallas_call | solution.py:644
  711.1 13.2 %expert_update.3 = (f32[8,3,64,1024]{3,2,1,0:T(8,128)}, f32[8,3,4,64,64]{4,3,2,1,0:T(8,128)}, f32[8,3,4,256,256]{4,3,2,1,0:T(8,128)}, f32[8,3,64,1024]{3,2,1,0:T(8,128)}) custom-call(bf16[512,1024]{1,0:T(8,128)(2,1)} %get-tuple-element.148.refs_0_, bf16[512,1024]{1,0:T(8,128)(2,1)} %collective-permute-done.50.refs_1_, ...), custom_call_target="tpu_custom_call" | custom-call | flops 12000000000 | bytes 1000 | tf_op jit(solution)/shard_map/expert_update/pallas_call | solution.py:718
  725.2 13.2 %expert_update.4 = (f32[8,3,64,1024]{3,2,1,0:T(8,128)}, f32[8,3,4,64,64]{4,3,2,1,0:T(8,128)}, f32[8,3,4,256,256]{4,3,2,1,0:T(8,128)}, f32[8,3,64,1024]{3,2,1,0:T(8,128)}) custom-call(bf16[512,1024]{1,0:T(8,128)(2,1)} %get-tuple-element.146.refs_0_, ...), custom_call_target="tpu_custom_call", output_to_operand_aliasing={{0}: (8, {}), {1}: (9, {}), {2}: (10, {}), {3}: (11, {})} | custom-call | flops 12000000000 | bytes 1000 | tf_op jit(solution)/shard_map/expert_update/pallas_call | solution.py:718
  757.7 14.0 %expert_update.5 = (f32[8,3,64,1024]{3,2,1,0:T(8,128)}, f32[8,3,4,64,64]{4,3,2,1,0:T(8,128)}, f32[8,3,4,256,256]{4,3,2,1,0:T(8,128)}, f32[8,3,64,1024]{3,2,1,0:T(8,128)}) custom-call(bf16[512,1024]{1,0:T(8,128)(2,1)} %get-tuple-element.160.refs_0_, ...), custom_call_target="tpu_custom_call", output_to_operand_aliasing={{0}: (9, {}), {1}: (10, {}), {2}: (11, {}), {3}: (12, {})} | custom-call | flops 12000000000 | bytes 1000 | tf_op jit(solution)/shard_map/expert_update/pallas_call | solution.py:718
  (375 shorter events, 179.9 us)
Async XLA Ops:
  7.2 764.5 %reduce-scatter.5.cloned.1.call-start = ((), (), s32[]{:S(2)}) async-start(), calls=%async_computation.3 | async-start | bytes 1114112 | tf_op jit(solution)/shard_map/reduce_scatter | solution.py:1056
  18.4 26.3 %collective-permute-start = (bf16[512,1024]{1,0:T(8,128)(2,1)}, bf16[512,1024]{1,0:T(8,128)(2,1)S(1)}, u32[]{:S(2)}, u32[]{:S(2)}) collective-permute-start(bf16[512,1024]{1,0:T(8,128)(2,1)} %fusion.3), channel_id=1, source_target_pairs={{0,1},{1,0},{2,3},{3,2},{4,5},{5,4},{6,7},{7,6},{8,9},{9,8},{10,11... | collective-permute-start | bytes 3145736 | tf_op jit(solution)/shard_map/ppermute | solution.py:66
  52.6 69.7 %collective-permute-start.12 = (bf16[4,3,64,1024]{3,2,1,0:T(8,128)(2,1)}, bf16[4,3,64,1024]{3,2,1,0:T(8,128)(2,1)S(1)}, u32[]{:S(2)}, u32[]{:S(2)}) collective-permute-start(bf16[4,3,64,1024]{3,2,1,0:T(8,128)(2,1)} %after.12), channel_id=1, source_target_pairs={{0,16},{2,18},{4,20},{6,22},{8,24},{10,26},{12,28},{14,30},{16,0},... | collective-permute-start | bytes 4718600 | tf_op jit(solution)/shard_map/ppermute | solution.py:61
  78.4 43.9 %collective-permute-start.13 = (bf16[3,3,64,1024]{3,2,1,0:T(8,128)(2,1)}, bf16[3,3,64,1024]{3,2,1,0:T(8,128)(2,1)S(1)}, u32[]{:S(2)}, u32[]{:S(2)}) collective-permute-start(bf16[3,3,64,1024]{3,2,1,0:T(8,128)(2,1)} %after.13), channel_id=1, source_target_pairs={{0,4},{2,6},{4,0},{6,2},{8,12},{10,14},{12,8},{14,10},{16,20},{18,... | collective-permute-start | bytes 3538952 | tf_op jit(solution)/shard_map/ppermute | solution.py:61
  81.6 30.8 %collective-permute-start.11 = (bf16[288,512]{1,0:T(8,128)(2,1)}, bf16[288,512]{1,0:T(8,128)(2,1)}, u32[]{:S(2)}, u32[]{:S(2)}) collective-permute-start(bf16[288,512]{1,0:T(8,128)(2,1)} %slice.107.refs_3_), channel_id=1, source_target_pairs={{0,6},{2,4},{4,2},{6,0},{8,14},{10,12},{12,10},{14,8},{16,22},{18,... | collective-permute-start | bytes 884744 | tf_op jit(solution)/shard_map/ppermute | solution.py:61
  83.1 36.2 %collective-permute-start.10 = (bf16[288,512]{1,0:T(8,128)(2,1)}, bf16[288,512]{1,0:T(8,128)(2,1)}, u32[]{:S(2)}, u32[]{:S(2)}) collective-permute-start(bf16[288,512]{1,0:T(8,128)(2,1)} %slice.107.refs_3_), channel_id=1, source_target_pairs={{0,4},{2,6},{4,0},{6,2},{8,12},{10,14},{12,8},{14,10},{16,20},{18,... | collective-permute-start | bytes 884744 | tf_op jit(solution)/shard_map/ppermute | solution.py:61
  83.9 35.4 %collective-permute-start.9 = (bf16[288,512]{1,0:T(8,128)(2,1)}, bf16[288,512]{1,0:T(8,128)(2,1)}, u32[]{:S(2)}, u32[]{:S(2)}) collective-permute-start(bf16[288,512]{1,0:T(8,128)(2,1)} %slice.107.refs_3_), channel_id=1, source_target_pairs={{0,2},{2,0},{4,6},{6,4},{8,10},{10,8},{12,14},{14,12},{16,18},{18,... | collective-permute-start | bytes 884744 | tf_op jit(solution)/shard_map/ppermute | solution.py:61
  132.8 46.5 %collective-permute-start.18 = (bf16[512,1024]{1,0:T(8,128)(2,1)}, bf16[512,1024]{1,0:T(8,128)(2,1)}, u32[]{:S(2)}, u32[]{:S(2)}) collective-permute-start(bf16[512,1024]{1,0:T(8,128)(2,1)} %multiply_convert_fusion.refs_0_), channel_id=1, source_target_pairs={{0,8},{2,10},{4,12},{6,14},{8,0},{10,2},{12,4},{14,6},{16,24},{18,... | collective-permute-start | bytes 3145736 | tf_op jit(solution)/shard_map/ppermute | solution.py:61
  132.8 47.9 %collective-permute-start.17 = (bf16[5,3,64,1024]{3,2,1,0:T(8,128)(2,1)}, bf16[5,3,64,1024]{3,2,1,0:T(8,128)(2,1)}, u32[]{:S(2)}, u32[]{:S(2)}) collective-permute-start(bf16[5,3,64,1024]{3,2,1,0:T(8,128)(2,1)} %get-tuple-element.98), channel_id=1, source_target_pairs={{0,4},{2,6},{4,0},{6,2},{8,12},{10,14},{12,8},{14,10},{16,20},{18,... | collective-permute-start | bytes 5898248 | tf_op jit(solution)/shard_map/ppermute | solution.py:61
  134.3 71.4 %collective-permute-start.16 = (bf16[4,3,64,1024]{3,2,1,0:T(8,128)(2,1)}, bf16[4,3,64,1024]{3,2,1,0:T(8,128)(2,1)}, u32[]{:S(2)}, u32[]{:S(2)}) collective-permute-start(bf16[4,3,64,1024]{3,2,1,0:T(8,128)(2,1)} %after.14), channel_id=1, source_target_pairs={{0,16},{2,18},{4,20},{6,22},{8,24},{10,26},{12,28},{14,30},{16,0},... | collective-permute-start | bytes 4718600 | tf_op jit(solution)/shard_map/ppermute | solution.py:61
  137.5 74.2 %collective-permute-start.20 = (bf16[4,3,64,1024]{3,2,1,0:T(8,128)(2,1)S(1)}, bf16[4,3,64,1024]{3,2,1,0:T(8,128)(2,1)}, u32[]{:S(2)}, u32[]{:S(2)}) collective-permute-start(bf16[4,3,64,1024]{3,2,1,0:T(8,128)(2,1)S(1)} %collective-permute-done.12.refs_7_.refs_3_.refs_9_.refs_11_), channel_id=1, source_target_pairs={{0,4},{2,6},{4,0},{6,2},{8,12},{10,14},{12,8},{14,10},{16,20},{18,... | collective-permute-start | bytes 4718600 | tf_op jit(solution)/shard_map/ppermute | solution.py:61
  138.0 67.7 %collective-permute-start.15 = (bf16[512,1024]{1,0:T(8,128)(2,1)}, bf16[512,1024]{1,0:T(8,128)(2,1)}, u32[]{:S(2)}, u32[]{:S(2)}) collective-permute-start(bf16[512,1024]{1,0:T(8,128)(2,1)} %multiply_convert_fusion.refs_0_), channel_id=1, source_target_pairs={{0,2},{2,0},{4,6},{6,4},{8,10},{10,8},{12,14},{14,12},{16,18},{18,... | collective-permute-start | bytes 3145736 | tf_op jit(solution)/shard_map/ppermute | solution.py:61
  179.3 32.4 %collective-permute-start.19 = (bf16[512,1024]{1,0:T(8,128)(2,1)}, bf16[512,1024]{1,0:T(8,128)(2,1)S(1)}, u32[]{:S(2)}, u32[]{:S(2)}) collective-permute-start(bf16[512,1024]{1,0:T(8,128)(2,1)} %collective-permute-done.18.refs_2_), channel_id=1, source_target_pairs={{0,2},{2,0},{4,6},{6,4},{8,10},{10,8},{12,14},{14,12},{16,18},{18,... | collective-permute-start | bytes 3145736 | tf_op jit(solution)/shard_map/ppermute | solution.py:61
  219.8 43.8 %collective-permute-start.22 = (bf16[4,3,64,1024]{3,2,1,0:T(8,128)(2,1)}, bf16[4,3,64,1024]{3,2,1,0:T(8,128)(2,1)S(1)}, u32[]{:S(2)}, u32[]{:S(2)}) collective-permute-start(bf16[4,3,64,1024]{3,2,1,0:T(8,128)(2,1)} %collective-permute-done.16.refs_1_.refs_4_.refs_10_.refs_12_), channel_id=1, source_target_pairs={{0,4},{2,6},{4,0},{6,2},{8,12},{10,14},{12,8},{14,10},{16,20},{18,... | collective-permute-start | bytes 4718600 | tf_op jit(solution)/shard_map/ppermute | solution.py:61
  312.7 26.1 %collective-permute-start.27 = (bf16[512,1024]{1,0:T(8,128)(2,1)S(1)}, bf16[512,1024]{1,0:T(8,128)(2,1)S(1)}, u32[]{:S(2)}, u32[]{:S(2)}) collective-permute-start(bf16[512,1024]{1,0:T(8,128)(2,1)S(1)} %add_convert_fusion.7), channel_id=1, source_target_pairs={{0,8},{2,10},{4,12},{6,14},{8,0},{10,2},{12,4},{14,6},{16,24},{18,... | collective-permute-start | bytes 3145736 | tf_op jit(solution)/shard_map/ppermute | solution.py:61
  314.9 45.3 %collective-permute-start.29 = (bf16[512,1024]{1,0:T(8,128)(2,1)S(1)}, bf16[512,1024]{1,0:T(8,128)(2,1)S(1)}, u32[]{:S(2)}, u32[]{:S(2)}) collective-permute-start(bf16[512,1024]{1,0:T(8,128)(2,1)S(1)} %add_convert_fusion.6), channel_id=1, source_target_pairs={{0,10},{2,8},{4,14},{6,12},{8,2},{10,0},{12,6},{14,4},{16,26},{18,... | collective-permute-start | bytes 3145736 | tf_op jit(solution)/shard_map/ppermute | solution.py:61
  364.2 28.7 %collective-permute-start.35 = (bf16[512,1024]{1,0:T(8,128)(2,1)}, bf16[512,1024]{1,0:T(8,128)(2,1)}, u32[]{:S(2)}, u32[]{:S(2)}) collective-permute-start(bf16[512,1024]{1,0:T(8,128)(2,1)} %multiply_convert_fusion.1.refs_0_), channel_id=1, source_target_pairs={{0,10},{2,8},{4,14},{6,12},{8,2},{10,0},{12,6},{14,4},{16,26},{18,... | collective-permute-start | bytes 3145736 | tf_op jit(solution)/shard_map/ppermute | solution.py:61
  366.8 46.7 %collective-permute-start.34 = (bf16[512,1024]{1,0:T(8,128)(2,1)}, bf16[512,1024]{1,0:T(8,128)(2,1)}, u32[]{:S(2)}, u32[]{:S(2)}) collective-permute-start(bf16[512,1024]{1,0:T(8,128)(2,1)} %multiply_convert_fusion.1.refs_0_), channel_id=1, source_target_pairs={{0,8},{2,10},{4,12},{6,14},{8,0},{10,2},{12,4},{14,6},{16,24},{18,... | collective-permute-start | bytes 3145736 | tf_op jit(solution)/shard_map/ppermute | solution.py:61
  367.1 46.4 %collective-permute-start.33 = (bf16[512,1024]{1,0:T(8,128)(2,1)}, bf16[512,1024]{1,0:T(8,128)(2,1)}, u32[]{:S(2)}, u32[]{:S(2)}) collective-permute-start(bf16[512,1024]{1,0:T(8,128)(2,1)} %multiply_convert_fusion.1.refs_0_), channel_id=1, source_target_pairs={{0,2},{2,0},{4,6},{6,4},{8,10},{10,8},{12,14},{14,12},{16,18},{18,... | collective-permute-start | bytes 3145736 | tf_op jit(solution)/shard_map/ppermute | solution.py:61
  415.7 133.9 %collective-permute-start.32 = (bf16[512,1024]{1,0:T(8,128)(2,1)}, bf16[512,1024]{1,0:T(8,128)(2,1)}, u32[]{:S(2)}, u32[]{:S(2)}) collective-permute-start(bf16[512,1024]{1,0:T(8,128)(2,1)} %get-tuple-element.114), channel_id=1, source_target_pairs={{0,1},{1,0},{2,3},{3,2},{4,5},{5,4},{6,7},{7,6},{8,9},{9,8},{10,11... | collective-permute-start | bytes 3145736 | tf_op jit(solution)/shard_map/ppermute | solution.py:66
  499.0 50.5 %collective-permute-start.38 = (bf16[512,1024]{1,0:T(8,128)(2,1)}, bf16[512,1024]{1,0:T(8,128)(2,1)}, u32[]{:S(2)}, u32[]{:S(2)}) collective-permute-start(bf16[512,1024]{1,0:T(8,128)(2,1)} %add_convert_fusion.5.refs_3_), channel_id=1, source_target_pairs={{0,2},{2,0},{4,6},{6,4},{8,10},{10,8},{12,14},{14,12},{16,18},{18,... | collective-permute-start | bytes 3145736 | tf_op jit(solution)/shard_map/ppermute | solution.py:61
  501.8 47.8 %collective-permute-start.40 = (bf16[512,1024]{1,0:T(8,128)(2,1)}, bf16[512,1024]{1,0:T(8,128)(2,1)}, u32[]{:S(2)}, u32[]{:S(2)}) collective-permute-start(bf16[512,1024]{1,0:T(8,128)(2,1)} %add_convert_fusion.4.refs_4_), channel_id=1, source_target_pairs={{0,8},{2,10},{4,12},{6,14},{8,0},{10,2},{12,4},{14,6},{16,24},{18,... | collective-permute-start | bytes 3145736 | tf_op jit(solution)/shard_map/ppermute | solution.py:61
  503.9 45.6 %collective-permute-start.42 = (bf16[512,1024]{1,0:T(8,128)(2,1)S(1)}, bf16[512,1024]{1,0:T(8,128)(2,1)}, u32[]{:S(2)}, u32[]{:S(2)}) collective-permute-start(bf16[512,1024]{1,0:T(8,128)(2,1)S(1)} %add_convert_fusion.3.refs_5_), channel_id=1, source_target_pairs={{0,10},{2,8},{4,14},{6,12},{8,2},{10,0},{12,6},{14,4},{16,26},{18,... | collective-permute-start | bytes 3145736 | tf_op jit(solution)/shard_map/ppermute | solution.py:61
  561.5 210.3 %reduce-scatter.3.cloned.1.call-start = ((), (), s32[]{:S(2)}) async-start(), calls=%async_computation.2 | async-start | bytes 2228224 | tf_op jit(solution)/shard_map/reduce_scatter | solution.py:1055
  561.5 41.8 %collective-permute-start.47 = (bf16[512,1024]{1,0:T(8,128)(2,1)}, bf16[512,1024]{1,0:T(8,128)(2,1)}, u32[]{:S(2)}, u32[]{:S(2)}) collective-permute-start(bf16[512,1024]{1,0:T(8,128)(2,1)} %get-tuple-element.133.refs_1_.refs_9_), channel_id=1, source_target_pairs={{0,4},{2,6},{4,0},{6,2},{8,12},{10,14},{12,8},{14,10},{16,20},{18,... | collective-permute-start | bytes 3145736 | tf_op jit(solution)/shard_map/ppermute | solution.py:61
  562.2 102.6 %collective-permute-start.59 = (bf16[512,1024]{1,0:T(8,128)(2,1)}, bf16[512,1024]{1,0:T(8,128)(2,1)}, u32[]{:S(2)}, u32[]{:S(2)}) collective-permute-start(bf16[512,1024]{1,0:T(8,128)(2,1)} %add_convert_fusion.2.refs_3_), channel_id=1, source_target_pairs={{0,16},{2,18},{4,20},{6,22},{8,24},{10,26},{12,28},{14,30},{16,0},... | collective-permute-start | bytes 3145736 | tf_op jit(solution)/shard_map/ppermute | solution.py:61
  565.1 124.8 %collective-permute-start.51 = (bf16[512,1024]{1,0:T(8,128)(2,1)}, bf16[512,1024]{1,0:T(8,128)(2,1)}, u32[]{:S(2)}, u32[]{:S(2)}) collective-permute-start(bf16[512,1024]{1,0:T(8,128)(2,1)} %add_convert_fusion.1.refs_2_.refs_10_), channel_id=1, source_target_pairs={{0,16},{2,18},{4,20},{6,22},{8,24},{10,26},{12,28},{14,30},{16,0},... | collective-permute-start | bytes 3145736 | tf_op jit(solution)/shard_map/ppermute | solution.py:61
  602.4 102.9 %collective-permute-start.46 = (bf16[512,1024]{1,0:T(8,128)(2,1)}, bf16[512,1024]{1,0:T(8,128)(2,1)}, u32[]{:S(2)}, u32[]{:S(2)}) collective-permute-start(bf16[512,1024]{1,0:T(8,128)(2,1)} %convolution_convert_fusion.2), channel_id=1, source_target_pairs={{0,1},{1,0},{2,3},{3,2},{4,5},{5,4},{6,7},{7,6},{8,9},{9,8},{10,11... | collective-permute-start | bytes 3145736 | tf_op jit(solution)/shard_map/ppermute | solution.py:66
  605.3 119.0 %collective-permute-start.49 = (bf16[512,1024]{1,0:T(8,128)(2,1)S(1)}, bf16[512,1024]{1,0:T(8,128)(2,1)}, u32[]{:S(2)}, u32[]{:S(2)}) collective-permute-start(bf16[512,1024]{1,0:T(8,128)(2,1)S(1)} %add_convert_fusion.refs_5_), channel_id=1, source_target_pairs={{0,16},{2,18},{4,20},{6,22},{8,24},{10,26},{12,28},{14,30},{16,0},... | collective-permute-start | bytes 3145736 | tf_op jit(solution)/shard_map/ppermute | solution.py:61
  640.2 84.1 %collective-permute-start.48 = (bf16[512,1024]{1,0:T(8,128)(2,1)}, bf16[512,1024]{1,0:T(8,128)(2,1)S(1)}, u32[]{:S(2)}, u32[]{:S(2)}) collective-permute-start(bf16[512,1024]{1,0:T(8,128)(2,1)} %get-tuple-element.147), channel_id=1, source_target_pairs={{0,4},{2,6},{4,0},{6,2},{8,12},{10,14},{12,8},{14,10},{16,20},{18,... | collective-permute-start | bytes 3145736 | tf_op jit(solution)/shard_map/ppermute | solution.py:61
  664.7 46.3 %collective-permute-start.50 = (bf16[512,1024]{1,0:T(8,128)(2,1)}, bf16[512,1024]{1,0:T(8,128)(2,1)}, u32[]{:S(2)}, u32[]{:S(2)}) collective-permute-start(bf16[512,1024]{1,0:T(8,128)(2,1)} %get-tuple-element.149.refs_2_), channel_id=1, source_target_pairs={{0,4},{2,6},{4,0},{6,2},{8,12},{10,14},{12,8},{14,10},{16,20},{18,... | collective-permute-start | bytes 3145736 | tf_op jit(solution)/shard_map/ppermute | solution.py:61
  705.3 52.3 %collective-permute-start.60 = (bf16[512,1024]{1,0:T(8,128)(2,1)}, bf16[512,1024]{1,0:T(8,128)(2,1)}, u32[]{:S(2)}, u32[]{:S(2)}) collective-permute-start(bf16[512,1024]{1,0:T(8,128)(2,1)} %get-tuple-element.161), channel_id=1, source_target_pairs={{0,4},{2,6},{4,0},{6,2},{8,12},{10,14},{12,8},{14,10},{16,20},{18,... | collective-permute-start | bytes 3145736 | tf_op jit(solution)/shard_map/ppermute | solution.py:61
  (108 other events, 1120.3 us)
Sparse Core Ops, SparseCore 0:
  561.6 120.7 reduce-scatter.4
  684.7 81.0 reduce-scatter.2

commit v4 on v3

--- a/solution.py
+++ b/solution.py
@@ -870,6 +870,26 @@
     return lax.axis_index("dp") ^ jnp.array(masks, jnp.int32)
 
 
+def scatter_rows(values):
+    low = jnp.bfloat16
+    count = lax.axis_size("dp")
+    bits = count.bit_length() - 1
+    values = values.reshape((2,) * bits + (values.shape[0] // count, values.shape[1]))
+    left = list(range(bits - 1, -1, -1))
+    order = [0, 2, 1] + list(range(3, bits))
+    stages = []
+    for bit in order:
+        axis = left.index(bit)
+        left.pop(axis)
+        here = (lax.axis_index("dp") >> bit) & 1
+        mine = lax.dynamic_index_in_dim(values, here, axis, keepdims=False)
+        other = lax.dynamic_index_in_dim(values, 1 - here, axis, keepdims=False)
+        sent = swap_dp(other, 1 << bit)
+        values = (mine.astype(jnp.float32) + sent.astype(jnp.float32)).astype(low)
+        stages.append(values)
+    return stages
+
+
 def add_grads(far, both):
     return (far.astype(jnp.float32) + swap_dp(both, WEIGHT_BITS[0]).astype(jnp.float32)).astype(
         jnp.bfloat16
@@ -1049,10 +1069,11 @@
     qkv_part = dot(normed, qkv_grad, 0, 0).astype(low)
     output_part = dot(branch_low, attended, 0, 0).astype(low)
     gate_up_near = weight_grads([gates[0], uppers[0]], mix, [qkv_part, output_part, upper_sum])
+    qkv_stages = scatter_rows(qkv_part)
+    qkv_part = qkv_stages[-1]
     down_near = weight_grads(
-        [inners[0]], output_low, [gate_up_near[0], far_down, far_gate]
-    )
-    qkv_part = lax.psum_scatter(qkv_part, "dp", scatter_dimension=0, tiled=True)
+        [inners[0]], output_low, [gate_up_near[0]]
+    )
     output_part = lax.psum_scatter(output_part, "dp", scatter_dimension=0, tiled=True)
     normed_grad_other = dot(other_half(qkv_grad), w_qkv, 1, 1).astype(low)
     normed_grad = dot(own_half(qkv_grad), w_qkv, 1, 1)
@@ -1067,12 +1088,14 @@
         1: grad_terms(gate_up_near[3], gate_up_near[2], far_upper),
     }
     state = (expert_master, expert_left, expert_right, expert_left_root, expert_right_root)
-    updated = expert_update(0, parts[0], state, None, [input_grad])
-    updated = expert_update(1, parts[1], state, updated)
+    updated = expert_update(
+        0, parts[0], state, None, [far_down, far_gate, qkv_stages[0]]
+    )
+    updated = expert_update(1, parts[1], state, updated, [input_grad, qkv_stages[1]] + parts[2][1:2])
     loss_row = jnp.full((1, D), loss_part)
     sums = jnp.concatenate([gain_attention[None], gain_mix[None], loss_row], axis=0)
     sums = sum_everywhere(after(sums, updated[0]))
-    updated = expert_update(2, parts[2], state, updated, [sums])
+    updated = expert_update(2, parts[2], state, updated, [sums, qkv_part, output_part])
     expert_grad, expert_left_new, expert_right_new, expert_new = updated
     attention_grad, attention_left_new, attention_right_new, attention_new = attention_update(
         qkv_part,

time: 796 us -> 787 us (0.989)
  waiting for transfers between devices: 245 us -> 232 us
    ppermute x44 -> x48, waiting for transfers between devices: 226 us -> 216 us  [swap_dp(): return lax.ppermute(values, 'dp', [(i, i ^ mask) for i in range(count)])]
    unnamed x160 -> x176, local copies, waits for them, and re-layouts: 20.1 us -> 16 us
    ppermute x44 -> x48, starting transfers between devices: 60.3 us -> 64.2 us  [swap_dp(): return lax.ppermute(values, 'dp', [(i, i ^ mask) for i in range(count)])]
  transfers between devices with their start and end apart: 63 -> 66, of which waited for: 30 -> 27; matrix products, arithmetic and copies ran while one was open for 7% -> 8% of each run, Pallas kernels for 39% -> 38%
where the time goes in v4:
time: 787 us; the launch traced here: 777 us
  Pallas kernels  353 us (45%)
  waiting for transfers between devices  232 us (29%)
  starting transfers between devices  67.7 us (9%)
  other arithmetic  55.5 us (7%)
  local copies, waits for them, and re-layouts  32.5 us (4%)
  between operations  25 us (3%)
  matrix products  11.2 us (1%)
    ppermute x48, waiting for transfers between devices, swap_dp(): return lax.ppermute(values, 'dp', [(i, i ^ mask) for i in range(count)])  216 us
    pallas_call x4, Pallas kernels, expert_call(): pl.pallas_call(kernel, grid=(steps,), in_specs=specs, out_specs=[fixed((r...  162 us
    pallas_call x5, Pallas kernels, weight_grads(): pl.pallas_call(functools.partial(weight_grad_kernel, count), grid=(2 * co...  87.9 us
    ppermute x48, starting transfers between devices, swap_dp(): return lax.ppermute(values, 'dp', [(i, i ^ mask) for i in range(count)])  64.2 us
    pallas_call x3, Pallas kernels, expert_update(): pl.pallas_call(functools.partial(expert_update_kernel, len(parts)), grid=...  40.7 us
    pallas_call x1, Pallas kernels, attention_backward(): pl.pallas_call(attention_backward_kernel, grid=(kv_here,), in_specs=[SCAL...  26.6 us
    pallas_call x1, Pallas kernels, attention_forward(): pl.pallas_call(attention_forward_kernel, grid=(kv_here,), in_specs=[SCALA...  22.9 us
    unnamed x176, local copies, waits for them, and re-layouts  16 us
  transfers between devices with their start and end apart: 66, of which 27 were waited for; matrix products, arithmetic and copies ran while one was open for 8% of the time, Pallas kernels for 38%

profile of v4, /device:TPU:0, one launch (start us, length us, event | category | flops | bytes accessed | tf_op | source)
XLA Modules:
  0.0 776.8 jit_solution(10405997790307604129)
XLA Ops:
  18.5 8.0 %collective-permute-done.1 = bf16[72,1536]{1,0:T(8,128)(2,1)S(1)} collective-permute-done((bf16[72,1536]{1,0:T(8,128)(2,1)S(1)}, bf16[72,1536]{1,0:T(8,128)(2,1)S(1)}, u32[]{:S(2)}, u32[]{:S(2)}) %collective-permute-start.1) | collective-permute-done | bytes 221216 | tf_op jit(solution)/shard_map/ppermute | solution.py:61
  31.5 8.5 %round_units.1 = (bf16[8,3,64,1024]{3,2,1,0:T(8,128)(2,1)}, bf16[4,3,64,1024]{3,2,1,0:T(8,128)(2,1)}, bf16[4,3,64,1024]{3,2,1,0:T(8,128)(2,1)}, bf16[3,3,64,1024]{3,2,1,0:T(8,128)(2,1)}, bf16[5,3,64,1024]{3,2,1,0:T(8,128)(2,1)}) custom-call(f32[8,3,64,1024]{3,2,1,0:T(8,128)} %refs_3_.5), custom_call_target="tpu_custom_call" | custom-call | flops 1000 | bytes 1000 | tf_op jit(solution)/shard_map/round_units/pallas_call | solution.py:313
  55.9 9.5 %collective-permute-done.6.refs_4_.refs_1_ = bf16[288,1024]{1,0:T(8,128)(2,1)} collective-permute-done((bf16[288,1024]{1,0:T(8,128)(2,1)S(1)}, bf16[288,1024]{1,0:T(8,128)(2,1)}, u32[]{:S(2)}, u32[]{:S(2)}) %collective-permute-start.6) | collective-permute-done | bytes 589856 | tf_op jit(solution)/shard_map/ppermute | solution.py:61
  65.4 11.6 %collective-permute-done.7.refs_5_.refs_2_ = bf16[288,1024]{1,0:T(8,128)(2,1)S(1)} collective-permute-done((bf16[288,1024]{1,0:T(8,128)(2,1)S(1)}, bf16[288,1024]{1,0:T(8,128)(2,1)S(1)}, u32[]{:S(2)}, u32[]{:S(2)}) %collective-permute-start.7) | collective-permute-done | bytes 589856 | tf_op jit(solution)/shard_map/ppermute | solution.py:61
  89.6 22.9 %attention_forward.1 = (bf16[1024,1024]{1,0:T(8,128)(2,1)}, bf16[1024,512]{1,0:T(8,128)(2,1)}, bf16[1024,512]{1,0:T(8,128)(2,1)}, bf16[1024,512]{1,0:T(8,128)(2,...) custom-call(s32[1]{0:T(128)} %copy.118.refs_0_, s32[4,4]{1,0:T(4,128)S(1)} %xor_multiply_fusion.refs_1_.refs_0_, ...), custom_call_target="tpu_custom_call" | custom-call | flops 1000 | bytes 1000 | tf_op jit(solution)/shard_map/attention_forward/pallas_call | solution.py:221
  116.5 5.8 collective-permute-done.12.refs_7_.refs_3_.refs_9_.refs_11_
  138.6 39.4 %collective-permute-done.18.refs_2_ = bf16[512,1024]{1,0:T(8,128)(2,1)} collective-permute-done((bf16[512,1024]{1,0:T(8,128)(2,1)S(1)}, bf16[512,1024]{1,0:T(8,128)(2,1)}, u32[]{:S(2)}, u32[]{:S(2)}) %collective-permute-start.18) | collective-permute-done | bytes 1048608 | tf_op jit(solution)/shard_map/ppermute | solution.py:61
  179.4 25.4 %collective-permute-done.16.refs_1_.refs_4_.refs_10_.refs_12_ = bf16[4,3,64,1024]{3,2,1,0:T(8,128)(2,1)} collective-permute-done((bf16[4,3,64,1024]{3,2,1,0:T(8,128)(2,1)}, bf16[4,3,64,1024]{3,2,1,0:T(8,128)(2,1)}, u32[]{:S(2)}, u32[]{:S(2)}) %collective-permute-start.16) | collective-permute-done | bytes 1572896 | tf_op jit(solution)/shard_map/ppermute | solution.py:61
  204.8 6.0 collective-permute-done.20.refs_1_.refs_5_.refs_11_.refs_13_
  222.0 39.5 %expert_first.1 = (bf16[4096,1024]{1,0:T(8,128)(2,1)}, bf16[4096,1024]{1,0:T(8,128)(2,1)}, bf16[4096,1024]{1,0:T(8,128)(2,1)}, bf16[4096,1024]{1,0:T(8,128)(2,1)}, bf16[4096,1024]{1,0:T(8,128)(2,1)}) custom-call(bf16[512,1024]{1,0:T(8,128)(2,1)} %copy-done.44, bf16[512,1024]{1,0:T(8,128)(2,1)} %after.15.refs_1_, ...), custom_call_target="tpu_custom_call" | custom-call | flops 25769803776 | bytes 1000 | tf_op jit(solution)/shard_map/expert_first/pallas_call | solution.py:542
  262.7 41.4 %expert_second.1 = (bf16[512,1024]{1,0:T(8,128)(2,1)}, bf16[512,1024]{1,0:T(8,128)(2,1)}, bf16[512,1024]{1,0:T(8,128)(2,1)}, bf16[512,1024]{1,0:T(8,128)(2,1)}, ...) custom-call(bf16[4096,1024]{1,0:T(8,128)(2,1)} %get-tuple-element.99, ...), custom_call_target="tpu_custom_call" | custom-call | flops 1000 | bytes 1000 | tf_op jit(solution)/shard_map/expert_second/pallas_call | solution.py:542
  325.5 8.5 %collective-permute-done.25 = bf16[512,1024]{1,0:T(8,128)(2,1)S(1)} collective-permute-done((bf16[512,1024]{1,0:T(8,128)(2,1)S(1)}, bf16[512,1024]{1,0:T(8,128)(2,1)S(1)}, u32[]{:S(2)}, u32[]{:S(2)}) %collective-permute-start.25) | collective-permute-done | bytes 1048608 | tf_op jit(solution)/shard_map/ppermute | solution.py:61
  336.8 21.4 %collective-permute-done.29 = bf16[512,1024]{1,0:T(8,128)(2,1)S(1)} collective-permute-done((bf16[512,1024]{1,0:T(8,128)(2,1)S(1)}, bf16[512,1024]{1,0:T(8,128)(2,1)S(1)}, u32[]{:S(2)}, u32[]{:S(2)}) %collective-permute-start.29) | collective-permute-done | bytes 1048608 | tf_op jit(solution)/shard_map/ppermute | solution.py:61
  365.6 25.2 %expert_backward.2 = (bf16[512,1024]{1,0:T(8,128)(2,1)}, bf16[512,1024]{1,0:T(8,128)(2,1)}, bf16[4096,1024]{1,0:T(8,128)(2,1)}, bf16[4096,1024]{1,0:T(8,128)(2,1...) custom-call(bf16[512,1024]{1,0:T(8,128)(2,1)} %multiply_convert_fusion.1.refs_0_, ...), custom_call_target="tpu_custom_call" | custom-call | flops 1000 | bytes 1000 | tf_op jit(solution)/shard_map/expert_backward/pallas_call | solution.py:542
  390.8 20.6 %collective-permute-done.34.refs_0_ = bf16[512,1024]{1,0:T(8,128)(2,1)} collective-permute-done((bf16[512,1024]{1,0:T(8,128)(2,1)}, bf16[512,1024]{1,0:T(8,128)(2,1)}, u32[]{:S(2)}, u32[]{:S(2)}) %collective-permute-start.34) | collective-permute-done | bytes 1048608 | tf_op jit(solution)/shard_map/ppermute | solution.py:61
  414.1 6.8 collective-permute-done.36.refs_3_
  420.9 55.9 %expert_backward.3 = (bf16[512,1024]{1,0:T(8,128)(2,1)}, bf16[512,1024]{1,0:T(8,128)(2,1)}, bf16[512,1024]{1,0:T(8,128)(2,1)}, bf16[512,1024]{1,0:T(8,128)(2,1)}...) custom-call(bf16[512,1024]{1,0:T(8,128)(2,1)} %after.17.refs_0_, ...), custom_call_target="tpu_custom_call", output_to_operand_aliasing={{6}: (15, {}), {7}: (16, {}), {8}: (17, {}), {9}: (18, {}),... | custom-call | flops 1000 | bytes 1000 | tf_op jit(solution)/shard_map/expert_backward/pallas_call | solution.py:542
  477.5 15.3 %weight_grads.5 = (bf16[512,1024]{1,0:T(8,128)(2,1)}, bf16[512,1024]{1,0:T(8,128)(2,1)}) custom-call(bf16[4096,1024]{1,0:T(8,128)(2,1)} %get-tuple-element.128.refs_0_, bf16[4096,1024]{1,0:T(8,128)(2,1)} %get-tuple-element.129.refs_1_), custom_call_target="tpu_custom_call" | custom-call | flops 30000001024 | bytes 1000 | tf_op jit(solution)/shard_map/weight_grads/pallas_call | solution.py:644
  504.7 15.5 %weight_grads.6 = (bf16[512,1024]{1,0:T(8,128)(2,1)}, bf16[512,1024]{1,0:T(8,128)(2,1)}) custom-call(bf16[4096,1024]{1,0:T(8,128)(2,1)} %get-tuple-element.127.refs_0_, bf16[4096,1024]{1,0:T(8,128)(2,1)} %get-tuple-element.99.refs_0_.refs_1_.refs_2_, bf16[512,1024]{1,0:T(8,128)(2,1)} %get-tuple-element.130.refs_2_, ...), custom_call_target="tpu_custom_call" | custom-call | flops 30000001024 | bytes 1000 | tf_op jit(solution)/shard_map/weight_grads/pallas_call | solution.py:644
  522.1 15.2 %weight_grads.7 = (bf16[512,1024]{1,0:T(8,128)(2,1)}, bf16[512,1024]{1,0:T(8,128)(2,1)}) custom-call(bf16[4096,1024]{1,0:T(8,128)(2,1)} %get-tuple-element.126.refs_0_, bf16[4096,1024]{1,0:T(8,128)(2,1)} %get-tuple-element.99.refs_0_.refs_1_.refs_2_, bf16[512,1024]{1,0:T(8,128)(2,1)} %get-tuple-element.131.refs_2_, bf16[512,1024]{1,0:T(8,128)(2,1)} %add_convert_fusion.2.refs_3_), custom_call_target="tpu_custom_call" | custom-call | flops 30000001024 | bytes 1000 | tf_op jit(solution)/shard_map/weight_grads/pallas_call | solution.py:644
  537.4 7.6 collective-permute-done.44
  560.5 26.6 %attention_backward.1 = (bf16[1024,512]{1,0:T(8,128)(2,1)S(1)}, bf16[1024,512]{1,0:T(8,128)(2,1)S(1)}) custom-call(s32[1]{0:T(128)} %copy.118.refs_0_, bf16[1024,1024]{1,0:T(8,128)(2,1)} %pad_maximum_fusion.3.refs_1_, bf16[1024,512]{1,0:T(8,128)(2,1)} %copy-done.17, bf16[1024,1024]{1,0:T(8,128)(2,1)} %get-tuple-element.136.refs_3_, ...), custom_call_target="tpu_custom_call" | custom-call | flops 1000 | bytes 1000 | tf_op jit(solution)/shard_map/attention_backward/pallas_call | solution.py:333
  604.0 26.6 %weight_grads.8 = (bf16[512,1024]{1,0:T(8,128)(2,1)}, bf16[512,1024]{1,0:T(8,128)(2,1)}, bf16[512,1024]{1,0:T(8,128)(2,1)}, bf16[512,1024]{1,0:T(8,128)(2,1)}) custom-call(bf16[4096,1024]{1,0:T(8,128)(2,1)} %get-tuple-element.143.refs_0_, bf16[4096,1024]{1,0:T(8,128)(2,1)} %get-tuple-element.144.refs_1_, ...), custom_call_target="tpu_custom_call" | custom-call | flops 1000 | bytes 1000 | tf_op jit(solution)/shard_map/weight_grads/pallas_call | solution.py:644
  633.0 15.3 %weight_grads.9 = (bf16[512,1024]{1,0:T(8,128)(2,1)}, bf16[512,1024]{1,0:T(8,128)(2,1)}) custom-call(bf16[4096,1024]{1,0:T(8,128)(2,1)} %get-tuple-element.148.refs_0_, bf16[4096,1024]{1,0:T(8,128)(2,1)} %get-tuple-element.129.refs_1_, bf16[512,1024]{1,0:T(8,128)(2,1)} %get-tuple-element.149.refs_2_), custom_call_target="tpu_custom_call" | custom-call | flops 1000 | bytes 1000 | tf_op jit(solution)/shard_map/weight_grads/pallas_call | solution.py:644
  654.2 4.2 fusion.9
  660.1 13.6 %expert_update.3 = (f32[8,3,64,1024]{3,2,1,0:T(8,128)}, f32[8,3,4,64,64]{4,3,2,1,0:T(8,128)}, f32[8,3,4,256,256]{4,3,2,1,0:T(8,128)}, f32[8,3,64,1024]{3,2,1,0:T(8,128)}) custom-call(bf16[512,1024]{1,0:T(8,128)(2,1)} %get-tuple-element.151.refs_0_, bf16[512,1024]{1,0:T(8,128)(2,1)} %collective-permute-done.53.refs_1_, ...), custom_call_target="tpu_custom_call" | custom-call | flops 12000000000 | bytes 1000 | tf_op jit(solution)/shard_map/expert_update/pallas_call | solution.py:718
  677.8 13.6 %collective-permute-done.51 = bf16[2,2,64,1024]{3,2,0,1:T(8,128)(2,1)S(1)} collective-permute-done((bf16[2,2,64,1024]{3,2,0,1:T(8,128)(2,1)S(1)}, bf16[2,2,64,1024]{3,2,0,1:T(8,128)(2,1)S(1)}, u32[]{:S(2)}, u32[]{:S(2)}) %collective-permute-start.51) | collective-permute-done | bytes 524320 | tf_op jit(solution)/shard_map/ppermute | solution.py:61
  692.5 12.0 %collective-permute-done.49.refs_2_ = bf16[512,1024]{1,0:T(8,128)(2,1)} collective-permute-done((bf16[512,1024]{1,0:T(8,128)(2,1)S(1)}, bf16[512,1024]{1,0:T(8,128)(2,1)}, u32[]{:S(2)}, u32[]{:S(2)}) %collective-permute-start.49) | collective-permute-done | bytes 1048608 | tf_op jit(solution)/shard_map/ppermute | solution.py:61
  704.5 7.4 collective-permute-done.48.refs_1_
  712.0 13.1 %expert_update.4 = (f32[8,3,64,1024]{3,2,1,0:T(8,128)}, f32[8,3,4,64,64]{4,3,2,1,0:T(8,128)}, f32[8,3,4,256,256]{4,3,2,1,0:T(8,128)}, f32[8,3,64,1024]{3,2,1,0:T(8,128)}) custom-call(bf16[512,1024]{1,0:T(8,128)(2,1)} %get-tuple-element.146.refs_0_, ...), custom_call_target="tpu_custom_call", output_to_operand_aliasing={{0}: (11, {}), {1}: (12, {}), {2}: (13, {}), {3}: (14, {})} | custom-call | flops 12000000000 | bytes 1000 | tf_op jit(solution)/shard_map/expert_update/pallas_call | solution.py:718
  746.6 5.4 collective-permute-done.64
  752.7 14.0 %expert_update.5 = (f32[8,3,64,1024]{3,2,1,0:T(8,128)}, f32[8,3,4,64,64]{4,3,2,1,0:T(8,128)}, f32[8,3,4,256,256]{4,3,2,1,0:T(8,128)}, f32[8,3,64,1024]{3,2,1,0:T(8,128)}) custom-call(bf16[512,1024]{1,0:T(8,128)(2,1)} %get-tuple-element.161.refs_0_, ...), custom_call_target="tpu_custom_call", output_to_operand_aliasing={{0}: (11, {}), {1}: (12, {}), {2}: (13, {}), {3}: (14, {})} | custom-call | flops 12000000000 | bytes 1000 | tf_op jit(solution)/shard_map/expert_update/pallas_call | solution.py:718
  (407 shorter events, 189.9 us)
Async XLA Ops:
  7.2 745.4 %reduce-scatter.2.cloned.1.call-start = ((), (), s32[]{:S(2)}) async-start(), calls=%async_computation.1 | async-start | bytes 1114112 | tf_op jit(solution)/shard_map/reduce_scatter | solution.py:1077
  52.6 69.7 %collective-permute-start.12 = (bf16[4,3,64,1024]{3,2,1,0:T(8,128)(2,1)}, bf16[4,3,64,1024]{3,2,1,0:T(8,128)(2,1)S(1)}, u32[]{:S(2)}, u32[]{:S(2)}) collective-permute-start(bf16[4,3,64,1024]{3,2,1,0:T(8,128)(2,1)} %after.12), channel_id=1, source_target_pairs={{0,16},{2,18},{4,20},{6,22},{8,24},{10,26},{12,28},{14,30},{16,0},... | collective-permute-start | bytes 4718600 | tf_op jit(solution)/shard_map/ppermute | solution.py:61
  78.7 43.6 %collective-permute-start.13 = (bf16[3,3,64,1024]{3,2,1,0:T(8,128)(2,1)}, bf16[3,3,64,1024]{3,2,1,0:T(8,128)(2,1)S(1)}, u32[]{:S(2)}, u32[]{:S(2)}) collective-permute-start(bf16[3,3,64,1024]{3,2,1,0:T(8,128)(2,1)} %after.13), channel_id=1, source_target_pairs={{0,4},{2,6},{4,0},{6,2},{8,12},{10,14},{12,8},{14,10},{16,20},{18,... | collective-permute-start | bytes 3538952 | tf_op jit(solution)/shard_map/ppermute | solution.py:61
  81.9 34.6 %collective-permute-start.10 = (bf16[288,512]{1,0:T(8,128)(2,1)}, bf16[288,512]{1,0:T(8,128)(2,1)}, u32[]{:S(2)}, u32[]{:S(2)}) collective-permute-start(bf16[288,512]{1,0:T(8,128)(2,1)} %slice.107.refs_3_), channel_id=1, source_target_pairs={{0,4},{2,6},{4,0},{6,2},{8,12},{10,14},{12,8},{14,10},{16,20},{18,... | collective-permute-start | bytes 884744 | tf_op jit(solution)/shard_map/ppermute | solution.py:61
  82.4 34.1 %collective-permute-start.11 = (bf16[288,512]{1,0:T(8,128)(2,1)}, bf16[288,512]{1,0:T(8,128)(2,1)}, u32[]{:S(2)}, u32[]{:S(2)}) collective-permute-start(bf16[288,512]{1,0:T(8,128)(2,1)} %slice.107.refs_3_), channel_id=1, source_target_pairs={{0,6},{2,4},{4,2},{6,0},{8,14},{10,12},{12,10},{14,8},{16,22},{18,... | collective-permute-start | bytes 884744 | tf_op jit(solution)/shard_map/ppermute | solution.py:61
  83.9 32.6 %collective-permute-start.9 = (bf16[288,512]{1,0:T(8,128)(2,1)}, bf16[288,512]{1,0:T(8,128)(2,1)}, u32[]{:S(2)}, u32[]{:S(2)}) collective-permute-start(bf16[288,512]{1,0:T(8,128)(2,1)} %slice.107.refs_3_), channel_id=1, source_target_pairs={{0,2},{2,0},{4,6},{6,4},{8,10},{10,8},{12,14},{14,12},{16,18},{18,... | collective-permute-start | bytes 884744 | tf_op jit(solution)/shard_map/ppermute | solution.py:61
  131.8 46.2 %collective-permute-start.18 = (bf16[512,1024]{1,0:T(8,128)(2,1)S(1)}, bf16[512,1024]{1,0:T(8,128)(2,1)}, u32[]{:S(2)}, u32[]{:S(2)}) collective-permute-start(bf16[512,1024]{1,0:T(8,128)(2,1)S(1)} %multiply_convert_fusion.refs_0_), channel_id=1, source_target_pairs={{0,8},{2,10},{4,12},{6,14},{8,0},{10,2},{12,4},{14,6},{16,24},{18,... | collective-permute-start | bytes 3145736 | tf_op jit(solution)/shard_map/ppermute | solution.py:61
  131.9 47.5 %collective-permute-start.17 = (bf16[5,3,64,1024]{3,2,1,0:T(8,128)(2,1)}, bf16[5,3,64,1024]{3,2,1,0:T(8,128)(2,1)}, u32[]{:S(2)}, u32[]{:S(2)}) collective-permute-start(bf16[5,3,64,1024]{3,2,1,0:T(8,128)(2,1)} %get-tuple-element.98), channel_id=1, source_target_pairs={{0,4},{2,6},{4,0},{6,2},{8,12},{10,14},{12,8},{14,10},{16,20},{18,... | collective-permute-start | bytes 5898248 | tf_op jit(solution)/shard_map/ppermute | solution.py:61
  133.5 71.3 %collective-permute-start.16 = (bf16[4,3,64,1024]{3,2,1,0:T(8,128)(2,1)}, bf16[4,3,64,1024]{3,2,1,0:T(8,128)(2,1)}, u32[]{:S(2)}, u32[]{:S(2)}) collective-permute-start(bf16[4,3,64,1024]{3,2,1,0:T(8,128)(2,1)} %after.14), channel_id=1, source_target_pairs={{0,16},{2,18},{4,20},{6,22},{8,24},{10,26},{12,28},{14,30},{16,0},... | collective-permute-start | bytes 4718600 | tf_op jit(solution)/shard_map/ppermute | solution.py:61
  136.6 74.2 %collective-permute-start.20 = (bf16[4,3,64,1024]{3,2,1,0:T(8,128)(2,1)S(1)}, bf16[4,3,64,1024]{3,2,1,0:T(8,128)(2,1)}, u32[]{:S(2)}, u32[]{:S(2)}) collective-permute-start(bf16[4,3,64,1024]{3,2,1,0:T(8,128)(2,1)S(1)} %collective-permute-done.12.refs_7_.refs_3_.refs_9_.refs_11_), channel_id=1, source_target_pairs={{0,4},{2,6},{4,0},{6,2},{8,12},{10,14},{12,8},{14,10},{16,20},{18,... | collective-permute-start | bytes 4718600 | tf_op jit(solution)/shard_map/ppermute | solution.py:61
  137.1 67.7 %collective-permute-start.15 = (bf16[512,1024]{1,0:T(8,128)(2,1)S(1)}, bf16[512,1024]{1,0:T(8,128)(2,1)}, u32[]{:S(2)}, u32[]{:S(2)}) collective-permute-start(bf16[512,1024]{1,0:T(8,128)(2,1)S(1)} %multiply_convert_fusion.refs_0_), channel_id=1, source_target_pairs={{0,2},{2,0},{4,6},{6,4},{8,10},{10,8},{12,14},{14,12},{16,18},{18,... | collective-permute-start | bytes 3145736 | tf_op jit(solution)/shard_map/ppermute | solution.py:61
  178.0 32.9 %collective-permute-start.19 = (bf16[512,1024]{1,0:T(8,128)(2,1)}, bf16[512,1024]{1,0:T(8,128)(2,1)}, u32[]{:S(2)}, u32[]{:S(2)}) collective-permute-start(bf16[512,1024]{1,0:T(8,128)(2,1)} %collective-permute-done.18.refs_2_), channel_id=1, source_target_pairs={{0,2},{2,0},{4,6},{6,4},{8,10},{10,8},{12,14},{14,12},{16,18},{18,... | collective-permute-start | bytes 3145736 | tf_op jit(solution)/shard_map/ppermute | solution.py:61
  217.8 43.7 %collective-permute-start.22 = (bf16[4,3,64,1024]{3,2,1,0:T(8,128)(2,1)}, bf16[4,3,64,1024]{3,2,1,0:T(8,128)(2,1)S(1)}, u32[]{:S(2)}, u32[]{:S(2)}) collective-permute-start(bf16[4,3,64,1024]{3,2,1,0:T(8,128)(2,1)} %collective-permute-done.16.refs_1_.refs_4_.refs_10_.refs_12_), channel_id=1, source_target_pairs={{0,4},{2,6},{4,0},{6,2},{8,12},{10,14},{12,8},{14,10},{16,20},{18,... | collective-permute-start | bytes 4718600 | tf_op jit(solution)/shard_map/ppermute | solution.py:61
  312.8 45.3 %collective-permute-start.29 = (bf16[512,1024]{1,0:T(8,128)(2,1)S(1)}, bf16[512,1024]{1,0:T(8,128)(2,1)S(1)}, u32[]{:S(2)}, u32[]{:S(2)}) collective-permute-start(bf16[512,1024]{1,0:T(8,128)(2,1)S(1)} %add_convert_fusion.6), channel_id=1, source_target_pairs={{0,10},{2,8},{4,14},{6,12},{8,2},{10,0},{12,6},{14,4},{16,26},{18,... | collective-permute-start | bytes 3145736 | tf_op jit(solution)/shard_map/ppermute | solution.py:61
  362.1 28.7 %collective-permute-start.35 = (bf16[512,1024]{1,0:T(8,128)(2,1)}, bf16[512,1024]{1,0:T(8,128)(2,1)}, u32[]{:S(2)}, u32[]{:S(2)}) collective-permute-start(bf16[512,1024]{1,0:T(8,128)(2,1)} %multiply_convert_fusion.1.refs_0_), channel_id=1, source_target_pairs={{0,10},{2,8},{4,14},{6,12},{8,2},{10,0},{12,6},{14,4},{16,26},{18,... | collective-permute-start | bytes 3145736 | tf_op jit(solution)/shard_map/ppermute | solution.py:61
  364.7 46.7 %collective-permute-start.34 = (bf16[512,1024]{1,0:T(8,128)(2,1)}, bf16[512,1024]{1,0:T(8,128)(2,1)}, u32[]{:S(2)}, u32[]{:S(2)}) collective-permute-start(bf16[512,1024]{1,0:T(8,128)(2,1)} %multiply_convert_fusion.1.refs_0_), channel_id=1, source_target_pairs={{0,8},{2,10},{4,12},{6,14},{8,0},{10,2},{12,4},{14,6},{16,24},{18,... | collective-permute-start | bytes 3145736 | tf_op jit(solution)/shard_map/ppermute | solution.py:61
  365.0 46.4 %collective-permute-start.33 = (bf16[512,1024]{1,0:T(8,128)(2,1)}, bf16[512,1024]{1,0:T(8,128)(2,1)}, u32[]{:S(2)}, u32[]{:S(2)}) collective-permute-start(bf16[512,1024]{1,0:T(8,128)(2,1)} %multiply_convert_fusion.1.refs_0_), channel_id=1, source_target_pairs={{0,2},{2,0},{4,6},{6,4},{8,10},{10,8},{12,14},{14,12},{16,18},{18,... | collective-permute-start | bytes 3145736 | tf_op jit(solution)/shard_map/ppermute | solution.py:61
  413.6 132.8 %collective-permute-start.32 = (bf16[512,1024]{1,0:T(8,128)(2,1)}, bf16[512,1024]{1,0:T(8,128)(2,1)}, u32[]{:S(2)}, u32[]{:S(2)}) collective-permute-start(bf16[512,1024]{1,0:T(8,128)(2,1)} %get-tuple-element.114), channel_id=1, source_target_pairs={{0,1},{1,0},{2,3},{3,2},{4,5},{5,4},{6,7},{7,6},{8,9},{9,8},{10,11... | collective-permute-start | bytes 3145736 | tf_op jit(solution)/shard_map/ppermute | solution.py:66
  492.8 27.4 %collective-permute-start.43 = (bf16[512,1024]{1,0:T(8,128)(2,1)}, bf16[512,1024]{1,0:T(8,128)(2,1)S(1)}, u32[]{:S(2)}, u32[]{:S(2)}) collective-permute-start(bf16[512,1024]{1,0:T(8,128)(2,1)} %get-tuple-element.130.refs_2_), channel_id=1, source_target_pairs={{0,4},{2,6},{4,0},{6,2},{8,12},{10,14},{12,8},{14,10},{16,20},{18,... | collective-permute-start | bytes 3145736 | tf_op jit(solution)/shard_map/ppermute | solution.py:61
  497.0 49.4 %collective-permute-start.42 = (bf16[512,1024]{1,0:T(8,128)(2,1)S(1)}, bf16[512,1024]{1,0:T(8,128)(2,1)}, u32[]{:S(2)}, u32[]{:S(2)}) collective-permute-start(bf16[512,1024]{1,0:T(8,128)(2,1)S(1)} %add_convert_fusion.3.refs_5_), channel_id=1, source_target_pairs={{0,10},{2,8},{4,14},{6,12},{8,2},{10,0},{12,6},{14,4},{16,26},{18,... | collective-permute-start | bytes 3145736 | tf_op jit(solution)/shard_map/ppermute | solution.py:61
  502.2 44.3 %collective-permute-start.40 = (bf16[512,1024]{1,0:T(8,128)(2,1)}, bf16[512,1024]{1,0:T(8,128)(2,1)}, u32[]{:S(2)}, u32[]{:S(2)}) collective-permute-start(bf16[512,1024]{1,0:T(8,128)(2,1)} %add_convert_fusion.4.refs_4_), channel_id=1, source_target_pairs={{0,8},{2,10},{4,12},{6,14},{8,0},{10,2},{12,4},{14,6},{16,24},{18,... | collective-permute-start | bytes 3145736 | tf_op jit(solution)/shard_map/ppermute | solution.py:61
  503.9 42.5 %collective-permute-start.38 = (bf16[512,1024]{1,0:T(8,128)(2,1)}, bf16[512,1024]{1,0:T(8,128)(2,1)}, u32[]{:S(2)}, u32[]{:S(2)}) collective-permute-start(bf16[512,1024]{1,0:T(8,128)(2,1)} %add_convert_fusion.5.refs_3_), channel_id=1, source_target_pairs={{0,2},{2,0},{4,6},{6,4},{8,10},{10,8},{12,14},{14,12},{16,18},{18,... | collective-permute-start | bytes 3145736 | tf_op jit(solution)/shard_map/ppermute | solution.py:61
  553.6 45.4 %collective-permute-start.47 = (bf16[512,1024]{1,0:T(8,128)(2,1)}, bf16[512,1024]{1,0:T(8,128)(2,1)}, u32[]{:S(2)}, u32[]{:S(2)}) collective-permute-start(bf16[512,1024]{1,0:T(8,128)(2,1)} %get-tuple-element.133.refs_1_.refs_9_), channel_id=1, source_target_pairs={{0,4},{2,6},{4,0},{6,2},{8,12},{10,14},{12,8},{14,10},{16,20},{18,... | collective-permute-start | bytes 3145736 | tf_op jit(solution)/shard_map/ppermute | solution.py:61
  554.1 104.3 %collective-permute-start.55 = (bf16[512,1024]{1,0:T(8,128)(2,1)}, bf16[512,1024]{1,0:T(8,128)(2,1)}, u32[]{:S(2)}, u32[]{:S(2)}) collective-permute-start(bf16[512,1024]{1,0:T(8,128)(2,1)} %add_convert_fusion.2.refs_3_), channel_id=1, source_target_pairs={{0,16},{2,18},{4,20},{6,22},{8,24},{10,26},{12,28},{14,30},{16,0},... | collective-permute-start | bytes 3145736 | tf_op jit(solution)/shard_map/ppermute | solution.py:61
  556.5 102.6 %collective-permute-start.54 = (bf16[512,1024]{1,0:T(8,128)(2,1)}, bf16[512,1024]{1,0:T(8,128)(2,1)}, u32[]{:S(2)}, u32[]{:S(2)}) collective-permute-start(bf16[512,1024]{1,0:T(8,128)(2,1)} %add_convert_fusion.1.refs_2_.refs_10_), channel_id=1, source_target_pairs={{0,16},{2,18},{4,20},{6,22},{8,24},{10,26},{12,28},{14,30},{16,0},... | collective-permute-start | bytes 3145736 | tf_op jit(solution)/shard_map/ppermute | solution.py:61
  595.8 52.5 %collective-permute-start.50 = (bf16[2,2,2,64,1024]{4,3,0,2,1:T(8,128)(2,1)}, bf16[2,2,2,64,1024]{4,3,0,2,1:T(8,128)(2,1)S(1)}, u32[]{:S(2)}, u32[]{:S(2)}) collective-permute-start(bf16[2,2,2,64,1024]{4,3,0,2,1:T(8,128)(2,1)} %bitcast.64), channel_id=1, source_target_pairs={{0,2},{2,0},{4,6},{6,4},{8,10},{10,8},{12,14},{14,12},{16,18},{18,... | collective-permute-start | bytes 3145736 | tf_op jit(solution)/shard_map/ppermute | solution.py:61
  599.0 53.8 %collective-permute-start.46 = (bf16[512,1024]{1,0:T(8,128)(2,1)}, bf16[512,1024]{1,0:T(8,128)(2,1)}, u32[]{:S(2)}, u32[]{:S(2)}) collective-permute-start(bf16[512,1024]{1,0:T(8,128)(2,1)} %convolution_convert_fusion.2), channel_id=1, source_target_pairs={{0,1},{1,0},{2,3},{3,2},{4,5},{5,4},{6,7},{7,6},{8,9},{9,8},{10,11... | collective-permute-start | bytes 3145736 | tf_op jit(solution)/shard_map/ppermute | solution.py:66
  630.7 29.4 %collective-permute-start.53 = (bf16[512,1024]{1,0:T(8,128)(2,1)}, bf16[512,1024]{1,0:T(8,128)(2,1)}, u32[]{:S(2)}, u32[]{:S(2)}) collective-permute-start(bf16[512,1024]{1,0:T(8,128)(2,1)} %get-tuple-element.149.refs_2_), channel_id=1, source_target_pairs={{0,4},{2,6},{4,0},{6,2},{8,12},{10,14},{12,8},{14,10},{16,20},{18,... | collective-permute-start | bytes 3145736 | tf_op jit(solution)/shard_map/ppermute | solution.py:61
  648.3 56.2 %collective-permute-start.49 = (bf16[512,1024]{1,0:T(8,128)(2,1)S(1)}, bf16[512,1024]{1,0:T(8,128)(2,1)}, u32[]{:S(2)}, u32[]{:S(2)}) collective-permute-start(bf16[512,1024]{1,0:T(8,128)(2,1)S(1)} %copy-done.34), channel_id=1, source_target_pairs={{0,16},{2,18},{4,20},{6,22},{8,24},{10,26},{12,28},{14,30},{16,0},... | collective-permute-start | bytes 3145736 | tf_op jit(solution)/shard_map/ppermute | solution.py:61
  652.8 51.8 %collective-permute-start.52 = (bf16[512,1024]{1,0:T(8,128)(2,1)}, bf16[512,1024]{1,0:T(8,128)(2,1)S(1)}, u32[]{:S(2)}, u32[]{:S(2)}) collective-permute-start(bf16[512,1024]{1,0:T(8,128)(2,1)} %get-tuple-element.150), channel_id=1, source_target_pairs={{0,4},{2,6},{4,0},{6,2},{8,12},{10,14},{12,8},{14,10},{16,20},{18,... | collective-permute-start | bytes 3145736 | tf_op jit(solution)/shard_map/ppermute | solution.py:61
  658.4 53.5 %collective-permute-start.48 = (bf16[512,1024]{1,0:T(8,128)(2,1)}, bf16[512,1024]{1,0:T(8,128)(2,1)}, u32[]{:S(2)}, u32[]{:S(2)}) collective-permute-start(bf16[512,1024]{1,0:T(8,128)(2,1)} %get-tuple-element.147), channel_id=1, source_target_pairs={{0,4},{2,6},{4,0},{6,2},{8,12},{10,14},{12,8},{14,10},{16,20},{18,... | collective-permute-start | bytes 3145736 | tf_op jit(solution)/shard_map/ppermute | solution.py:61
  659.1 32.3 %collective-permute-start.51 = (bf16[2,2,64,1024]{3,2,0,1:T(8,128)(2,1)S(1)}, bf16[2,2,64,1024]{3,2,0,1:T(8,128)(2,1)S(1)}, u32[]{:S(2)}, u32[]{:S(2)}) collective-permute-start(bf16[2,2,64,1024]{3,2,0,1:T(8,128)(2,1)S(1)} %dynamic-slice_bitcast_fusion), channel_id=1, source_target_pairs={{0,8},{2,10},{4,12},{6,14},{8,0},{10,2},{12,4},{14,6},{16,24},{18,... | collective-permute-start | bytes 1572872 | tf_op jit(solution)/shard_map/ppermute | solution.py:61
  (119 other events, 1348.1 us)
Sparse Core Ops, SparseCore 0:
  633.1 79.4 reduce-scatter.1

commit v5 on v4

--- a/solution.py
+++ b/solution.py
@@ -66,11 +66,14 @@
     return lax.ppermute(values, "tensor", [(i, i ^ 1) for i in range(count)])
 
 
-def sum_everywhere(values):
+def sum_group(values):
     values = values + swap_core(values)
-    own = sum(values if mask == 0 else swap_dp(values, mask) for mask in TOKEN_MASKS)
+    return sum(values if mask == 0 else swap_dp(values, mask) for mask in TOKEN_MASKS)
+
+
+def sum_groups(values):
     masks = [m for m in range(1, lax.axis_size("dp")) if not m & TOKEN_MASKS[-1]]
-    return own + sum(swap_dp(own, mask) for mask in masks)
+    return values + sum(swap_dp(values, mask) for mask in masks)
 
 
 def in_order(own, other):
@@ -1089,13 +1092,16 @@
     }
     state = (expert_master, expert_left, expert_right, expert_left_root, expert_right_root)
     updated = expert_update(
-        0, parts[0], state, None, [far_down, far_gate, qkv_stages[0]]
-    )
-    updated = expert_update(1, parts[1], state, updated, [input_grad, qkv_stages[1]] + parts[2][1:2])
+        0, parts[0], state, None, [far_down, swap_core(far_gate), qkv_stages[0]] + parts[1][1:2]
+    )
     loss_row = jnp.full((1, D), loss_part)
     sums = jnp.concatenate([gain_attention[None], gain_mix[None], loss_row], axis=0)
-    sums = sum_everywhere(after(sums, updated[0]))
-    updated = expert_update(2, parts[2], state, updated, [sums, qkv_part, output_part])
+    sums = sum_group(after(sums, updated[0]))
+    updated = expert_update(
+        1, parts[1], state, updated, [input_grad, qkv_stages[2], sums] + parts[2][1:2]
+    )
+    sums = sum_groups(sums)
+    updated = expert_update(2, parts[2], state, updated, [output_part])
     expert_grad, expert_left_new, expert_right_new, expert_new = updated
     attention_grad, attention_left_new, attention_right_new, attention_new = attention_update(
         qkv_part,

time: 787 us -> 798 us (1.014)
    unnamed x176 -> x180, local copies, waits for them, and re-layouts: 16 us -> 18.1 us
  transfers between devices with their start and end apart: 66 -> 67, of which waited for: 27 -> 23; matrix products, arithmetic and copies ran while one was open for 8% -> 9% of each run, Pallas kernels for 38% -> 37%
where the time goes in v5:
time: 798 us; the launch traced here: 788 us
  Pallas kernels  353 us (44%)
  waiting for transfers between devices  237 us (30%)
  starting transfers between devices  65.8 us (8%)
  other arithmetic  60.1 us (8%)
  local copies, waits for them, and re-layouts  34.4 us (4%)
  between operations  24.9 us (3%)
  matrix products  12.9 us (2%)
    ppermute x48, waiting for transfers between devices, swap_dp(): return lax.ppermute(values, 'dp', [(i, i ^ mask) for i in range(count)])  221 us
    pallas_call x4, Pallas kernels, expert_call(): pl.pallas_call(kernel, grid=(steps,), in_specs=specs, out_specs=[fixed((r...  162 us
    pallas_call x5, Pallas kernels, weight_grads(): pl.pallas_call(functools.partial(weight_grad_kernel, count), grid=(2 * co...  88 us
    ppermute x48, starting transfers between devices, swap_dp(): return lax.ppermute(values, 'dp', [(i, i ^ mask) for i in range(count)])  62.2 us
    pallas_call x3, Pallas kernels, expert_update(): pl.pallas_call(functools.partial(expert_update_kernel, len(parts)), grid=...  40.2 us
    pallas_call x1, Pallas kernels, attention_backward(): pl.pallas_call(attention_backward_kernel, grid=(kv_here,), in_specs=[SCAL...  26.6 us
    pallas_call x1, Pallas kernels, attention_forward(): pl.pallas_call(attention_forward_kernel, grid=(kv_here,), in_specs=[SCALA...  22.9 us
    unnamed x180, local copies, waits for them, and re-layouts  18.1 us
  transfers between devices with their start and end apart: 67, of which 23 were waited for; matrix products, arithmetic and copies ran while one was open for 9% of the time, Pallas kernels for 37%

profile of v5, /device:TPU:0, one launch (start us, length us, event | category | flops | bytes accessed | tf_op | source)
XLA Modules:
  0.0 787.8 jit_solution(13810072705289412854)
XLA Ops:
  18.5 7.9 %collective-permute-done.1 = bf16[72,1536]{1,0:T(8,128)(2,1)S(1)} collective-permute-done((bf16[72,1536]{1,0:T(8,128)(2,1)S(1)}, bf16[72,1536]{1,0:T(8,128)(2,1)S(1)}, u32[]{:S(2)}, u32[]{:S(2)}) %collective-permute-start.1) | collective-permute-done | bytes 221216 | tf_op jit(solution)/shard_map/ppermute | solution.py:61
  31.5 8.5 %round_units.1 = (bf16[8,3,64,1024]{3,2,1,0:T(8,128)(2,1)}, bf16[4,3,64,1024]{3,2,1,0:T(8,128)(2,1)}, bf16[4,3,64,1024]{3,2,1,0:T(8,128)(2,1)}, bf16[3,3,64,1024]{3,2,1,0:T(8,128)(2,1)}, bf16[5,3,64,1024]{3,2,1,0:T(8,128)(2,1)}) custom-call(f32[8,3,64,1024]{3,2,1,0:T(8,128)} %refs_3_.5), custom_call_target="tpu_custom_call" | custom-call | flops 1000 | bytes 1000 | tf_op jit(solution)/shard_map/round_units/pallas_call | solution.py:316
  55.9 9.5 %collective-permute-done.6.refs_4_.refs_1_ = bf16[288,1024]{1,0:T(8,128)(2,1)} collective-permute-done((bf16[288,1024]{1,0:T(8,128)(2,1)S(1)}, bf16[288,1024]{1,0:T(8,128)(2,1)}, u32[]{:S(2)}, u32[]{:S(2)}) %collective-permute-start.6) | collective-permute-done | bytes 589856 | tf_op jit(solution)/shard_map/ppermute | solution.py:61
  65.4 11.6 %collective-permute-done.7.refs_5_.refs_2_ = bf16[288,1024]{1,0:T(8,128)(2,1)S(1)} collective-permute-done((bf16[288,1024]{1,0:T(8,128)(2,1)S(1)}, bf16[288,1024]{1,0:T(8,128)(2,1)S(1)}, u32[]{:S(2)}, u32[]{:S(2)}) %collective-permute-start.7) | collective-permute-done | bytes 589856 | tf_op jit(solution)/shard_map/ppermute | solution.py:61
  89.7 22.9 %attention_forward.1 = (bf16[1024,1024]{1,0:T(8,128)(2,1)}, bf16[1024,512]{1,0:T(8,128)(2,1)}, bf16[1024,512]{1,0:T(8,128)(2,1)}, bf16[1024,512]{1,0:T(8,128)(2,...) custom-call(s32[1]{0:T(128)} %copy.115.refs_0_, s32[4,4]{1,0:T(4,128)S(1)} %xor_multiply_fusion.refs_1_.refs_0_, ...), custom_call_target="tpu_custom_call" | custom-call | flops 1000 | bytes 1000 | tf_op jit(solution)/shard_map/attention_forward/pallas_call | solution.py:224
  116.5 5.8 collective-permute-done.12.refs_7_.refs_3_.refs_9_.refs_11_
  139.5 39.8 %collective-permute-done.18.refs_2_ = bf16[512,1024]{1,0:T(8,128)(2,1)} collective-permute-done((bf16[512,1024]{1,0:T(8,128)(2,1)}, bf16[512,1024]{1,0:T(8,128)(2,1)}, u32[]{:S(2)}, u32[]{:S(2)}) %collective-permute-start.18) | collective-permute-done | bytes 1048608 | tf_op jit(solution)/shard_map/ppermute | solution.py:61
  180.8 25.0 %collective-permute-done.16.refs_1_.refs_4_.refs_10_.refs_12_ = bf16[4,3,64,1024]{3,2,1,0:T(8,128)(2,1)} collective-permute-done((bf16[4,3,64,1024]{3,2,1,0:T(8,128)(2,1)}, bf16[4,3,64,1024]{3,2,1,0:T(8,128)(2,1)}, u32[]{:S(2)}, u32[]{:S(2)}) %collective-permute-start.16) | collective-permute-done | bytes 1572896 | tf_op jit(solution)/shard_map/ppermute | solution.py:61
  205.8 6.0 collective-permute-done.20.refs_1_.refs_5_.refs_11_.refs_13_
  224.0 39.5 %expert_first.1 = (bf16[4096,1024]{1,0:T(8,128)(2,1)}, bf16[4096,1024]{1,0:T(8,128)(2,1)}, bf16[4096,1024]{1,0:T(8,128)(2,1)}, bf16[4096,1024]{1,0:T(8,128)(2,1)}, bf16[4096,1024]{1,0:T(8,128)(2,1)}) custom-call(bf16[512,1024]{1,0:T(8,128)(2,1)} %multiply_convert_fusion.refs_0_, bf16[512,1024]{1,0:T(8,128)(2,1)} %after.15.refs_1_, ...), custom_call_target="tpu_custom_call" | custom-call | flops 25769803776 | bytes 1000 | tf_op jit(solution)/shard_map/expert_first/pallas_call | solution.py:545
  264.6 41.4 %expert_second.1 = (bf16[512,1024]{1,0:T(8,128)(2,1)}, bf16[512,1024]{1,0:T(8,128)(2,1)}, bf16[512,1024]{1,0:T(8,128)(2,1)}, bf16[512,1024]{1,0:T(8,128)(2,1)}, ...) custom-call(bf16[4096,1024]{1,0:T(8,128)(2,1)} %get-tuple-element.99, ...), custom_call_target="tpu_custom_call" | custom-call | flops 1000 | bytes 1000 | tf_op jit(solution)/shard_map/expert_second/pallas_call | solution.py:545
  327.5 8.4 %collective-permute-done.25 = bf16[512,1024]{1,0:T(8,128)(2,1)S(1)} collective-permute-done((bf16[512,1024]{1,0:T(8,128)(2,1)S(1)}, bf16[512,1024]{1,0:T(8,128)(2,1)S(1)}, u32[]{:S(2)}, u32[]{:S(2)}) %collective-permute-start.25) | collective-permute-done | bytes 1048608 | tf_op jit(solution)/shard_map/ppermute | solution.py:61
  338.7 21.4 %collective-permute-done.29 = bf16[512,1024]{1,0:T(8,128)(2,1)S(1)} collective-permute-done((bf16[512,1024]{1,0:T(8,128)(2,1)S(1)}, bf16[512,1024]{1,0:T(8,128)(2,1)S(1)}, u32[]{:S(2)}, u32[]{:S(2)}) %collective-permute-start.29) | collective-permute-done | bytes 1048608 | tf_op jit(solution)/shard_map/ppermute | solution.py:61
  367.6 25.2 %expert_backward.2 = (bf16[512,1024]{1,0:T(8,128)(2,1)}, bf16[512,1024]{1,0:T(8,128)(2,1)}, bf16[4096,1024]{1,0:T(8,128)(2,1)}, bf16[4096,1024]{1,0:T(8,128)(2,1...) custom-call(bf16[512,1024]{1,0:T(8,128)(2,1)} %multiply_convert_fusion.1.refs_0_, ...), custom_call_target="tpu_custom_call" | custom-call | flops 1000 | bytes 1000 | tf_op jit(solution)/shard_map/expert_backward/pallas_call | solution.py:545
  392.8 20.5 %collective-permute-done.34.refs_0_ = bf16[512,1024]{1,0:T(8,128)(2,1)} collective-permute-done((bf16[512,1024]{1,0:T(8,128)(2,1)}, bf16[512,1024]{1,0:T(8,128)(2,1)}, u32[]{:S(2)}, u32[]{:S(2)}) %collective-permute-start.34) | collective-permute-done | bytes 1048608 | tf_op jit(solution)/shard_map/ppermute | solution.py:61
  416.0 6.8 collective-permute-done.36.refs_3_
  422.8 55.9 %expert_backward.3 = (bf16[512,1024]{1,0:T(8,128)(2,1)}, bf16[512,1024]{1,0:T(8,128)(2,1)}, bf16[512,1024]{1,0:T(8,128)(2,1)}, bf16[512,1024]{1,0:T(8,128)(2,1)}...) custom-call(bf16[512,1024]{1,0:T(8,128)(2,1)} %after.17.refs_0_, ...), custom_call_target="tpu_custom_call", output_to_operand_aliasing={{6}: (15, {}), {7}: (16, {}), {8}: (17, {}), {9}: (18, {}),... | custom-call | flops 1000 | bytes 1000 | tf_op jit(solution)/shard_map/expert_backward/pallas_call | solution.py:545
  479.4 15.3 %weight_grads.5 = (bf16[512,1024]{1,0:T(8,128)(2,1)}, bf16[512,1024]{1,0:T(8,128)(2,1)}) custom-call(bf16[4096,1024]{1,0:T(8,128)(2,1)} %get-tuple-element.128.refs_0_, bf16[4096,1024]{1,0:T(8,128)(2,1)} %get-tuple-element.129.refs_1_), custom_call_target="tpu_custom_call" | custom-call | flops 30000001024 | bytes 1000 | tf_op jit(solution)/shard_map/weight_grads/pallas_call | solution.py:647
  506.7 15.5 %weight_grads.6 = (bf16[512,1024]{1,0:T(8,128)(2,1)}, bf16[512,1024]{1,0:T(8,128)(2,1)}) custom-call(bf16[4096,1024]{1,0:T(8,128)(2,1)} %get-tuple-element.127.refs_0_, bf16[4096,1024]{1,0:T(8,128)(2,1)} %get-tuple-element.99.refs_0_.refs_1_.refs_2_, bf16[512,1024]{1,0:T(8,128)(2,1)} %get-tuple-element.130.refs_2_, ...), custom_call_target="tpu_custom_call" | custom-call | flops 30000001024 | bytes 1000 | tf_op jit(solution)/shard_map/weight_grads/pallas_call | solution.py:647
  524.2 15.3 %weight_grads.7 = (bf16[512,1024]{1,0:T(8,128)(2,1)}, bf16[512,1024]{1,0:T(8,128)(2,1)}) custom-call(bf16[4096,1024]{1,0:T(8,128)(2,1)} %get-tuple-element.126.refs_0_, bf16[4096,1024]{1,0:T(8,128)(2,1)} %get-tuple-element.99.refs_0_.refs_1_.refs_2_, bf16[512,1024]{1,0:T(8,128)(2,1)} %get-tuple-element.131.refs_2_, bf16[512,1024]{1,0:T(8,128)(2,1)} %add_convert_fusion.2.refs_3_), custom_call_target="tpu_custom_call" | custom-call | flops 30000001024 | bytes 1000 | tf_op jit(solution)/shard_map/weight_grads/pallas_call | solution.py:647
  539.5 7.5 collective-permute-done.44
  562.0 26.6 %attention_backward.1 = (bf16[1024,512]{1,0:T(8,128)(2,1)S(1)}, bf16[1024,512]{1,0:T(8,128)(2,1)S(1)}) custom-call(s32[1]{0:T(128)} %copy.115.refs_0_, bf16[1024,1024]{1,0:T(8,128)(2,1)} %pad_maximum_fusion.3.refs_1_, bf16[1024,512]{1,0:T(8,128)(2,1)} %copy-done.16, bf16[1024,1024]{1,0:T(8,128)(2,1)} %get-tuple-element.136.refs_3_, ...), custom_call_target="tpu_custom_call" | custom-call | flops 1000 | bytes 1000 | tf_op jit(solution)/shard_map/attention_backward/pallas_call | solution.py:336
  610.8 26.6 %weight_grads.8 = (bf16[512,1024]{1,0:T(8,128)(2,1)}, bf16[512,1024]{1,0:T(8,128)(2,1)}, bf16[512,1024]{1,0:T(8,128)(2,1)}, bf16[512,1024]{1,0:T(8,128)(2,1)}) custom-call(bf16[4096,1024]{1,0:T(8,128)(2,1)} %get-tuple-element.143.refs_0_, bf16[4096,1024]{1,0:T(8,128)(2,1)} %get-tuple-element.144.refs_1_, ...), custom_call_target="tpu_custom_call" | custom-call | flops 1000 | bytes 1000 | tf_op jit(solution)/shard_map/weight_grads/pallas_call | solution.py:647
  638.0 15.3 %weight_grads.9 = (bf16[512,1024]{1,0:T(8,128)(2,1)}, bf16[512,1024]{1,0:T(8,128)(2,1)}) custom-call(bf16[4096,1024]{1,0:T(8,128)(2,1)} %get-tuple-element.154.refs_0_, bf16[4096,1024]{1,0:T(8,128)(2,1)} %get-tuple-element.129.refs_1_, bf16[512,1024]{1,0:T(8,128)(2,1)} %get-tuple-element.147.refs_2_), custom_call_target="tpu_custom_call" | custom-call | flops 1000 | bytes 1000 | tf_op jit(solution)/shard_map/weight_grads/pallas_call | solution.py:647
  659.2 4.2 fusion.9
  668.2 24.1 %collective-permute-done.53.refs_11_.refs_1_ = bf16[512,1024]{1,0:T(8,128)(2,1)S(1)} collective-permute-done((bf16[512,1024]{1,0:T(8,128)(2,1)}, bf16[512,1024]{1,0:T(8,128)(2,1)S(1)}, u32[]{:S(2)}, u32[]{:S(2)}) %collective-permute-start.53) | collective-permute-done | bytes 1048608 | tf_op jit(solution)/shard_map/ppermute | solution.py:61
  693.2 13.1 %expert_update.3 = (f32[8,3,64,1024]{3,2,1,0:T(8,128)}, f32[8,3,4,64,64]{4,3,2,1,0:T(8,128)}, f32[8,3,4,256,256]{4,3,2,1,0:T(8,128)}, f32[8,3,64,1024]{3,2,1,0:T(8,128)}) custom-call(bf16[512,1024]{1,0:T(8,128)(2,1)} %get-tuple-element.146.refs_0_, bf16[512,1024]{1,0:T(8,128)(2,1)} %copy-done.48, bf16[512,1024]{1,0:T(8,128)(2,1)} %collective-permute-done.49.refs_2_, ...), custom_call_target="tpu_custom_call" | custom-call | flops 12000000000 | bytes 1000 | tf_op jit(solution)/shard_map/expert_update/pallas_call | solution.py:721
  712.1 4.2 fusion.8.refs_8_
  722.2 19.2 %collective-permute-done.58 = f32[3,1024]{1,0:T(4,128)S(1)} collective-permute-done((f32[3,1024]{1,0:T(4,128)S(1)}, f32[3,1024]{1,0:T(4,128)S(1)}, u32[]{:S(2)}, u32[]{:S(2)}) %collective-permute-start.58) | collective-permute-done | bytes 12320 | tf_op jit(solution)/shard_map/ppermute | solution.py:61
  743.5 4.5 collective-permute-done.62
  749.5 13.1 %expert_update.4 = (f32[8,3,64,1024]{3,2,1,0:T(8,128)}, f32[8,3,4,64,64]{4,3,2,1,0:T(8,128)}, f32[8,3,4,256,256]{4,3,2,1,0:T(8,128)}, f32[8,3,64,1024]{3,2,1,0:T(8,128)}) custom-call(bf16[512,1024]{1,0:T(8,128)(2,1)} %get-tuple-element.157.refs_0_, ...), custom_call_target="tpu_custom_call", output_to_operand_aliasing={{0}: (12, {}), {1}: (13, {}), {2}: (14, {}), {3}: (15, {})} | custom-call | flops 12000000000 | bytes 1000 | tf_op jit(solution)/shard_map/expert_update/pallas_call | solution.py:721
  763.6 14.0 %expert_update.5 = (f32[8,3,64,1024]{3,2,1,0:T(8,128)}, f32[8,3,4,64,64]{4,3,2,1,0:T(8,128)}, f32[8,3,4,256,256]{4,3,2,1,0:T(8,128)}, f32[8,3,64,1024]{3,2,1,0:T(8,128)}) custom-call(bf16[512,1024]{1,0:T(8,128)(2,1)} %get-tuple-element.155.refs_0_, ...), custom_call_target="tpu_custom_call", output_to_operand_aliasing={{0}: (9, {}), {1}: (10, {}), {2}: (11, {}), {3}: (12, {})} | custom-call | flops 12000000000 | bytes 1000 | tf_op jit(solution)/shard_map/expert_update/pallas_call | solution.py:721
  (412 shorter events, 188.2 us)
Async XLA Ops:
  7.2 756.4 %reduce-scatter.2.cloned.1.call-start = ((), (), s32[]{:S(2)}) async-start(), calls=%async_computation.1 | async-start | bytes 1114112 | tf_op jit(solution)/shard_map/reduce_scatter | solution.py:1080
  52.6 69.7 %collective-permute-start.12 = (bf16[4,3,64,1024]{3,2,1,0:T(8,128)(2,1)}, bf16[4,3,64,1024]{3,2,1,0:T(8,128)(2,1)S(1)}, u32[]{:S(2)}, u32[]{:S(2)}) collective-permute-start(bf16[4,3,64,1024]{3,2,1,0:T(8,128)(2,1)} %after.12), channel_id=1, source_target_pairs={{0,16},{2,18},{4,20},{6,22},{8,24},{10,26},{12,28},{14,30},{16,0},... | collective-permute-start | bytes 4718600 | tf_op jit(solution)/shard_map/ppermute | solution.py:61
  78.7 43.5 %collective-permute-start.13 = (bf16[3,3,64,1024]{3,2,1,0:T(8,128)(2,1)}, bf16[3,3,64,1024]{3,2,1,0:T(8,128)(2,1)S(1)}, u32[]{:S(2)}, u32[]{:S(2)}) collective-permute-start(bf16[3,3,64,1024]{3,2,1,0:T(8,128)(2,1)} %after.13), channel_id=1, source_target_pairs={{0,4},{2,6},{4,0},{6,2},{8,12},{10,14},{12,8},{14,10},{16,20},{18,... | collective-permute-start | bytes 3538952 | tf_op jit(solution)/shard_map/ppermute | solution.py:61
  81.9 34.6 %collective-permute-start.10 = (bf16[288,512]{1,0:T(8,128)(2,1)}, bf16[288,512]{1,0:T(8,128)(2,1)}, u32[]{:S(2)}, u32[]{:S(2)}) collective-permute-start(bf16[288,512]{1,0:T(8,128)(2,1)} %slice.107.refs_3_), channel_id=1, source_target_pairs={{0,4},{2,6},{4,0},{6,2},{8,12},{10,14},{12,8},{14,10},{16,20},{18,... | collective-permute-start | bytes 884744 | tf_op jit(solution)/shard_map/ppermute | solution.py:61
  82.4 34.1 %collective-permute-start.11 = (bf16[288,512]{1,0:T(8,128)(2,1)}, bf16[288,512]{1,0:T(8,128)(2,1)}, u32[]{:S(2)}, u32[]{:S(2)}) collective-permute-start(bf16[288,512]{1,0:T(8,128)(2,1)} %slice.107.refs_3_), channel_id=1, source_target_pairs={{0,6},{2,4},{4,2},{6,0},{8,14},{10,12},{12,10},{14,8},{16,22},{18,... | collective-permute-start | bytes 884744 | tf_op jit(solution)/shard_map/ppermute | solution.py:61
  83.9 32.6 %collective-permute-start.9 = (bf16[288,512]{1,0:T(8,128)(2,1)}, bf16[288,512]{1,0:T(8,128)(2,1)}, u32[]{:S(2)}, u32[]{:S(2)}) collective-permute-start(bf16[288,512]{1,0:T(8,128)(2,1)} %slice.107.refs_3_), channel_id=1, source_target_pairs={{0,2},{2,0},{4,6},{6,4},{8,10},{10,8},{12,14},{14,12},{16,18},{18,... | collective-permute-start | bytes 884744 | tf_op jit(solution)/shard_map/ppermute | solution.py:61
  132.8 46.5 %collective-permute-start.18 = (bf16[512,1024]{1,0:T(8,128)(2,1)}, bf16[512,1024]{1,0:T(8,128)(2,1)}, u32[]{:S(2)}, u32[]{:S(2)}) collective-permute-start(bf16[512,1024]{1,0:T(8,128)(2,1)} %multiply_convert_fusion.refs_0_), channel_id=1, source_target_pairs={{0,8},{2,10},{4,12},{6,14},{8,0},{10,2},{12,4},{14,6},{16,24},{18,... | collective-permute-start | bytes 3145736 | tf_op jit(solution)/shard_map/ppermute | solution.py:61
  132.8 48.0 %collective-permute-start.17 = (bf16[5,3,64,1024]{3,2,1,0:T(8,128)(2,1)}, bf16[5,3,64,1024]{3,2,1,0:T(8,128)(2,1)}, u32[]{:S(2)}, u32[]{:S(2)}) collective-permute-start(bf16[5,3,64,1024]{3,2,1,0:T(8,128)(2,1)} %get-tuple-element.98), channel_id=1, source_target_pairs={{0,4},{2,6},{4,0},{6,2},{8,12},{10,14},{12,8},{14,10},{16,20},{18,... | collective-permute-start | bytes 5898248 | tf_op jit(solution)/shard_map/ppermute | solution.py:61
  134.4 71.4 %collective-permute-start.16 = (bf16[4,3,64,1024]{3,2,1,0:T(8,128)(2,1)}, bf16[4,3,64,1024]{3,2,1,0:T(8,128)(2,1)}, u32[]{:S(2)}, u32[]{:S(2)}) collective-permute-start(bf16[4,3,64,1024]{3,2,1,0:T(8,128)(2,1)} %after.14), channel_id=1, source_target_pairs={{0,16},{2,18},{4,20},{6,22},{8,24},{10,26},{12,28},{14,30},{16,0},... | collective-permute-start | bytes 4718600 | tf_op jit(solution)/shard_map/ppermute | solution.py:61
  137.6 74.2 %collective-permute-start.20 = (bf16[4,3,64,1024]{3,2,1,0:T(8,128)(2,1)S(1)}, bf16[4,3,64,1024]{3,2,1,0:T(8,128)(2,1)}, u32[]{:S(2)}, u32[]{:S(2)}) collective-permute-start(bf16[4,3,64,1024]{3,2,1,0:T(8,128)(2,1)S(1)} %collective-permute-done.12.refs_7_.refs_3_.refs_9_.refs_11_), channel_id=1, source_target_pairs={{0,4},{2,6},{4,0},{6,2},{8,12},{10,14},{12,8},{14,10},{16,20},{18,... | collective-permute-start | bytes 4718600 | tf_op jit(solution)/shard_map/ppermute | solution.py:61
  138.1 67.7 %collective-permute-start.15 = (bf16[512,1024]{1,0:T(8,128)(2,1)}, bf16[512,1024]{1,0:T(8,128)(2,1)}, u32[]{:S(2)}, u32[]{:S(2)}) collective-permute-start(bf16[512,1024]{1,0:T(8,128)(2,1)} %multiply_convert_fusion.refs_0_), channel_id=1, source_target_pairs={{0,2},{2,0},{4,6},{6,4},{8,10},{10,8},{12,14},{14,12},{16,18},{18,... | collective-permute-start | bytes 3145736 | tf_op jit(solution)/shard_map/ppermute | solution.py:61
  179.3 32.4 %collective-permute-start.19 = (bf16[512,1024]{1,0:T(8,128)(2,1)}, bf16[512,1024]{1,0:T(8,128)(2,1)S(1)}, u32[]{:S(2)}, u32[]{:S(2)}) collective-permute-start(bf16[512,1024]{1,0:T(8,128)(2,1)} %collective-permute-done.18.refs_2_), channel_id=1, source_target_pairs={{0,2},{2,0},{4,6},{6,4},{8,10},{10,8},{12,14},{14,12},{16,18},{18,... | collective-permute-start | bytes 3145736 | tf_op jit(solution)/shard_map/ppermute | solution.py:61
  219.7 43.8 %collective-permute-start.22 = (bf16[4,3,64,1024]{3,2,1,0:T(8,128)(2,1)}, bf16[4,3,64,1024]{3,2,1,0:T(8,128)(2,1)S(1)}, u32[]{:S(2)}, u32[]{:S(2)}) collective-permute-start(bf16[4,3,64,1024]{3,2,1,0:T(8,128)(2,1)} %collective-permute-done.16.refs_1_.refs_4_.refs_10_.refs_12_), channel_id=1, source_target_pairs={{0,4},{2,6},{4,0},{6,2},{8,12},{10,14},{12,8},{14,10},{16,20},{18,... | collective-permute-start | bytes 4718600 | tf_op jit(solution)/shard_map/ppermute | solution.py:61
  314.8 45.3 %collective-permute-start.29 = (bf16[512,1024]{1,0:T(8,128)(2,1)S(1)}, bf16[512,1024]{1,0:T(8,128)(2,1)S(1)}, u32[]{:S(2)}, u32[]{:S(2)}) collective-permute-start(bf16[512,1024]{1,0:T(8,128)(2,1)S(1)} %add_convert_fusion.6), channel_id=1, source_target_pairs={{0,10},{2,8},{4,14},{6,12},{8,2},{10,0},{12,6},{14,4},{16,26},{18,... | collective-permute-start | bytes 3145736 | tf_op jit(solution)/shard_map/ppermute | solution.py:61
  364.1 28.7 %collective-permute-start.35 = (bf16[512,1024]{1,0:T(8,128)(2,1)}, bf16[512,1024]{1,0:T(8,128)(2,1)}, u32[]{:S(2)}, u32[]{:S(2)}) collective-permute-start(bf16[512,1024]{1,0:T(8,128)(2,1)} %multiply_convert_fusion.1.refs_0_), channel_id=1, source_target_pairs={{0,10},{2,8},{4,14},{6,12},{8,2},{10,0},{12,6},{14,4},{16,26},{18,... | collective-permute-start | bytes 3145736 | tf_op jit(solution)/shard_map/ppermute | solution.py:61
  366.7 46.7 %collective-permute-start.34 = (bf16[512,1024]{1,0:T(8,128)(2,1)}, bf16[512,1024]{1,0:T(8,128)(2,1)}, u32[]{:S(2)}, u32[]{:S(2)}) collective-permute-start(bf16[512,1024]{1,0:T(8,128)(2,1)} %multiply_convert_fusion.1.refs_0_), channel_id=1, source_target_pairs={{0,8},{2,10},{4,12},{6,14},{8,0},{10,2},{12,4},{14,6},{16,24},{18,... | collective-permute-start | bytes 3145736 | tf_op jit(solution)/shard_map/ppermute | solution.py:61
  367.0 46.4 %collective-permute-start.33 = (bf16[512,1024]{1,0:T(8,128)(2,1)}, bf16[512,1024]{1,0:T(8,128)(2,1)}, u32[]{:S(2)}, u32[]{:S(2)}) collective-permute-start(bf16[512,1024]{1,0:T(8,128)(2,1)} %multiply_convert_fusion.1.refs_0_), channel_id=1, source_target_pairs={{0,2},{2,0},{4,6},{6,4},{8,10},{10,8},{12,14},{14,12},{16,18},{18,... | collective-permute-start | bytes 3145736 | tf_op jit(solution)/shard_map/ppermute | solution.py:61
  415.5 133.0 %collective-permute-start.32 = (bf16[512,1024]{1,0:T(8,128)(2,1)}, bf16[512,1024]{1,0:T(8,128)(2,1)}, u32[]{:S(2)}, u32[]{:S(2)}) collective-permute-start(bf16[512,1024]{1,0:T(8,128)(2,1)} %get-tuple-element.114), channel_id=1, source_target_pairs={{0,1},{1,0},{2,3},{3,2},{4,5},{5,4},{6,7},{7,6},{8,9},{9,8},{10,11... | collective-permute-start | bytes 3145736 | tf_op jit(solution)/shard_map/ppermute | solution.py:66
  498.9 49.5 %collective-permute-start.42 = (bf16[512,1024]{1,0:T(8,128)(2,1)S(1)}, bf16[512,1024]{1,0:T(8,128)(2,1)}, u32[]{:S(2)}, u32[]{:S(2)}) collective-permute-start(bf16[512,1024]{1,0:T(8,128)(2,1)S(1)} %add_convert_fusion.3.refs_5_), channel_id=1, source_target_pairs={{0,10},{2,8},{4,14},{6,12},{8,2},{10,0},{12,6},{14,4},{16,26},{18,... | collective-permute-start | bytes 3145736 | tf_op jit(solution)/shard_map/ppermute | solution.py:61
  504.2 44.3 %collective-permute-start.40 = (bf16[512,1024]{1,0:T(8,128)(2,1)}, bf16[512,1024]{1,0:T(8,128)(2,1)}, u32[]{:S(2)}, u32[]{:S(2)}) collective-permute-start(bf16[512,1024]{1,0:T(8,128)(2,1)} %add_convert_fusion.4.refs_4_), channel_id=1, source_target_pairs={{0,8},{2,10},{4,12},{6,14},{8,0},{10,2},{12,4},{14,6},{16,24},{18,... | collective-permute-start | bytes 3145736 | tf_op jit(solution)/shard_map/ppermute | solution.py:61
  505.8 42.7 %collective-permute-start.38 = (bf16[512,1024]{1,0:T(8,128)(2,1)}, bf16[512,1024]{1,0:T(8,128)(2,1)}, u32[]{:S(2)}, u32[]{:S(2)}) collective-permute-start(bf16[512,1024]{1,0:T(8,128)(2,1)} %add_convert_fusion.5.refs_3_), channel_id=1, source_target_pairs={{0,2},{2,0},{4,6},{6,4},{8,10},{10,8},{12,14},{14,12},{16,18},{18,... | collective-permute-start | bytes 3145736 | tf_op jit(solution)/shard_map/ppermute | solution.py:61
  555.6 50.1 %collective-permute-start.47 = (bf16[512,1024]{1,0:T(8,128)(2,1)}, bf16[512,1024]{1,0:T(8,128)(2,1)}, u32[]{:S(2)}, u32[]{:S(2)}) collective-permute-start(bf16[512,1024]{1,0:T(8,128)(2,1)} %get-tuple-element.133.refs_1_.refs_9_), channel_id=1, source_target_pairs={{0,4},{2,6},{4,0},{6,2},{8,12},{10,14},{12,8},{14,10},{16,20},{18,... | collective-permute-start | bytes 3145736 | tf_op jit(solution)/shard_map/ppermute | solution.py:61
  556.1 97.1 %collective-permute-start.49 = (bf16[512,1024]{1,0:T(8,128)(2,1)}, bf16[512,1024]{1,0:T(8,128)(2,1)}, u32[]{:S(2)}, u32[]{:S(2)}) collective-permute-start(bf16[512,1024]{1,0:T(8,128)(2,1)} %add_convert_fusion.1.refs_2_.refs_10_), channel_id=1, source_target_pairs={{0,16},{2,18},{4,20},{6,22},{8,24},{10,26},{12,28},{14,30},{16,0},... | collective-permute-start | bytes 3145736 | tf_op jit(solution)/shard_map/ppermute | solution.py:61
  597.3 57.5 %collective-permute-start.52 = (bf16[2,2,2,64,1024]{4,3,0,2,1:T(8,128)(2,1)}, bf16[2,2,2,64,1024]{4,3,0,2,1:T(8,128)(2,1)}, u32[]{:S(2)}, u32[]{:S(2)}) collective-permute-start(bf16[2,2,2,64,1024]{4,3,0,2,1:T(8,128)(2,1)} %bitcast.64), channel_id=1, source_target_pairs={{0,2},{2,0},{4,6},{6,4},{8,10},{10,8},{12,14},{14,12},{16,18},{18,... | collective-permute-start | bytes 3145736 | tf_op jit(solution)/shard_map/ppermute | solution.py:61
  599.4 64.6 %collective-permute-start.50 = (bf16[512,1024]{1,0:T(8,128)(2,1)}, bf16[512,1024]{1,0:T(8,128)(2,1)S(1)}, u32[]{:S(2)}, u32[]{:S(2)}) collective-permute-start(bf16[512,1024]{1,0:T(8,128)(2,1)} %add_convert_fusion.2.refs_3_), channel_id=1, source_target_pairs={{0,16},{2,18},{4,20},{6,22},{8,24},{10,26},{12,28},{14,30},{16,0},... | collective-permute-start | bytes 3145736 | tf_op jit(solution)/shard_map/ppermute | solution.py:61
  605.8 52.8 %collective-permute-start.46 = (bf16[512,1024]{1,0:T(8,128)(2,1)}, bf16[512,1024]{1,0:T(8,128)(2,1)}, u32[]{:S(2)}, u32[]{:S(2)}) collective-permute-start(bf16[512,1024]{1,0:T(8,128)(2,1)} %convolution_convert_fusion.2), channel_id=1, source_target_pairs={{0,1},{1,0},{2,3},{3,2},{4,5},{5,4},{6,7},{7,6},{8,9},{9,8},{10,11... | collective-permute-start | bytes 3145736 | tf_op jit(solution)/shard_map/ppermute | solution.py:66
  637.5 30.7 %collective-permute-start.48 = (bf16[512,1024]{1,0:T(8,128)(2,1)}, bf16[512,1024]{1,0:T(8,128)(2,1)S(1)}, u32[]{:S(2)}, u32[]{:S(2)}) collective-permute-start(bf16[512,1024]{1,0:T(8,128)(2,1)} %get-tuple-element.147.refs_2_), channel_id=1, source_target_pairs={{0,4},{2,6},{4,0},{6,2},{8,12},{10,14},{12,8},{14,10},{16,20},{18,... | collective-permute-start | bytes 3145736 | tf_op jit(solution)/shard_map/ppermute | solution.py:61
  653.3 39.0 %collective-permute-start.53 = (bf16[512,1024]{1,0:T(8,128)(2,1)}, bf16[512,1024]{1,0:T(8,128)(2,1)S(1)}, u32[]{:S(2)}, u32[]{:S(2)}) collective-permute-start(bf16[512,1024]{1,0:T(8,128)(2,1)} %get-tuple-element.148), channel_id=1, source_target_pairs={{0,4},{2,6},{4,0},{6,2},{8,12},{10,14},{12,8},{14,10},{16,20},{18,... | collective-permute-start | bytes 3145736 | tf_op jit(solution)/shard_map/ppermute | solution.py:61
  654.8 37.5 %collective-permute-start.51 = (bf16[512,1024]{1,0:T(8,128)(2,1)}, bf16[512,1024]{1,0:T(8,128)(2,1)}, u32[]{:S(2)}, u32[]{:S(2)}) collective-permute-start(bf16[512,1024]{1,0:T(8,128)(2,1)} %collective-permute-done.49.refs_2_), channel_id=1, source_target_pairs={{0,1},{1,0},{2,3},{3,2},{4,5},{5,4},{6,7},{7,6},{8,9},{9,8},{10,11... | collective-permute-start | bytes 3145736 | tf_op jit(solution)/shard_map/ppermute | solution.py:66
  658.6 89.9 %collective-permute-start.65 = (bf16[512,1024]{1,0:T(8,128)(2,1)}, bf16[512,1024]{1,0:T(8,128)(2,1)}, u32[]{:S(2)}, u32[]{:S(2)}) collective-permute-start(bf16[512,1024]{1,0:T(8,128)(2,1)} %add_convert_fusion.refs_5_), channel_id=1, source_target_pairs={{0,16},{2,18},{4,20},{6,22},{8,24},{10,26},{12,28},{14,30},{16,0},... | collective-permute-start | bytes 3145736 | tf_op jit(solution)/shard_map/ppermute | solution.py:61
  664.1 54.6 %collective-permute-start.61 = (bf16[2,2,64,1024]{3,2,0,1:T(8,128)(2,1)}, bf16[2,2,64,1024]{3,2,0,1:T(8,128)(2,1)}, u32[]{:S(2)}, u32[]{:S(2)}) collective-permute-start(bf16[2,2,64,1024]{3,2,0,1:T(8,128)(2,1)} %dynamic-slice_bitcast_fusion), channel_id=1, source_target_pairs={{0,8},{2,10},{4,12},{6,14},{8,0},{10,2},{12,4},{14,6},{16,24},{18,... | collective-permute-start | bytes 1572872 | tf_op jit(solution)/shard_map/ppermute | solution.py:61
  716.2 32.3 %collective-permute-start.64 = (bf16[512,1024]{1,0:T(8,128)(2,1)S(1)}, bf16[512,1024]{1,0:T(8,128)(2,1)S(1)}, u32[]{:S(2)}, u32[]{:S(2)}) collective-permute-start(bf16[512,1024]{1,0:T(8,128)(2,1)S(1)} %copy-done.85), channel_id=1, source_target_pairs={{0,4},{2,6},{4,0},{6,2},{8,12},{10,14},{12,8},{14,10},{16,20},{18,... | collective-permute-start | bytes 3145736 | tf_op jit(solution)/shard_map/ppermute | solution.py:61
  (122 other events, 1414.9 us)
Sparse Core Ops, SparseCore 0:
  611.0 77.3 reduce-scatter.1

commit v6 on v4

--- a/solution.py
+++ b/solution.py
@@ -1091,11 +1091,11 @@
     updated = expert_update(
         0, parts[0], state, None, [far_down, far_gate, qkv_stages[0]]
     )
-    updated = expert_update(1, parts[1], state, updated, [input_grad, qkv_stages[1]] + parts[2][1:2])
+    updated = expert_update(2, parts[2], state, updated, [input_grad, qkv_stages[1]] + parts[1][1:2])
+    updated = expert_update(1, parts[1], state, updated)
     loss_row = jnp.full((1, D), loss_part)
     sums = jnp.concatenate([gain_attention[None], gain_mix[None], loss_row], axis=0)
-    sums = sum_everywhere(after(sums, updated[0]))
-    updated = expert_update(2, parts[2], state, updated, [sums, qkv_part, output_part])
+    sums = sum_everywhere(after(sums, updated[0], output_part))
     expert_grad, expert_left_new, expert_right_new, expert_new = updated
     attention_grad, attention_left_new, attention_right_new, attention_new = attention_update(
         qkv_part,

time: 787 us -> 778 us (0.989)
  waiting for transfers between devices: 232 us -> 222 us
    ppermute x48, waiting for transfers between devices: 216 us -> 206 us  [swap_dp(): return lax.ppermute(values, 'dp', [(i, i ^ mask) for i in range(count)])]
    unnamed x176 -> x170, local copies, waits for them, and re-layouts: 16 us -> 17.7 us
  transfers between devices with their start and end apart: 66 -> 66, of which waited for: 27 -> 24; matrix products, arithmetic and copies ran while one was open for 8% -> 8% of each run, Pallas kernels for 38% -> 40%
where the time goes in v6:
time: 778 us; the launch traced here: 768 us
  Pallas kernels  352 us (45%)
  waiting for transfers between devices  222 us (29%)
  starting transfers between devices  68 us (9%)
  other arithmetic  56.3 us (7%)
  local copies, waits for them, and re-layouts  32.8 us (4%)
  between operations  25.2 us (3%)
  matrix products  11.2 us (1%)
    ppermute x48, waiting for transfers between devices, swap_dp(): return lax.ppermute(values, 'dp', [(i, i ^ mask) for i in range(count)])  206 us
    pallas_call x4, Pallas kernels, expert_call(): pl.pallas_call(kernel, grid=(steps,), in_specs=specs, out_specs=[fixed((r...  162 us
    pallas_call x5, Pallas kernels, weight_grads(): pl.pallas_call(functools.partial(weight_grad_kernel, count), grid=(2 * co...  88 us
    ppermute x48, starting transfers between devices, swap_dp(): return lax.ppermute(values, 'dp', [(i, i ^ mask) for i in range(count)])  64.5 us
    pallas_call x3, Pallas kernels, expert_update(): pl.pallas_call(functools.partial(expert_update_kernel, len(parts)), grid=...  39.8 us
    pallas_call x1, Pallas kernels, attention_backward(): pl.pallas_call(attention_backward_kernel, grid=(kv_here,), in_specs=[SCAL...  26.6 us
    pallas_call x1, Pallas kernels, attention_forward(): pl.pallas_call(attention_forward_kernel, grid=(kv_here,), in_specs=[SCALA...  22.9 us
    unnamed x170, local copies, waits for them, and re-layouts  17.7 us
  transfers between devices with their start and end apart: 66, of which 24 were waited for; matrix products, arithmetic and copies ran while one was open for 8% of the time, Pallas kernels for 40%

profile of v6, /device:TPU:0, one launch (start us, length us, event | category | flops | bytes accessed | tf_op | source)
XLA Modules:
  0.0 767.7 jit_solution(10121150983042188446)
XLA Ops:
  12.2 4.1 collective-permute-start.1
  18.5 8.0 %collective-permute-done.1 = bf16[72,1536]{1,0:T(8,128)(2,1)S(1)} collective-permute-done((bf16[72,1536]{1,0:T(8,128)(2,1)S(1)}, bf16[72,1536]{1,0:T(8,128)(2,1)S(1)}, u32[]{:S(2)}, u32[]{:S(2)}) %collective-permute-start.1) | collective-permute-done | bytes 221216 | tf_op jit(solution)/shard_map/ppermute | solution.py:61
  31.5 8.5 %round_units.1 = (bf16[8,3,64,1024]{3,2,1,0:T(8,128)(2,1)}, bf16[4,3,64,1024]{3,2,1,0:T(8,128)(2,1)}, bf16[4,3,64,1024]{3,2,1,0:T(8,128)(2,1)}, bf16[3,3,64,1024]{3,2,1,0:T(8,128)(2,1)}, bf16[5,3,64,1024]{3,2,1,0:T(8,128)(2,1)}) custom-call(f32[8,3,64,1024]{3,2,1,0:T(8,128)} %refs_3_.5), custom_call_target="tpu_custom_call" | custom-call | flops 1000 | bytes 1000 | tf_op jit(solution)/shard_map/round_units/pallas_call | solution.py:313
  55.9 9.5 %collective-permute-done.6.refs_4_.refs_1_ = bf16[288,1024]{1,0:T(8,128)(2,1)} collective-permute-done((bf16[288,1024]{1,0:T(8,128)(2,1)S(1)}, bf16[288,1024]{1,0:T(8,128)(2,1)}, u32[]{:S(2)}, u32[]{:S(2)}) %collective-permute-start.6) | collective-permute-done | bytes 589856 | tf_op jit(solution)/shard_map/ppermute | solution.py:61
  65.4 11.6 %collective-permute-done.7.refs_5_.refs_2_ = bf16[288,1024]{1,0:T(8,128)(2,1)S(1)} collective-permute-done((bf16[288,1024]{1,0:T(8,128)(2,1)S(1)}, bf16[288,1024]{1,0:T(8,128)(2,1)S(1)}, u32[]{:S(2)}, u32[]{:S(2)}) %collective-permute-start.7) | collective-permute-done | bytes 589856 | tf_op jit(solution)/shard_map/ppermute | solution.py:61
  89.7 22.9 %attention_forward.1 = (bf16[1024,1024]{1,0:T(8,128)(2,1)}, bf16[1024,512]{1,0:T(8,128)(2,1)}, bf16[1024,512]{1,0:T(8,128)(2,1)}, bf16[1024,512]{1,0:T(8,128)(2,...) custom-call(s32[1]{0:T(128)} %copy.118.refs_0_, s32[4,4]{1,0:T(4,128)S(1)} %xor_multiply_fusion.refs_1_.refs_0_, ...), custom_call_target="tpu_custom_call" | custom-call | flops 1000 | bytes 1000 | tf_op jit(solution)/shard_map/attention_forward/pallas_call | solution.py:221
  116.5 5.8 collective-permute-done.12.refs_7_.refs_3_.refs_9_.refs_11_
  138.6 39.4 %collective-permute-done.18.refs_2_ = bf16[512,1024]{1,0:T(8,128)(2,1)} collective-permute-done((bf16[512,1024]{1,0:T(8,128)(2,1)S(1)}, bf16[512,1024]{1,0:T(8,128)(2,1)}, u32[]{:S(2)}, u32[]{:S(2)}) %collective-permute-start.18) | collective-permute-done | bytes 1048608 | tf_op jit(solution)/shard_map/ppermute | solution.py:61
  179.4 25.4 %collective-permute-done.16.refs_1_.refs_4_.refs_10_.refs_12_ = bf16[4,3,64,1024]{3,2,1,0:T(8,128)(2,1)} collective-permute-done((bf16[4,3,64,1024]{3,2,1,0:T(8,128)(2,1)}, bf16[4,3,64,1024]{3,2,1,0:T(8,128)(2,1)}, u32[]{:S(2)}, u32[]{:S(2)}) %collective-permute-start.16) | collective-permute-done | bytes 1572896 | tf_op jit(solution)/shard_map/ppermute | solution.py:61
  204.8 6.0 collective-permute-done.20.refs_1_.refs_5_.refs_11_.refs_13_
  222.1 39.5 %expert_first.1 = (bf16[4096,1024]{1,0:T(8,128)(2,1)}, bf16[4096,1024]{1,0:T(8,128)(2,1)}, bf16[4096,1024]{1,0:T(8,128)(2,1)}, bf16[4096,1024]{1,0:T(8,128)(2,1)}, bf16[4096,1024]{1,0:T(8,128)(2,1)}) custom-call(bf16[512,1024]{1,0:T(8,128)(2,1)} %copy-done.42, bf16[512,1024]{1,0:T(8,128)(2,1)} %after.15.refs_1_, ...), custom_call_target="tpu_custom_call" | custom-call | flops 25769803776 | bytes 1000 | tf_op jit(solution)/shard_map/expert_first/pallas_call | solution.py:542
  262.8 41.4 %expert_second.1 = (bf16[512,1024]{1,0:T(8,128)(2,1)}, bf16[512,1024]{1,0:T(8,128)(2,1)}, bf16[512,1024]{1,0:T(8,128)(2,1)}, bf16[512,1024]{1,0:T(8,128)(2,1)}, ...) custom-call(bf16[4096,1024]{1,0:T(8,128)(2,1)} %get-tuple-element.99, ...), custom_call_target="tpu_custom_call" | custom-call | flops 1000 | bytes 1000 | tf_op jit(solution)/shard_map/expert_second/pallas_call | solution.py:542
  325.8 8.3 %collective-permute-done.25 = bf16[512,1024]{1,0:T(8,128)(2,1)S(1)} collective-permute-done((bf16[512,1024]{1,0:T(8,128)(2,1)S(1)}, bf16[512,1024]{1,0:T(8,128)(2,1)S(1)}, u32[]{:S(2)}, u32[]{:S(2)}) %collective-permute-start.25) | collective-permute-done | bytes 1048608 | tf_op jit(solution)/shard_map/ppermute | solution.py:61
  336.8 21.4 %collective-permute-done.29 = bf16[512,1024]{1,0:T(8,128)(2,1)S(1)} collective-permute-done((bf16[512,1024]{1,0:T(8,128)(2,1)S(1)}, bf16[512,1024]{1,0:T(8,128)(2,1)S(1)}, u32[]{:S(2)}, u32[]{:S(2)}) %collective-permute-start.29) | collective-permute-done | bytes 1048608 | tf_op jit(solution)/shard_map/ppermute | solution.py:61
  365.7 25.2 %expert_backward.2 = (bf16[512,1024]{1,0:T(8,128)(2,1)}, bf16[512,1024]{1,0:T(8,128)(2,1)}, bf16[4096,1024]{1,0:T(8,128)(2,1)}, bf16[4096,1024]{1,0:T(8,128)(2,1...) custom-call(bf16[512,1024]{1,0:T(8,128)(2,1)} %multiply_convert_fusion.1.refs_0_, ...), custom_call_target="tpu_custom_call" | custom-call | flops 1000 | bytes 1000 | tf_op jit(solution)/shard_map/expert_backward/pallas_call | solution.py:542
  390.9 20.6 %collective-permute-done.34.refs_0_ = bf16[512,1024]{1,0:T(8,128)(2,1)} collective-permute-done((bf16[512,1024]{1,0:T(8,128)(2,1)}, bf16[512,1024]{1,0:T(8,128)(2,1)}, u32[]{:S(2)}, u32[]{:S(2)}) %collective-permute-start.34) | collective-permute-done | bytes 1048608 | tf_op jit(solution)/shard_map/ppermute | solution.py:61
  414.2 6.8 collective-permute-done.36.refs_3_
  420.9 55.9 %expert_backward.3 = (bf16[512,1024]{1,0:T(8,128)(2,1)}, bf16[512,1024]{1,0:T(8,128)(2,1)}, bf16[512,1024]{1,0:T(8,128)(2,1)}, bf16[512,1024]{1,0:T(8,128)(2,1)}...) custom-call(bf16[512,1024]{1,0:T(8,128)(2,1)} %after.17.refs_0_, ...), custom_call_target="tpu_custom_call", output_to_operand_aliasing={{6}: (15, {}), {7}: (16, {}), {8}: (17, {}), {9}: (18, {}),... | custom-call | flops 1000 | bytes 1000 | tf_op jit(solution)/shard_map/expert_backward/pallas_call | solution.py:542
  477.6 15.3 %weight_grads.5 = (bf16[512,1024]{1,0:T(8,128)(2,1)}, bf16[512,1024]{1,0:T(8,128)(2,1)}) custom-call(bf16[4096,1024]{1,0:T(8,128)(2,1)} %get-tuple-element.128.refs_0_, bf16[4096,1024]{1,0:T(8,128)(2,1)} %get-tuple-element.129.refs_1_), custom_call_target="tpu_custom_call" | custom-call | flops 30000001024 | bytes 1000 | tf_op jit(solution)/shard_map/weight_grads/pallas_call | solution.py:644
  504.8 15.5 %weight_grads.6 = (bf16[512,1024]{1,0:T(8,128)(2,1)}, bf16[512,1024]{1,0:T(8,128)(2,1)}) custom-call(bf16[4096,1024]{1,0:T(8,128)(2,1)} %get-tuple-element.127.refs_0_, bf16[4096,1024]{1,0:T(8,128)(2,1)} %get-tuple-element.99.refs_0_.refs_1_.refs_2_, bf16[512,1024]{1,0:T(8,128)(2,1)} %get-tuple-element.130.refs_2_, ...), custom_call_target="tpu_custom_call" | custom-call | flops 30000001024 | bytes 1000 | tf_op jit(solution)/shard_map/weight_grads/pallas_call | solution.py:644
  522.2 15.2 %weight_grads.7 = (bf16[512,1024]{1,0:T(8,128)(2,1)}, bf16[512,1024]{1,0:T(8,128)(2,1)}) custom-call(bf16[4096,1024]{1,0:T(8,128)(2,1)} %get-tuple-element.126.refs_0_, bf16[4096,1024]{1,0:T(8,128)(2,1)} %get-tuple-element.99.refs_0_.refs_1_.refs_2_, bf16[512,1024]{1,0:T(8,128)(2,1)} %get-tuple-element.131.refs_2_, bf16[512,1024]{1,0:T(8,128)(2,1)} %add_convert_fusion.2.refs_3_), custom_call_target="tpu_custom_call" | custom-call | flops 30000001024 | bytes 1000 | tf_op jit(solution)/shard_map/weight_grads/pallas_call | solution.py:644
  537.4 7.6 collective-permute-done.44
  547.2 4.0 multiply_reduce_fusion.1
  560.5 26.6 %attention_backward.1 = (bf16[1024,512]{1,0:T(8,128)(2,1)S(1)}, bf16[1024,512]{1,0:T(8,128)(2,1)S(1)}) custom-call(s32[1]{0:T(128)} %copy.118.refs_0_, bf16[1024,1024]{1,0:T(8,128)(2,1)} %pad_maximum_fusion.3.refs_1_, bf16[1024,512]{1,0:T(8,128)(2,1)} %copy-done.16, bf16[1024,1024]{1,0:T(8,128)(2,1)} %get-tuple-element.136.refs_3_, ...), custom_call_target="tpu_custom_call" | custom-call | flops 1000 | bytes 1000 | tf_op jit(solution)/shard_map/attention_backward/pallas_call | solution.py:333
  603.8 26.7 %weight_grads.8 = (bf16[512,1024]{1,0:T(8,128)(2,1)}, bf16[512,1024]{1,0:T(8,128)(2,1)}, bf16[512,1024]{1,0:T(8,128)(2,1)}, bf16[512,1024]{1,0:T(8,128)(2,1)}) custom-call(bf16[4096,1024]{1,0:T(8,128)(2,1)} %get-tuple-element.143.refs_0_, bf16[4096,1024]{1,0:T(8,128)(2,1)} %get-tuple-element.144.refs_1_, ...), custom_call_target="tpu_custom_call" | custom-call | flops 1000 | bytes 1000 | tf_op jit(solution)/shard_map/weight_grads/pallas_call | solution.py:644
  632.7 15.3 %weight_grads.9 = (bf16[512,1024]{1,0:T(8,128)(2,1)}, bf16[512,1024]{1,0:T(8,128)(2,1)}) custom-call(bf16[4096,1024]{1,0:T(8,128)(2,1)} %get-tuple-element.148.refs_0_, bf16[4096,1024]{1,0:T(8,128)(2,1)} %get-tuple-element.129.refs_1_, bf16[512,1024]{1,0:T(8,128)(2,1)} %get-tuple-element.149.refs_2_), custom_call_target="tpu_custom_call" | custom-call | flops 1000 | bytes 1000 | tf_op jit(solution)/shard_map/weight_grads/pallas_call | solution.py:644
  655.0 4.2 fusion.9
  660.5 13.6 %expert_update.3 = (f32[8,3,64,1024]{3,2,1,0:T(8,128)}, f32[8,3,4,64,64]{4,3,2,1,0:T(8,128)}, f32[8,3,4,256,256]{4,3,2,1,0:T(8,128)}, f32[8,3,64,1024]{3,2,1,0:T(8,128)}) custom-call(bf16[512,1024]{1,0:T(8,128)(2,1)} %get-tuple-element.152.refs_0_, bf16[512,1024]{1,0:T(8,128)(2,1)} %collective-permute-done.54.refs_1_, ...), custom_call_target="tpu_custom_call" | custom-call | flops 12000000000 | bytes 1000 | tf_op jit(solution)/shard_map/expert_update/pallas_call | solution.py:718
  678.3 12.9 %collective-permute-done.53 = bf16[2,2,64,1024]{3,2,0,1:T(8,128)(2,1)S(1)} collective-permute-done((bf16[2,2,64,1024]{3,2,0,1:T(8,128)(2,1)S(1)}, bf16[2,2,64,1024]{3,2,0,1:T(8,128)(2,1)S(1)}, u32[]{:S(2)}, u32[]{:S(2)}) %collective-permute-start.53) | collective-permute-done | bytes 524320 | tf_op jit(solution)/shard_map/ppermute | solution.py:61
  692.3 19.8 %collective-permute-done.48.refs_10_.refs_1_ = bf16[512,1024]{1,0:T(8,128)(2,1)S(1)} collective-permute-done((bf16[512,1024]{1,0:T(8,128)(2,1)}, bf16[512,1024]{1,0:T(8,128)(2,1)S(1)}, u32[]{:S(2)}, u32[]{:S(2)}) %collective-permute-start.48) | collective-permute-done | bytes 1048608 | tf_op jit(solution)/shard_map/ppermute | solution.py:61
  713.0 13.1 %expert_update.4 = (f32[8,3,64,1024]{3,2,1,0:T(8,128)}, f32[8,3,4,64,64]{4,3,2,1,0:T(8,128)}, f32[8,3,4,256,256]{4,3,2,1,0:T(8,128)}, f32[8,3,64,1024]{3,2,1,0:T(8,128)}) custom-call(bf16[512,1024]{1,0:T(8,128)(2,1)} %get-tuple-element.150.refs_0_, ...), custom_call_target="tpu_custom_call", output_to_operand_aliasing={{0}: (11, {}), {1}: (12, {}), {2}: (13, {}), {3}: (14, {})} | custom-call | flops 12000000000 | bytes 1000 | tf_op jit(solution)/shard_map/expert_update/pallas_call | solution.py:718
  726.2 13.1 %expert_update.5 = (f32[8,3,64,1024]{3,2,1,0:T(8,128)}, f32[8,3,4,64,64]{4,3,2,1,0:T(8,128)}, f32[8,3,4,256,256]{4,3,2,1,0:T(8,128)}, f32[8,3,64,1024]{3,2,1,0:T(8,128)}) custom-call(bf16[512,1024]{1,0:T(8,128)(2,1)} %get-tuple-element.146.refs_0_, ...), custom_call_target="tpu_custom_call", output_to_operand_aliasing={{0}: (8, {}), {1}: (9, {}), {2}: (10, {}), {3}: (11, {})} | custom-call | flops 12000000000 | bytes 1000 | tf_op jit(solution)/shard_map/expert_update/pallas_call | solution.py:718
  (401 shorter events, 179.3 us)
Async XLA Ops:
  7.2 732.1 %reduce-scatter.2.cloned.1.call-start = ((), (), s32[]{:S(2)}) async-start(), calls=%async_computation.1 | async-start | bytes 1114112 | tf_op jit(solution)/shard_map/reduce_scatter | solution.py:1077
  52.6 69.7 %collective-permute-start.12 = (bf16[4,3,64,1024]{3,2,1,0:T(8,128)(2,1)}, bf16[4,3,64,1024]{3,2,1,0:T(8,128)(2,1)S(1)}, u32[]{:S(2)}, u32[]{:S(2)}) collective-permute-start(bf16[4,3,64,1024]{3,2,1,0:T(8,128)(2,1)} %after.12), channel_id=1, source_target_pairs={{0,16},{2,18},{4,20},{6,22},{8,24},{10,26},{12,28},{14,30},{16,0},... | collective-permute-start | bytes 4718600 | tf_op jit(solution)/shard_map/ppermute | solution.py:61
  78.7 43.6 %collective-permute-start.13 = (bf16[3,3,64,1024]{3,2,1,0:T(8,128)(2,1)}, bf16[3,3,64,1024]{3,2,1,0:T(8,128)(2,1)S(1)}, u32[]{:S(2)}, u32[]{:S(2)}) collective-permute-start(bf16[3,3,64,1024]{3,2,1,0:T(8,128)(2,1)} %after.13), channel_id=1, source_target_pairs={{0,4},{2,6},{4,0},{6,2},{8,12},{10,14},{12,8},{14,10},{16,20},{18,... | collective-permute-start | bytes 3538952 | tf_op jit(solution)/shard_map/ppermute | solution.py:61
  81.9 34.6 %collective-permute-start.10 = (bf16[288,512]{1,0:T(8,128)(2,1)}, bf16[288,512]{1,0:T(8,128)(2,1)}, u32[]{:S(2)}, u32[]{:S(2)}) collective-permute-start(bf16[288,512]{1,0:T(8,128)(2,1)} %slice.107.refs_3_), channel_id=1, source_target_pairs={{0,4},{2,6},{4,0},{6,2},{8,12},{10,14},{12,8},{14,10},{16,20},{18,... | collective-permute-start | bytes 884744 | tf_op jit(solution)/shard_map/ppermute | solution.py:61
  82.4 34.1 %collective-permute-start.11 = (bf16[288,512]{1,0:T(8,128)(2,1)}, bf16[288,512]{1,0:T(8,128)(2,1)}, u32[]{:S(2)}, u32[]{:S(2)}) collective-permute-start(bf16[288,512]{1,0:T(8,128)(2,1)} %slice.107.refs_3_), channel_id=1, source_target_pairs={{0,6},{2,4},{4,2},{6,0},{8,14},{10,12},{12,10},{14,8},{16,22},{18,... | collective-permute-start | bytes 884744 | tf_op jit(solution)/shard_map/ppermute | solution.py:61
  83.9 32.6 %collective-permute-start.9 = (bf16[288,512]{1,0:T(8,128)(2,1)}, bf16[288,512]{1,0:T(8,128)(2,1)}, u32[]{:S(2)}, u32[]{:S(2)}) collective-permute-start(bf16[288,512]{1,0:T(8,128)(2,1)} %slice.107.refs_3_), channel_id=1, source_target_pairs={{0,2},{2,0},{4,6},{6,4},{8,10},{10,8},{12,14},{14,12},{16,18},{18,... | collective-permute-start | bytes 884744 | tf_op jit(solution)/shard_map/ppermute | solution.py:61
  131.8 46.2 %collective-permute-start.18 = (bf16[512,1024]{1,0:T(8,128)(2,1)S(1)}, bf16[512,1024]{1,0:T(8,128)(2,1)}, u32[]{:S(2)}, u32[]{:S(2)}) collective-permute-start(bf16[512,1024]{1,0:T(8,128)(2,1)S(1)} %multiply_convert_fusion.refs_0_), channel_id=1, source_target_pairs={{0,8},{2,10},{4,12},{6,14},{8,0},{10,2},{12,4},{14,6},{16,24},{18,... | collective-permute-start | bytes 3145736 | tf_op jit(solution)/shard_map/ppermute | solution.py:61
  131.9 47.5 %collective-permute-start.17 = (bf16[5,3,64,1024]{3,2,1,0:T(8,128)(2,1)}, bf16[5,3,64,1024]{3,2,1,0:T(8,128)(2,1)}, u32[]{:S(2)}, u32[]{:S(2)}) collective-permute-start(bf16[5,3,64,1024]{3,2,1,0:T(8,128)(2,1)} %get-tuple-element.98), channel_id=1, source_target_pairs={{0,4},{2,6},{4,0},{6,2},{8,12},{10,14},{12,8},{14,10},{16,20},{18,... | collective-permute-start | bytes 5898248 | tf_op jit(solution)/shard_map/ppermute | solution.py:61
  133.5 71.3 %collective-permute-start.16 = (bf16[4,3,64,1024]{3,2,1,0:T(8,128)(2,1)}, bf16[4,3,64,1024]{3,2,1,0:T(8,128)(2,1)}, u32[]{:S(2)}, u32[]{:S(2)}) collective-permute-start(bf16[4,3,64,1024]{3,2,1,0:T(8,128)(2,1)} %after.14), channel_id=1, source_target_pairs={{0,16},{2,18},{4,20},{6,22},{8,24},{10,26},{12,28},{14,30},{16,0},... | collective-permute-start | bytes 4718600 | tf_op jit(solution)/shard_map/ppermute | solution.py:61
  136.6 74.2 %collective-permute-start.20 = (bf16[4,3,64,1024]{3,2,1,0:T(8,128)(2,1)S(1)}, bf16[4,3,64,1024]{3,2,1,0:T(8,128)(2,1)}, u32[]{:S(2)}, u32[]{:S(2)}) collective-permute-start(bf16[4,3,64,1024]{3,2,1,0:T(8,128)(2,1)S(1)} %collective-permute-done.12.refs_7_.refs_3_.refs_9_.refs_11_), channel_id=1, source_target_pairs={{0,4},{2,6},{4,0},{6,2},{8,12},{10,14},{12,8},{14,10},{16,20},{18,... | collective-permute-start | bytes 4718600 | tf_op jit(solution)/shard_map/ppermute | solution.py:61
  137.1 67.7 %collective-permute-start.15 = (bf16[512,1024]{1,0:T(8,128)(2,1)S(1)}, bf16[512,1024]{1,0:T(8,128)(2,1)}, u32[]{:S(2)}, u32[]{:S(2)}) collective-permute-start(bf16[512,1024]{1,0:T(8,128)(2,1)S(1)} %multiply_convert_fusion.refs_0_), channel_id=1, source_target_pairs={{0,2},{2,0},{4,6},{6,4},{8,10},{10,8},{12,14},{14,12},{16,18},{18,... | collective-permute-start | bytes 3145736 | tf_op jit(solution)/shard_map/ppermute | solution.py:61
  178.0 32.9 %collective-permute-start.19 = (bf16[512,1024]{1,0:T(8,128)(2,1)}, bf16[512,1024]{1,0:T(8,128)(2,1)}, u32[]{:S(2)}, u32[]{:S(2)}) collective-permute-start(bf16[512,1024]{1,0:T(8,128)(2,1)} %collective-permute-done.18.refs_2_), channel_id=1, source_target_pairs={{0,2},{2,0},{4,6},{6,4},{8,10},{10,8},{12,14},{14,12},{16,18},{18,... | collective-permute-start | bytes 3145736 | tf_op jit(solution)/shard_map/ppermute | solution.py:61
  217.8 43.8 %collective-permute-start.22 = (bf16[4,3,64,1024]{3,2,1,0:T(8,128)(2,1)}, bf16[4,3,64,1024]{3,2,1,0:T(8,128)(2,1)S(1)}, u32[]{:S(2)}, u32[]{:S(2)}) collective-permute-start(bf16[4,3,64,1024]{3,2,1,0:T(8,128)(2,1)} %collective-permute-done.16.refs_1_.refs_4_.refs_10_.refs_12_), channel_id=1, source_target_pairs={{0,4},{2,6},{4,0},{6,2},{8,12},{10,14},{12,8},{14,10},{16,20},{18,... | collective-permute-start | bytes 4718600 | tf_op jit(solution)/shard_map/ppermute | solution.py:61
  312.9 45.3 %collective-permute-start.29 = (bf16[512,1024]{1,0:T(8,128)(2,1)S(1)}, bf16[512,1024]{1,0:T(8,128)(2,1)S(1)}, u32[]{:S(2)}, u32[]{:S(2)}) collective-permute-start(bf16[512,1024]{1,0:T(8,128)(2,1)S(1)} %add_convert_fusion.6), channel_id=1, source_target_pairs={{0,10},{2,8},{4,14},{6,12},{8,2},{10,0},{12,6},{14,4},{16,26},{18,... | collective-permute-start | bytes 3145736 | tf_op jit(solution)/shard_map/ppermute | solution.py:61
  362.2 28.7 %collective-permute-start.35 = (bf16[512,1024]{1,0:T(8,128)(2,1)}, bf16[512,1024]{1,0:T(8,128)(2,1)}, u32[]{:S(2)}, u32[]{:S(2)}) collective-permute-start(bf16[512,1024]{1,0:T(8,128)(2,1)} %multiply_convert_fusion.1.refs_0_), channel_id=1, source_target_pairs={{0,10},{2,8},{4,14},{6,12},{8,2},{10,0},{12,6},{14,4},{16,26},{18,... | collective-permute-start | bytes 3145736 | tf_op jit(solution)/shard_map/ppermute | solution.py:61
  364.7 46.7 %collective-permute-start.34 = (bf16[512,1024]{1,0:T(8,128)(2,1)}, bf16[512,1024]{1,0:T(8,128)(2,1)}, u32[]{:S(2)}, u32[]{:S(2)}) collective-permute-start(bf16[512,1024]{1,0:T(8,128)(2,1)} %multiply_convert_fusion.1.refs_0_), channel_id=1, source_target_pairs={{0,8},{2,10},{4,12},{6,14},{8,0},{10,2},{12,4},{14,6},{16,24},{18,... | collective-permute-start | bytes 3145736 | tf_op jit(solution)/shard_map/ppermute | solution.py:61
  365.1 46.4 %collective-permute-start.33 = (bf16[512,1024]{1,0:T(8,128)(2,1)}, bf16[512,1024]{1,0:T(8,128)(2,1)}, u32[]{:S(2)}, u32[]{:S(2)}) collective-permute-start(bf16[512,1024]{1,0:T(8,128)(2,1)} %multiply_convert_fusion.1.refs_0_), channel_id=1, source_target_pairs={{0,2},{2,0},{4,6},{6,4},{8,10},{10,8},{12,14},{14,12},{16,18},{18,... | collective-permute-start | bytes 3145736 | tf_op jit(solution)/shard_map/ppermute | solution.py:61
  413.7 132.9 %collective-permute-start.32 = (bf16[512,1024]{1,0:T(8,128)(2,1)}, bf16[512,1024]{1,0:T(8,128)(2,1)}, u32[]{:S(2)}, u32[]{:S(2)}) collective-permute-start(bf16[512,1024]{1,0:T(8,128)(2,1)} %get-tuple-element.114), channel_id=1, source_target_pairs={{0,1},{1,0},{2,3},{3,2},{4,5},{5,4},{6,7},{7,6},{8,9},{9,8},{10,11... | collective-permute-start | bytes 3145736 | tf_op jit(solution)/shard_map/ppermute | solution.py:66
  497.1 49.4 %collective-permute-start.42 = (bf16[512,1024]{1,0:T(8,128)(2,1)S(1)}, bf16[512,1024]{1,0:T(8,128)(2,1)}, u32[]{:S(2)}, u32[]{:S(2)}) collective-permute-start(bf16[512,1024]{1,0:T(8,128)(2,1)S(1)} %add_convert_fusion.3.refs_5_), channel_id=1, source_target_pairs={{0,10},{2,8},{4,14},{6,12},{8,2},{10,0},{12,6},{14,4},{16,26},{18,... | collective-permute-start | bytes 3145736 | tf_op jit(solution)/shard_map/ppermute | solution.py:61
  502.3 44.3 %collective-permute-start.40 = (bf16[512,1024]{1,0:T(8,128)(2,1)}, bf16[512,1024]{1,0:T(8,128)(2,1)}, u32[]{:S(2)}, u32[]{:S(2)}) collective-permute-start(bf16[512,1024]{1,0:T(8,128)(2,1)} %add_convert_fusion.4.refs_4_), channel_id=1, source_target_pairs={{0,8},{2,10},{4,12},{6,14},{8,0},{10,2},{12,4},{14,6},{16,24},{18,... | collective-permute-start | bytes 3145736 | tf_op jit(solution)/shard_map/ppermute | solution.py:61
  504.0 42.6 %collective-permute-start.38 = (bf16[512,1024]{1,0:T(8,128)(2,1)}, bf16[512,1024]{1,0:T(8,128)(2,1)}, u32[]{:S(2)}, u32[]{:S(2)}) collective-permute-start(bf16[512,1024]{1,0:T(8,128)(2,1)} %add_convert_fusion.5.refs_3_), channel_id=1, source_target_pairs={{0,2},{2,0},{4,6},{6,4},{8,10},{10,8},{12,14},{14,12},{16,18},{18,... | collective-permute-start | bytes 3145736 | tf_op jit(solution)/shard_map/ppermute | solution.py:61
  553.7 45.1 %collective-permute-start.47 = (bf16[512,1024]{1,0:T(8,128)(2,1)}, bf16[512,1024]{1,0:T(8,128)(2,1)}, u32[]{:S(2)}, u32[]{:S(2)}) collective-permute-start(bf16[512,1024]{1,0:T(8,128)(2,1)} %get-tuple-element.133.refs_1_.refs_9_), channel_id=1, source_target_pairs={{0,4},{2,6},{4,0},{6,2},{8,12},{10,14},{12,8},{14,10},{16,20},{18,... | collective-permute-start | bytes 3145736 | tf_op jit(solution)/shard_map/ppermute | solution.py:61
  554.2 105.1 %collective-permute-start.51 = (bf16[512,1024]{1,0:T(8,128)(2,1)}, bf16[512,1024]{1,0:T(8,128)(2,1)}, u32[]{:S(2)}, u32[]{:S(2)}) collective-permute-start(bf16[512,1024]{1,0:T(8,128)(2,1)} %add_convert_fusion.2.refs_3_), channel_id=1, source_target_pairs={{0,16},{2,18},{4,20},{6,22},{8,24},{10,26},{12,28},{14,30},{16,0},... | collective-permute-start | bytes 3145736 | tf_op jit(solution)/shard_map/ppermute | solution.py:61
  556.6 103.6 %collective-permute-start.55 = (bf16[512,1024]{1,0:T(8,128)(2,1)}, bf16[512,1024]{1,0:T(8,128)(2,1)}, u32[]{:S(2)}, u32[]{:S(2)}) collective-permute-start(bf16[512,1024]{1,0:T(8,128)(2,1)} %add_convert_fusion.1.refs_2_.refs_10_), channel_id=1, source_target_pairs={{0,16},{2,18},{4,20},{6,22},{8,24},{10,26},{12,28},{14,30},{16,0},... | collective-permute-start | bytes 3145736 | tf_op jit(solution)/shard_map/ppermute | solution.py:61
  595.5 52.5 %collective-permute-start.52 = (bf16[2,2,2,64,1024]{4,3,0,2,1:T(8,128)(2,1)}, bf16[2,2,2,64,1024]{4,3,0,2,1:T(8,128)(2,1)}, u32[]{:S(2)}, u32[]{:S(2)}) collective-permute-start(bf16[2,2,2,64,1024]{4,3,0,2,1:T(8,128)(2,1)} %bitcast.64), channel_id=1, source_target_pairs={{0,2},{2,0},{4,6},{6,4},{8,10},{10,8},{12,14},{14,12},{16,18},{18,... | collective-permute-start | bytes 3145736 | tf_op jit(solution)/shard_map/ppermute | solution.py:61
  598.7 55.1 %collective-permute-start.46 = (bf16[512,1024]{1,0:T(8,128)(2,1)}, bf16[512,1024]{1,0:T(8,128)(2,1)}, u32[]{:S(2)}, u32[]{:S(2)}) collective-permute-start(bf16[512,1024]{1,0:T(8,128)(2,1)} %convolution_convert_fusion.2), channel_id=1, source_target_pairs={{0,1},{1,0},{2,3},{3,2},{4,5},{5,4},{6,7},{7,6},{8,9},{9,8},{10,11... | collective-permute-start | bytes 3145736 | tf_op jit(solution)/shard_map/ppermute | solution.py:66
  630.4 30.1 %collective-permute-start.54 = (bf16[512,1024]{1,0:T(8,128)(2,1)}, bf16[512,1024]{1,0:T(8,128)(2,1)}, u32[]{:S(2)}, u32[]{:S(2)}) collective-permute-start(bf16[512,1024]{1,0:T(8,128)(2,1)} %get-tuple-element.149.refs_2_), channel_id=1, source_target_pairs={{0,4},{2,6},{4,0},{6,2},{8,12},{10,14},{12,8},{14,10},{16,20},{18,... | collective-permute-start | bytes 3145736 | tf_op jit(solution)/shard_map/ppermute | solution.py:61
  648.0 78.1 %collective-permute-start.49 = (bf16[512,1024]{1,0:T(8,128)(2,1)S(1)}, bf16[512,1024]{1,0:T(8,128)(2,1)}, u32[]{:S(2)}, u32[]{:S(2)}) collective-permute-start(bf16[512,1024]{1,0:T(8,128)(2,1)S(1)} %copy-done.33), channel_id=1, source_target_pairs={{0,16},{2,18},{4,20},{6,22},{8,24},{10,26},{12,28},{14,30},{16,0},... | collective-permute-start | bytes 3145736 | tf_op jit(solution)/shard_map/ppermute | solution.py:61
  653.8 38.5 %collective-permute-start.50 = (bf16[512,1024]{1,0:T(8,128)(2,1)}, bf16[512,1024]{1,0:T(8,128)(2,1)}, u32[]{:S(2)}, u32[]{:S(2)}) collective-permute-start(bf16[512,1024]{1,0:T(8,128)(2,1)} %get-tuple-element.151), channel_id=1, source_target_pairs={{0,4},{2,6},{4,0},{6,2},{8,12},{10,14},{12,8},{14,10},{16,20},{18,... | collective-permute-start | bytes 3145736 | tf_op jit(solution)/shard_map/ppermute | solution.py:61
  659.3 52.8 %collective-permute-start.48 = (bf16[512,1024]{1,0:T(8,128)(2,1)}, bf16[512,1024]{1,0:T(8,128)(2,1)S(1)}, u32[]{:S(2)}, u32[]{:S(2)}) collective-permute-start(bf16[512,1024]{1,0:T(8,128)(2,1)} %get-tuple-element.147), channel_id=1, source_target_pairs={{0,4},{2,6},{4,0},{6,2},{8,12},{10,14},{12,8},{14,10},{16,20},{18,... | collective-permute-start | bytes 3145736 | tf_op jit(solution)/shard_map/ppermute | solution.py:61
  660.2 31.0 %collective-permute-start.53 = (bf16[2,2,64,1024]{3,2,0,1:T(8,128)(2,1)S(1)}, bf16[2,2,64,1024]{3,2,0,1:T(8,128)(2,1)S(1)}, u32[]{:S(2)}, u32[]{:S(2)}) collective-permute-start(bf16[2,2,64,1024]{3,2,0,1:T(8,128)(2,1)S(1)} %dynamic-slice_bitcast_fusion), channel_id=1, source_target_pairs={{0,8},{2,10},{4,12},{6,14},{8,0},{10,2},{12,4},{14,6},{16,24},{18,... | collective-permute-start | bytes 1572872 | tf_op jit(solution)/shard_map/ppermute | solution.py:61
  692.2 47.3 %collective-permute-start.63 = (bf16[2,64,1024]{2,1,0:T(8,128)(2,1)S(1)}, bf16[2,64,1024]{2,1,0:T(8,128)(2,1)S(1)}, u32[]{:S(2)}, u32[]{:S(2)}) collective-permute-start(bf16[2,64,1024]{2,1,0:T(8,128)(2,1)S(1)} %dynamic-slice_bitcast_fusion.1), channel_id=1, source_target_pairs={{0,4},{2,6},{4,0},{6,2},{8,12},{10,14},{12,8},{14,10},{16,20},{18,... | collective-permute-start | bytes 786440 | tf_op jit(solution)/shard_map/ppermute | solution.py:61
  (116 other events, 1311.2 us)
Sparse Core Ops, SparseCore 0:
  632.8 80.0 reduce-scatter.1
